TPU v7x, 128 devices: a whole 4x4x4 slice. The times are simulated.
128 devices in a mesh: fsdp: 32 (over y, z, x_lo), mp: 4 (over x_hi, core).
Axes of the slice: x: 4 (x_hi: 2, x_lo: 2; x = x_hi * 2 + x_lo), y: 4, z: 4, core: 2. Of those that a mesh axis runs over, the one named last changes fastest.
Arguments:
- tokens: bfloat16 [4096, 8192], P('fsdp'), may hold values from -22 to 22
- cotangent: bfloat16 [4096, 16384], P('fsdp', 'mp'), may hold values from -22 to 22
- weight: bfloat16 [8192, 16384], P('fsdp', 'mp'), may hold values from -0.0625 to 0.0625
- row_prev: float32 [8192], P('fsdp'), may hold values from 0.01 to 0.3
- col_prev: float32 [16384], P('mp'), may hold values from 0.01 to 0.3
Outputs:
- input_grad: bfloat16 [4096, 8192], P('mp', 'fsdp')
- update: float32 [8192, 16384], P('fsdp', 'mp')
- row_next: float32 [8192], P('fsdp')
- col_next: float32 [16384], P('mp')
- update_rms: float32 [], replicated
All inputs are finite; a program needn't handle non-finite values.
Results may differ from a plain program's by a relative error of at most 0.00055.
Values may be sent and summed in bfloat16 or wider, within the bound.
No kernel may reach another device: no remote copies, remote signals or barrier semaphores. Data moves between devices by JAX's collectives and lax.ppermute only.
A program may use at most 128 MiB of HBM per device.

v0:
```python
import jax
import jax.numpy as jnp
from jax import lax
from jax.sharding import PartitionSpec as P

D = 8192
FF = 16384


decay_rate = 0.84
tiny_eps = 1e-30


def body(tokens, cotangent, weight, row_prev, col_prev):
    feature_cols = lax.all_to_all(tokens, "fsdp", split_axis=1, concat_axis=0, tiled=True)
    total_tokens = feature_cols.shape[0]
    gathered = lax.all_gather(cotangent, "fsdp", axis=0, tiled=True)
    grad_sum = lax.dot_general(
        feature_cols, gathered, (((0,), (0,)), ((), ())), preferred_element_type=jnp.float32
    )
    terms = lax.dot_general(
        gathered, weight, (((1,), (1,)), ((), ())), preferred_element_type=jnp.float32
    )
    grad = grad_sum * float(total_tokens) ** (-0.5)
    input_grad = lax.psum_scatter(terms, "mp", scatter_dimension=0, tiled=True).astype(jnp.bfloat16)
    squares = grad * grad
    row_sum = lax.psum(jnp.sum(squares, axis=1), "mp")
    row_next = decay_rate * row_prev + (1.0 - decay_rate) * (row_sum / FF + tiny_eps)
    col_sum = lax.psum(jnp.sum(squares, axis=0), "fsdp")
    row_total = lax.psum(jnp.sum(row_next), "fsdp")
    col_next = decay_rate * col_prev + (1.0 - decay_rate) * (col_sum / D + tiny_eps)
    row_mean = row_total / D
    raw = grad / jnp.sqrt(row_next[:, None] * col_next[None, :] / row_mean)
    square_total = lax.psum(jnp.sum(raw * raw), ("fsdp", "mp"))
    update_rms = jnp.sqrt(square_total / (D * FF))
    update = raw / jnp.maximum(1.0, update_rms)
    return (input_grad, update, row_next, col_next, update_rms)


def solution(mesh):
    in_specs = (P("fsdp", None), P("fsdp", "mp"), P("fsdp", "mp"), P("fsdp"), P("mp"))
    out_specs = (P("mp", "fsdp"), P("fsdp", "mp"), P("fsdp"), P("mp"), P())
    return jax.shard_map(body, mesh=mesh, in_specs=in_specs, out_specs=out_specs, check_vma=False)
```

profile of v0, /device:TPU:0, one launch (start us, length us, event | category | flops | bytes accessed | tf_op | source)
XLA Modules:
  0.0 1055.8 jit_solution(11391547980047862024)
XLA Ops:
  7.2 0.0 copy-start
  7.2 0.0 all-gather.2.cloned.1.call-start
  7.2 0.7 all-gather.2.cloned.1.call-update
  7.9 0.0 reduce-scatter.2.cloned.1.call-start
  8.0 714.8 %all-gather.2.cloned.1.call-done = bf16[4096,4096]{1,0:T(8,128)(2,1)} async-done(((bf16[128,4096]{1,0:T(8,128)(2,1)}), bf16[4096,4096]{1,0:T(8,128)(2,1)}) %all-gather.2.cloned.1.call-update) | async-done | bytes 33554448 | tf_op jit(solution)/shard_map/all_gather | solution.py:17
  722.8 0.0 copy-done
  722.8 17.2 %fusion.1 = f32[4096,256]{1,0:T(8,128)} fusion(bf16[4096,4096]{1,0:T(8,128)(2,1)} %all-gather.2.cloned.1.call-done, bf16[256,4096]{1,0:T(8,128)(2,1)S(1)} %copy-done), kind=kOutput, calls=%fused_computation.9 | convolution fusion | flops 8589934592 | bytes 39845888 | tf_op jit(solution)/shard_map/dot_general | solution.py:21
  740.0 0.0 reduce-scatter.2.cloned.1.call-update
  740.0 4.1 copy.10
  744.1 45.8 %all_to_all.19 = bf16[128,32,256]{0,2,1:T(8,128)(2,1)} all-to-all(bf16[128,32,256]{0,2,1:T(8,128)(2,1)} %bitcast.9), channel_id=1, replica_groups=mesh['fsdp'=32,'mp'=4] {'fsdp'}, dimensions={1} | all-to-all | bytes 4194304 | tf_op jit(solution)/shard_map/all_to_all | solution.py:15
  789.8 4.1 copy.11
  793.9 0.0 copy-start.4
  793.9 0.0 copy-start.2
  793.9 17.1 %multiply_reduce_fusion.1 = (f32[4096]{0:T(1024)S(1)}, f32[256]{0:T(256)S(1)}, f32[256,4096]{1,0:T(8,128)}) fusion(bf16[4096,256]{1,0:T(8,128)(2,1)} %bitcast.7, bf16[4096,4096]{1,0:T(8,128)(2,1)} %all-gather.2.cloned.1.call-done), kind=kOutput, calls=%fused_computation.3 | convolution fusion | flops 8594124800 | bytes 39863296 | tf_op jit(solution)/shard_map/dot_general | solution.py:18
  811.0 7.1 psum.28
  818.1 0.0 copy-done.4
  818.1 0.6 fusion
  818.8 0.0 copy-start.3
  818.8 153.6 %all-reduce = (f32[]{:T(128)}, f32[4096]{0:T(1024)S(1)}) all-reduce(f32[]{:T(128)} %get-tuple-element.9, f32[4096]{0:T(1024)S(1)} %get-tuple-element.5), channel_id=1, replica_groups=mesh['fsdp'=32,'mp'=4] {'fsdp'}, use_global_device_ids=true, to_apply=%region_6.0 | all-reduce | flops 4097 | bytes 32776 | tf_op jit(solution)/shard_map/psum | solution.py:30
  973.0 0.0 copy-done.2
  973.1 0.0 copy-start.1
  973.1 4.0 multiply_reduce_fusion
  977.0 62.9 %psum.31 = f32[]{:T(128)} all-reduce(f32[]{:T(128)} %multiply_reduce_fusion), channel_id=1, replica_groups=mesh['fsdp'=32,'mp'=4] {'fsdp','mp'}, use_global_device_ids=true, to_apply=%region_8.0 | all-reduce | flops 1 | bytes 8 | tf_op jit(solution)/shard_map/psum | solution.py:34
  1040.7 5.1 broadcast_divide_fusion
  1045.8 0.0 copy-done.3
  1045.8 0.0 copy-done.1
  1045.8 0.0 reduce-scatter.2.cloned.1.call-done
  1045.8 2.1 convert_element_type.3
  (1 shorter events, 0.0 us)
Async XLA Ops:
  7.2 715.6 %copy-start = (bf16[256,4096]{1,0:T(8,128)(2,1)S(1)}, bf16[256,4096]{1,0:T(8,128)(2,1)}, u32[]{:S(2)}) copy-start(bf16[256,4096]{1,0:T(8,128)(2,1)} %param.7) | copy-start | bytes 6291460
  7.2 715.6 %all-gather.2.cloned.1.call-start = ((), (), s32[]{:S(2)}) async-start(), calls=%async_computation.2 | async-start | bytes 34603008 | tf_op jit(solution)/shard_map/all_gather | solution.py:17
  7.9 1037.9 %reduce-scatter.2.cloned.1.call-start = ((), (), s32[]{:S(2)}) async-start(), calls=%async_computation.3 | async-start | bytes 5242880 | tf_op jit(solution)/shard_map/reduce_scatter | solution.py:25
  793.9 24.3 %copy-start.4 = (f32[256]{0:T(256)S(1)}, f32[256]{0:T(256)}, u32[]{:S(2)}) copy-start(f32[256]{0:T(256)} %param.8) | copy-start | bytes 3076
  793.9 179.2 %copy-start.2 = (f32[4096]{0:T(1024)S(1)}, f32[4096]{0:T(1024)}, u32[]{:S(2)}) copy-start(f32[4096]{0:T(1024)} %param.9) | copy-start | bytes 49156
  818.8 227.0 %copy-start.3 = (f32[256]{0:T(256)}, f32[256]{0:T(256)S(1)}, u32[]{:S(2)}) copy-start(f32[256]{0:T(256)S(1)} %get-tuple-element.10) | copy-start | bytes 3076
  973.1 72.7 %copy-start.1 = (f32[4096]{0:T(1024)}, f32[4096]{0:T(1024)S(1)}, u32[]{:S(2)}) copy-start(f32[4096]{0:T(1024)S(1)} %multiply_add_fusion) | copy-start | bytes 49156
Sparse Core Ops, SparseCore 0:
  9.7 713.0 all-gather.1
  740.1 59.5 reduce-scatter.1
where the time goes:
time: 1060 us
  waiting for transfers between devices  716 us (68%)
  blocking collectives  269 us (25%)
  matrix products  34.3 us (3%)
  between operations  16.6 us (2%)
  other arithmetic  11.7 us (1%)
    all_gather x1, waiting for transfers between devices, body(): gathered = lax.all_gather(cotangent, 'fsdp', axis=0, tiled=True)  715 us
    psum x1, blocking collectives, body(): row_total = lax.psum(jnp.sum(row_next), 'fsdp')  154 us
    psum x1, blocking collectives, body(): square_total = lax.psum(jnp.sum(raw * raw), ('fsdp', 'mp'))  62.9 us
    all_to_all x1, blocking collectives, body(): lax.all_to_all(tokens, 'fsdp', split_axis=1, concat_axis=0, tiled=True)  45.8 us
  transfers between devices with their start and end apart: 2, of which 1 were waited for; matrix products, arithmetic and copies ran while one was open for 3% of the time, Pallas kernels for 0%

commit v1 on v0

v1 whole, which is shorter than its diff:
```python
import jax
import jax.numpy as jnp
from jax import lax
from jax.sharding import Mesh, PartitionSpec as P

D = 8192
FF = 16384
TOKENS = 4096
F32 = jnp.float32

decay_rate = 0.84
tiny_eps = 1e-30

AXES = ("y", "z", "xl", "xh", "c")
SIZES = (4, 4, 2, 2, 2)
SWAP = [(0, 1), (1, 0)]
DIAG = [(0, 3), (3, 0), (1, 2), (2, 1)]
CHUNKS = ((0, 1024), (1024, 1024))


def spread(value, axes, count):
    copies = jnp.broadcast_to(value[None], (count,) + value.shape)
    return lax.all_to_all(copies, axes, split_axis=0, concat_axis=0, tiled=True)


def body(tokens, cotangent, weight, row_prev, col_prev):
    xl = lax.axis_index("xl")
    xh = lax.axis_index("xh")
    c = lax.axis_index("c")
    half = cotangent.shape[1] // 2

    def mine(a, n, axis, index):
        return lax.dynamic_slice_in_dim(a, index * n, n, axis)

    own = mine(cotangent, half, 1, xl)
    other = lax.ppermute(mine(cotangent, half, 1, 1 - xl), "xl", SWAP)
    shard = jnp.stack([own, other])

    part = mine(tokens, 64, 0, c).reshape(64, 16, 512)
    xo = lax.all_to_all(part, ("y", "z"), split_axis=1, concat_axis=0, tiled=False)
    xp = lax.ppermute(xo, "xl", SWAP)
    x_mine = jnp.stack([xo, xp], 1)
    x_theirs = lax.ppermute(x_mine, "c", SWAP)
    x_lo = jnp.where(c == 0, x_mine, x_theirs)
    x_hi = jnp.where(c == 0, x_theirs, x_mine)
    x_all = jnp.stack([x_lo, x_hi], 2).reshape(4096, 2, 256)
    x_rel = jnp.where(xl == 0, x_all, x_all[:, ::-1]).reshape(4096, 512)

    w_own = mine(weight, half, 1, xl)
    w_other = lax.ppermute(mine(weight, half, 1, 1 - xl), "xl", SWAP)
    w_all = jnp.concatenate([w_own, w_other], 0)

    grads, rows, cols, received, partial = [], [], [], [], None
    for first, width in CHUNKS:
        piece = lax.slice_in_dim(shard, first, first + width, axis=2)
        c_all = lax.all_gather(piece, ("y", "z"), axis=0, tiled=False).reshape(4096, width)
        g = lax.dot_general(x_rel, c_all, (((0,), (0,)), ((), ())), preferred_element_type=F32)
        g = g * float(TOKENS) ** (-0.5)
        squares = g * g
        rows.append(jnp.sum(squares, axis=1))
        cols.append(jnp.sum(squares, axis=0))
        grads.append(g)
        received.append(lax.ppermute(g[256:], "xl", SWAP))
        w = lax.slice_in_dim(w_all, first, first + width, axis=1)
        term = lax.dot_general(c_all, w, (((1,), (1,)), ((), ())), preferred_element_type=F32)
        partial = term if partial is None else partial + term

    def flip(v):
        return jnp.where(xl == 0, v, jnp.concatenate([v[256:], v[:256]]))

    row_all = jnp.sum(spread(flip(sum(rows)), ("xl", "xh", "c"), 8), 0)
    row_sum = flip(row_all)
    row_prev_other = lax.ppermute(row_prev, "xl", SWAP)
    row_next = decay_rate * jnp.concatenate([row_prev, row_prev_other]) + (1.0 - decay_rate) * (
        row_sum / FF + tiny_eps
    )
    col_sum = jnp.sum(spread(jnp.concatenate(cols), ("y", "z"), 16), 0)
    col_prev_mine = mine(col_prev, half, 0, xl)
    col_half = decay_rate * col_prev_mine + (1.0 - decay_rate) * (col_sum / D + tiny_eps)
    col_other = lax.ppermute(col_half, "xl", SWAP)

    s = jnp.zeros((), F32)
    for (first, width), g in zip(CHUNKS, grads):
        s = s + jnp.sum((g * g) / (row_next[:, None] * col_half[None, first : first + width]))
    rows_own = jnp.sum(row_next[:256])
    lane = lax.broadcasted_iota(jnp.int32, (128,), 0)
    pair = jnp.where(lane == 0, s, jnp.where(lane == 1, rows_own, 0.0))
    totals = jnp.sum(spread(pair, AXES, 128), 0)
    row_mean = totals[1] / 4.0 / D
    update_rms = jnp.sqrt(row_mean * (totals[0] / (D * FF)))
    scale = jnp.sqrt(row_mean) / jnp.maximum(1.0, update_rms)

    row_own = row_next[:256]
    g_mine = jnp.concatenate([g[:256] for g in grads], 1) / jnp.sqrt(row_own[:, None] * col_half[None, :]) * scale
    g_recv = jnp.concatenate(received, 1) / jnp.sqrt(row_own[:, None] * col_other[None, :]) * scale
    update = jnp.where(
        xl == 0, jnp.concatenate([g_mine, g_recv], 1), jnp.concatenate([g_recv, g_mine], 1)
    )
    col_next = jnp.where(
        xl == 0, jnp.concatenate([col_half, col_other]), jnp.concatenate([col_other, col_half])
    )

    blocks = partial.reshape(2, 2, 1024, 512)
    keep = lax.dynamic_index_in_dim(blocks, c, 1, keepdims=False)
    send = lax.dynamic_index_in_dim(blocks, 1 - c, 1, keepdims=False)
    chip = keep + lax.ppermute(send, "c", SWAP)

    def turn(v):
        v = v.reshape(4, 2, 128, 2, 256)
        return v[:, ::-1, :, ::-1].reshape(1024, 512)

    keep = lax.dynamic_index_in_dim(chip, xh, 0, keepdims=False)
    send = lax.dynamic_index_in_dim(chip, 1 - xh, 0, keepdims=False)
    two = keep + turn(lax.ppermute(send, ("xl", "xh"), DIAG))
    got = lax.ppermute(two[:, 256:], "xl", SWAP).reshape(4, 2, 128, 256)[:, ::-1]
    total = two[:, :256].reshape(4, 2, 128, 256) + got
    total = jnp.where(xl == 0, total, total[:, ::-1]).reshape(1024, 256)
    return (total.astype(jnp.bfloat16), update, row_own, col_next, update_rms)


def solution(mesh):
    fine = Mesh(mesh.devices.reshape(SIZES), AXES)
    fsdp, mp = ("y", "z", "xl"), ("xh", "c")
    in_specs = (P(fsdp, None), P(fsdp, mp), P(fsdp, mp), P(fsdp), P(mp))
    out_specs = (P(mp, fsdp), P(fsdp, mp), P(fsdp), P(mp), P())
    return jax.shard_map(body, mesh=fine, in_specs=in_specs, out_specs=out_specs, check_vma=False)
```

time: 1060 us -> 387 us (0.37)
  waiting for transfers between devices: 716 us -> 164 us
  blocking collectives: 269 us -> 30.3 us
  local copies, waits for them, and re-layouts: 8.15 us -> 80.5 us
  starting transfers between devices: 0.08 us -> 30 us
  other arithmetic: 11.7 us -> 25.5 us
    all_gather x1 -> x2, waiting for transfers between devices: 715 us -> 61.2 us  [body(): lax.all_gather(piece, ('y', 'z'), axis=0, tiled=False).reshape(4096, width)]
    psum x3 -> x0, blocking collectives: 224 us -> none  [the longest x1 154 us: body(): row_total = lax.psum(jnp.sum(row_next), 'fsdp')]
    ppermute x0 -> x11, waiting for transfers between devices: none -> 79.7 us  [the longest x1 19 us: body(): lax.ppermute(two[:, 256:], 'xl', SWAP).reshape(4, 2, 128, 256)[:, ::-1]]
    rev x0 -> x2, local copies, waits for them, and re-layouts: none -> 45.7 us  [the longest x1 37.6 us: body(): x_rel = jnp.where(xl == 0, x_all, x_all[:, ::-1]).reshape(4096, 512)]
    all_to_all x0 -> x3, waiting for transfers between devices: none -> 22.2 us  [spread(): return lax.all_to_all(copies, axes, split_axis=0, concat_axis=0, tiled=True)]
    all_to_all x0 -> x3, starting transfers between devices: none -> 19 us  [spread(): return lax.all_to_all(copies, axes, split_axis=0, concat_axis=0, tiled=True)]
    all_to_all x1, blocking collectives: 45.8 us -> 30.3 us  [body(): lax.all_to_all(part, ('y', 'z'), split_axis=1, concat_axis=0, tiled=False)]
    ppermute x0 -> x11, starting transfers between devices: none -> 10.9 us  [the longest x2 2.71 us: body(): received.append(lax.ppermute(g[256:], 'xl', SWAP))]
  transfers between devices with their start and end apart: 2 -> 16, of which waited for: 1 -> 8; matrix products, arithmetic and copies ran while one was open for 3% -> 34% of each run, Pallas kernels for 0% -> 0%
where the time goes in v1:
time: 387 us; the launch traced here: 384 us
  waiting for transfers between devices  164 us (42%)
  local copies, waits for them, and re-layouts  80.5 us (21%)
  matrix products  35.1 us (9%)
  blocking collectives  30.3 us (8%)
  starting transfers between devices  30 us (8%)
  other arithmetic  25.5 us (7%)
  between operations  18.9 us (5%)
    all_gather x2, waiting for transfers between devices, body(): lax.all_gather(piece, ('y', 'z'), axis=0, tiled=False).reshape(4096, width)  61.2 us
    rev x1, local copies, waits for them, and re-layouts, body(): x_rel = jnp.where(xl == 0, x_all, x_all[:, ::-1]).reshape(4096, 512)  37.6 us
    all_to_all x1, blocking collectives, body(): lax.all_to_all(part, ('y', 'z'), split_axis=1, concat_axis=0, tiled=False)  30.3 us
    all_to_all x3, waiting for transfers between devices, spread(): return lax.all_to_all(copies, axes, split_axis=0, concat_axis=0, tiled=True)  22.2 us
    dot_general x2, matrix products, body(): lax.dot_general(c_all, w, (((1,), (1,)), ((), ())), preferred_element_typ...  21.8 us
    ppermute x1, waiting for transfers between devices, body(): lax.ppermute(two[:, 256:], 'xl', SWAP).reshape(4, 2, 128, 256)[:, ::-1]  19 us
    all_to_all x3, starting transfers between devices, spread(): return lax.all_to_all(copies, axes, split_axis=0, concat_axis=0, tiled=True)  19 us
    ppermute x1, waiting for transfers between devices, body(): w_other = lax.ppermute(mine(weight, half, 1, 1 - xl), 'xl', SWAP)  18.6 us
  transfers between devices with their start and end apart: 16, of which 8 were waited for; matrix products, arithmetic and copies ran while one was open for 34% of the time, Pallas kernels for 0%

profile of v1, /device:TPU:0, one launch (start us, length us, event | category | flops | bytes accessed | tf_op | source)
XLA Modules:
  0.0 384.1 jit_solution(14296730057061232586)
XLA Ops:
  8.7 1.7 collective-permute-start
  10.3 11.9 %collective-permute-done = bf16[128,2048]{1,0:T(8,128)(2,1)S(1)} collective-permute-done((bf16[128,2048]{1,0:T(8,128)(2,1)S(1)}, bf16[128,2048]{1,0:T(8,128)(2,1)S(1)}, u32[]{:S(2)}, u32[]{:S(2)}) %collective-permute-start) | collective-permute-done | bytes 524320 | tf_op jit(solution)/shard_map/ppermute | solution.py:36
  25.1 30.3 %all_to_all.33 = bf16[1,64,16,512]{3,1,0,2:T(8,128)(2,1)S(1)} all-to-all(bf16[1,64,16,512]{3,1,0,2:T(8,128)(2,1)S(1)} %copy.17), channel_id=1, replica_groups=mesh['y'=4,'z'=4,'xl'=2,'xh'=2,'c'=2] {'y','z'}, dimensions={2} | all-to-all | bytes 2097152 | tf_op jit(solution)/shard_map/all_to_all | solution.py:40
  57.0 17.1 %collective-permute-done.5 = bf16[16,64,512]{2,1,0:T(8,128)(2,1)S(1)} collective-permute-done((bf16[16,64,512]{2,1,0:T(8,128)(2,1)S(1)}, bf16[16,64,512]{2,1,0:T(8,128)(2,1)S(1)}, u32[]{:S(2)}, u32[]{:S(2)}) %collective-permute-start.5) | collective-permute-done | bytes 1048608 | tf_op jit(solution)/shard_map/ppermute | solution.py:41
  80.1 4.0 %select_bitcast_fusion.1 = (bf16[16,2,1,64,512]{4,3,0,1,2:T(8,128)(2,1)}, bf16[16,2,1,64,512]{4,3,0,1,2:T(8,128)(2,1)}) fusion(bf16[16,2,64,512]{3,2,0,1:T(8,128)(2,1)} %collective-permute-done.6, pred[]{:T(512)S(6)} %eq.33, bf16[16,1,64,512]{3,2,0,1:T(8,128)(2,1)S(1)} %bitcast.65, bf16[16,1,64,512]{3,2,0,1:T(8,128)(2,1)S(1)} %bitcast.56), kind=kLoop, calls=%fused_computation.17 | loop fusion | flops 3145728 | bytes 8388609 | tf_op jit(solution)/shard_map/stack | solution.py:46
  84.1 18.6 %collective-permute-done.1 = bf16[256,2048]{1,0:T(8,128)(2,1)} collective-permute-done((bf16[256,2048]{1,0:T(8,128)(2,1)}, bf16[256,2048]{1,0:T(8,128)(2,1)}, u32[]{:S(2)}, u32[]{:S(2)}) %collective-permute-start.1) | collective-permute-done | bytes 1048608 | tf_op jit(solution)/shard_map/ppermute | solution.py:50
  102.6 11.3 %fusion.7 = f32[4096,512]{1,0:T(8,128)} fusion(bf16[4096,1024]{1,0:T(8,128)(2,1)} %bitcast.72, bf16[256,2048]{1,0:T(8,128)(2,1)} %collective-permute-done.1, bf16[256,2048]{1,0:T(8,128)(2,1)S(1)} %get-tuple-element.21), kind=kOutput, calls=%fused_computation.31 | convolution fusion | flops 4297064448 | bytes 18874368 | tf_op jit(solution)/shard_map/dot_general | solution.py:65
  113.9 61.2 %all-gather.5.cloned.1.call-done = bf16[32,128,1024]{2,1,0:T(8,128)(2,1)} async-done(((bf16[2,128,1024]{2,1,0:T(8,128)(2,1)}), bf16[32,128,1024]{2,1,0:T(8,128)(2,1)}) %all-gather.5.cloned.1.call-update) | async-done | bytes 8388624 | tf_op jit(solution)/shard_map/all_gather | solution.py:56
  175.1 10.5 %convolution_add_fusion = f32[4096,512]{1,0:T(8,128)S(1)} fusion(f32[4096,512]{1,0:T(8,128)} %fusion.7, bf16[4096,1024]{1,0:T(8,128)(2,1)} %bitcast.74, bf16[256,2048]{1,0:T(8,128)(2,1)S(1)} %get-tuple-element.21, bf16[256,2048]{1,0:T(8,128)(2,1)} %collective-permute-done.1), kind=kOutput, calls=%fused_computation.1 | convolution fusion | flops 4299161600 | bytes 27262976 | tf_op jit(solution)/shard_map/dot_general | solution.py:65
  185.6 2.5 dynamic-slice_bitcast_fusion
  188.1 3.1 copy-done.4
  191.6 2.6 copy.18
  194.2 6.9 %reshape.142 = bf16[4096,2,256]{2,1,0:T(2,128)(2,1)} reshape(bf16[16,2,2,64,512]{4,3,2,1,0:T(8,128)(2,1)} %copy.18) | data formatting | bytes 8388608 | tf_op jit(solution)/shard_map/reshape | solution.py:46
  201.1 37.6 %rev.15 = bf16[4096,2,256]{2,1,0:T(2,128)(2,1)} reverse(bf16[4096,2,256]{2,1,0:T(2,128)(2,1)} %reshape.142), dimensions={1} | reverse | bytes 8388608 | tf_op jit(solution)/shard_map/rev | solution.py:47
  238.7 2.6 broadcast_select_fusion
  242.1 7.5 %multiply_reduce_fusion.1 = (f32[512]{0:T(512)S(1)}, f32[1024]{0:T(1024)S(1)}, f32[512,1024]{1,0:T(8,128)S(1)}) fusion(bf16[4096,512]{1,0:T(8,128)(2,1)S(1)} %bitcast.62, bf16[4096,1024]{1,0:T(8,128)(2,1)} %bitcast.73), kind=kOutput, calls=%fused_computation.22 | convolution fusion | flops 4297062912 | bytes 14686208 | tf_op jit(solution)/shard_map/dot_general | solution.py:57
  249.6 5.9 %multiply_reduce_fusion.3 = (f32[512]{0:T(512)S(1)}, f32[1024]{0:T(1024)S(1)}, f32[512,1024]{1,0:T(8,128)}) fusion(bf16[4096,512]{1,0:T(8,128)(2,1)S(1)} %bitcast.63, bf16[4096,1024]{1,0:T(8,128)(2,1)S(1)} %bitcast.77), kind=kOutput, calls=%fused_computation.24 | convolution fusion | flops 4297062912 | bytes 14686208 | tf_op jit(solution)/shard_map/dot_general | solution.py:57
  256.1 4.4 %all-to-all-start.1 = ((f32[8,1,512]{2,1,0:T(1,128)}), f32[8,1,512]{2,1,0:T(1,128)S(1)}, u32[]{:S(2)}, u32[]{:S(2)}) async-start(f32[8,1,512]{2,1,0:T(1,128)} %broadcast_in_dim.18), calls=%async_computation.1 | async-start | bytes 32768 | tf_op jit(solution)/shard_map/all_to_all | solution.py:23
  261.8 2.0 collective-permute-start.9
  266.7 5.3 %all-to-all-start.2 = ((f32[16,1,2048]{2,1,0:T(1,128)}), f32[16,1,2048]{2,1,0:T(1,128)S(1)}, u32[]{:S(2)}, u32[]{:S(2)}) async-start(f32[16,1,2048]{2,1,0:T(1,128)} %broadcast_in_dim.19), calls=%async_computation.2 | async-start | bytes 262144 | tf_op jit(solution)/shard_map/all_to_all | solution.py:23
  272.0 4.5 %bitcast_add_fusion = f32[2,1024,512]{2,1,0:T(8,128)S(1)} fusion(f32[2,1024,512]{2,1,0:T(8,128)} %collective-permute-done.2, f32[2,2,1024,512]{3,2,1,0:T(8,128)} %bitcast.59, s32[]{:T(128)S(6)} %select_n.109), kind=kLoop, calls=%fused_computation.4 | loop fusion | flops 1048576 | bytes 12582916 | tf_op jit(solution)/shard_map/add | solution.py:106
  279.1 2.5 collective-permute-start.3
  282.8 3.1 fusion.3
  288.5 9.4 %all-to-all-start.3 = ((f32[128,1,128]{2,1,0:T(1,128)}), f32[128,1,128]{2,1,0:T(1,128)S(1)}, u32[]{:S(2)}, u32[]{:S(2)}) async-start(f32[128,1,128]{2,1,0:T(1,128)} %broadcast_in_dim.23), calls=%async_computation.3 | async-start | bytes 131072 | tf_op jit(solution)/shard_map/all_to_all | solution.py:23
  297.9 12.7 %collective-permute-done.10 = f32[2048]{0:T(1024)S(1)} collective-permute-done((f32[2048]{0:T(1024)S(1)}, f32[2048]{0:T(1024)S(1)}, u32[]{:S(2)}, u32[]{:S(2)}) %collective-permute-start.10) | collective-permute-done | bytes 8224 | tf_op jit(solution)/shard_map/ppermute | solution.py:80
  311.1 22.2 %all-to-all-done.3 = f32[128,1,128]{2,1,0:T(1,128)S(1)} async-done(((f32[128,1,128]{2,1,0:T(1,128)}), f32[128,1,128]{2,1,0:T(1,128)S(1)}, u32[]{:S(2)}, u32[]{:S(2)}) %all-to-all-start.3) | async-done | bytes 65568 | tf_op jit(solution)/shard_map/all_to_all | solution.py:23
  336.0 2.6 reshape.138
  338.6 8.1 %rev.12 = f32[4,2,128,2,256]{4,3,2,1,0:T(2,128)} reverse(f32[4,2,128,2,256]{4,3,2,1,0:T(2,128)S(1)} %reshape.138), dimensions={1,3} | reverse | bytes 4194304 | tf_op jit(solution)/shard_map/rev | solution.py:110
  346.7 1.9 copy.24
  351.3 2.2 fusion
  353.4 2.5 maximum_select_fusion
  356.0 19.0 %collective-permute-done.4 = f32[1024,256]{1,0:T(8,128)S(1)} collective-permute-done((f32[1024,256]{1,0:T(8,128)S(1)}, f32[1024,256]{1,0:T(8,128)S(1)}, u32[]{:S(2)}, u32[]{:S(2)}) %collective-permute-start.4) | collective-permute-done | bytes 1048608 | tf_op jit(solution)/shard_map/ppermute | solution.py:115
  (85 shorter events, 27.7 us)
Async XLA Ops:
  7.2 16.9 %copy-start = (bf16[128,8192]{1,0:T(8,128)(2,1)S(1)}, bf16[128,8192]{1,0:T(8,128)(2,1)}, u32[]{:S(2)}) copy-start(bf16[128,8192]{1,0:T(8,128)(2,1)} %param.5) | copy-start | bytes 6291460
  7.2 95.4 %all-gather.7.cloned.1.call-start = ((), (), s32[]{:S(2)}) async-start(), calls=%async_computation.5 | async-start | bytes 8912896 | tf_op jit(solution)/shard_map/all_gather | solution.py:56
  8.7 13.6 %collective-permute-start = (bf16[128,2048]{1,0:T(8,128)(2,1)S(1)}, bf16[128,2048]{1,0:T(8,128)(2,1)S(1)}, u32[]{:S(2)}, u32[]{:S(2)}) collective-permute-start(bf16[128,2048]{1,0:T(8,128)(2,1)S(1)} %get-tuple-element.26), channel_id=1, source_target_pairs={{0,4},{4,0},{1,5},{5,1},{2,6},{6,2},{3,7},{7,3},{8,12},{12,8},{9,1... | collective-permute-start | bytes 1572872 | tf_op jit(solution)/shard_map/ppermute | solution.py:36
  23.3 151.8 %all-gather.5.cloned.1.call-start = ((), (), s32[]{:S(2)}) async-start(), calls=%async_computation.4 | async-start | bytes 8912896 | tf_op jit(solution)/shard_map/all_gather | solution.py:56
  55.5 18.6 %collective-permute-start.5 = (bf16[16,64,512]{2,1,0:T(8,128)(2,1)S(1)}, bf16[16,64,512]{2,1,0:T(8,128)(2,1)S(1)}, u32[]{:S(2)}, u32[]{:S(2)}) collective-permute-start(bf16[16,64,512]{2,1,0:T(8,128)(2,1)S(1)} %bitcast.54), channel_id=1, source_target_pairs={{0,4},{4,0},{1,5},{5,1},{2,6},{6,2},{3,7},{7,3},{8,12},{12,8},{9,1... | collective-permute-start | bytes 3145736 | tf_op jit(solution)/shard_map/ppermute | solution.py:41
  74.1 2.4 copy-start.9
  75.6 3.5 copy-start.12
  75.6 4.5 %collective-permute-start.6 = (bf16[16,2,64,512]{3,2,0,1:T(8,128)(2,1)}, bf16[16,2,64,512]{3,2,0,1:T(8,128)(2,1)}, u32[]{:S(2)}, u32[]{:S(2)}) collective-permute-start(bf16[16,2,64,512]{3,2,0,1:T(8,128)(2,1)} %pad_maximum_fusion.1), channel_id=1, source_target_pairs={{0,1},{1,0},{2,3},{3,2},{4,5},{5,4},{6,7},{7,6},{8,9},{9,8},{10,11... | collective-permute-start | bytes 6291464 | tf_op jit(solution)/shard_map/ppermute | solution.py:43
  77.6 25.0 %collective-permute-start.1 = (bf16[256,2048]{1,0:T(8,128)(2,1)}, bf16[256,2048]{1,0:T(8,128)(2,1)}, u32[]{:S(2)}, u32[]{:S(2)}) collective-permute-start(bf16[256,2048]{1,0:T(8,128)(2,1)} %get-tuple-element.22), channel_id=1, source_target_pairs={{0,4},{4,0},{1,5},{5,1},{2,6},{6,2},{3,7},{7,3},{8,12},{12,8},{9,1... | collective-permute-start | bytes 3145736 | tf_op jit(solution)/shard_map/ppermute | solution.py:50
  79.1 202.6 %collective-permute-start.7 = (f32[256]{0:T(256)S(1)}, f32[256]{0:T(256)S(1)}, u32[]{:S(2)}, u32[]{:S(2)}) collective-permute-start(f32[256]{0:T(256)S(1)} %copy-done.12), channel_id=1, source_target_pairs={{0,4},{4,0},{1,5},{5,1},{2,6},{6,2},{3,7},{7,3},{8,12},{12,8},{9,1... | collective-permute-start | bytes 3080 | tf_op jit(solution)/shard_map/ppermute | solution.py:73
  185.6 5.6 %copy-start.4 = (f32[4096,512]{1,0:T(8,128)}, f32[4096,512]{1,0:T(8,128)S(1)}, u32[]{:S(2)}) copy-start(f32[4096,512]{1,0:T(8,128)S(1)} %convolution_add_fusion) | copy-start | bytes 25165828
  185.6 5.6 %copy-start.6 = (bf16[16,2,1,64,512]{4,3,0,1,2:T(8,128)(2,1)S(1)}, bf16[16,2,1,64,512]{4,3,0,1,2:T(8,128)(2,1)}, u32[]{:S(2)}) copy-start(bf16[16,2,1,64,512]{4,3,0,1,2:T(8,128)(2,1)} %get-tuple-element.13) | copy-start | bytes 6291460
  185.6 5.6 %copy-start.7 = (bf16[16,2,1,64,512]{4,3,0,1,2:T(8,128)(2,1)S(1)}, bf16[16,2,1,64,512]{4,3,0,1,2:T(8,128)(2,1)}, u32[]{:S(2)}) copy-start(bf16[16,2,1,64,512]{4,3,0,1,2:T(8,128)(2,1)} %get-tuple-element.14) | copy-start | bytes 6291460
  191.2 80.8 %collective-permute-start.2 = (f32[2,1024,512]{2,1,0:T(8,128)}, f32[2,1024,512]{2,1,0:T(8,128)}, u32[]{:S(2)}, u32[]{:S(2)}) collective-permute-start(f32[2,1024,512]{2,1,0:T(8,128)} %dynamic-slice_bitcast_fusion), channel_id=1, source_target_pairs={{0,1},{1,0},{2,3},{3,2},{4,5},{5,4},{6,7},{7,6},{8,9},{9,8},{10,11... | collective-permute-start | bytes 12582920 | tf_op jit(solution)/shard_map/ppermute | solution.py:106
  241.3 8.3 %slice-start = ((s8[8388608]{0:T(1024)(128)(4,1)}), s8[4194304]{0:T(1024)(128)(4,1)S(1)}, s32[]{:S(2)}) async-start(s8[8388608]{0:T(1024)(128)(4,1)} %bitcast.75), calls=%async_computation.6 | async-start | bytes 8388608
  242.1 7.5 %slice-start.1 = ((s8[8388608]{0:T(1024)(128)(4,1)}), s8[4194304]{0:T(1024)(128)(4,1)S(1)}, s32[]{:S(2)}) async-start(s8[8388608]{0:T(1024)(128)(4,1)} %bitcast.75), calls=%async_computation.7 | async-start | bytes 8388608
  256.1 9.8 %all-to-all-start.1 = ((f32[8,1,512]{2,1,0:T(1,128)}), f32[8,1,512]{2,1,0:T(1,128)S(1)}, u32[]{:S(2)}, u32[]{:S(2)}) async-start(f32[8,1,512]{2,1,0:T(1,128)} %broadcast_in_dim.18), calls=%async_computation.1 | async-start | bytes 32768 | tf_op jit(solution)/shard_map/all_to_all | solution.py:23
  260.5 3.3 copy-start.5
  261.8 88.5 %collective-permute-start.9 = (f32[256,1024]{1,0:T(8,128)}, f32[256,1024]{1,0:T(8,128)}, u32[]{:S(2)}, u32[]{:S(2)}) collective-permute-start(f32[256,1024]{1,0:T(8,128)} %get-tuple-element.18), channel_id=1, source_target_pairs={{0,4},{4,0},{1,5},{5,1},{2,6},{6,2},{3,7},{7,3},{8,12},{12,8},{9,1... | collective-permute-start | bytes 3145736 | tf_op jit(solution)/shard_map/ppermute | solution.py:63
  265.2 85.1 %collective-permute-start.8 = (f32[256,1024]{1,0:T(8,128)}, f32[256,1024]{1,0:T(8,128)}, u32[]{:S(2)}, u32[]{:S(2)}) collective-permute-start(f32[256,1024]{1,0:T(8,128)} %get-tuple-element.16), channel_id=1, source_target_pairs={{0,4},{4,0},{1,5},{5,1},{2,6},{6,2},{3,7},{7,3},{8,12},{12,8},{9,1... | collective-permute-start | bytes 3145736 | tf_op jit(solution)/shard_map/ppermute | solution.py:63
  266.7 15.7 %all-to-all-start.2 = ((f32[16,1,2048]{2,1,0:T(1,128)}), f32[16,1,2048]{2,1,0:T(1,128)S(1)}, u32[]{:S(2)}, u32[]{:S(2)}) async-start(f32[16,1,2048]{2,1,0:T(1,128)} %broadcast_in_dim.19), calls=%async_computation.2 | async-start | bytes 262144 | tf_op jit(solution)/shard_map/all_to_all | solution.py:23
  276.5 2.6 copy-start.2
  276.5 5.9 %copy-start.11 = (f32[4096]{0:T(1024)S(1)}, f32[4096]{0:T(1024)}, u32[]{:S(2)}) copy-start(f32[4096]{0:T(1024)} %param.9) | copy-start | bytes 49156
  279.1 56.9 %collective-permute-start.3 = (f32[1024,512]{1,0:T(8,128)}, f32[1024,512]{1,0:T(8,128)}, u32[]{:S(2)}, u32[]{:S(2)}) collective-permute-start(f32[1024,512]{1,0:T(8,128)} %dynamic-slice_bitcast_fusion.1), channel_id=1, source_target_pairs={{0,6},{6,0},{2,4},{4,2},{1,7},{7,1},{3,5},{5,3},{8,14},{14,8},{10,... | collective-permute-start | bytes 6291464 | tf_op jit(solution)/shard_map/ppermute | solution.py:114
  282.3 68.0 %copy-start.10 = (f32[256]{0:T(256)}, f32[256]{0:T(256)S(1)}, u32[]{:S(2)}) copy-start(f32[256]{0:T(256)S(1)} %get-tuple-element.12) | copy-start | bytes 3076
  282.4 28.1 %collective-permute-start.10 = (f32[2048]{0:T(1024)S(1)}, f32[2048]{0:T(1024)S(1)}, u32[]{:S(2)}, u32[]{:S(2)}) collective-permute-start(f32[2048]{0:T(1024)S(1)} %multiply_add_fusion), channel_id=1, source_target_pairs={{0,4},{4,0},{1,5},{5,1},{2,6},{6,2},{3,7},{7,3},{8,12},{12,8},{9,1... | collective-permute-start | bytes 24584 | tf_op jit(solution)/shard_map/ppermute | solution.py:80
  288.5 44.9 %all-to-all-start.3 = ((f32[128,1,128]{2,1,0:T(1,128)}), f32[128,1,128]{2,1,0:T(1,128)S(1)}, u32[]{:S(2)}, u32[]{:S(2)}) async-start(f32[128,1,128]{2,1,0:T(1,128)} %broadcast_in_dim.23), calls=%async_computation.3 | async-start | bytes 131072 | tf_op jit(solution)/shard_map/all_to_all | solution.py:23
  346.7 2.8 copy-start.3
  350.0 1.2 copy-start.8
  350.2 24.8 %collective-permute-start.4 = (f32[1024,256]{1,0:T(8,128)S(1)}, f32[1024,256]{1,0:T(8,128)S(1)}, u32[]{:S(2)}, u32[]{:S(2)}) collective-permute-start(f32[1024,256]{1,0:T(8,128)S(1)} %get-tuple-element.19), channel_id=1, source_target_pairs={{0,4},{4,0},{1,5},{5,1},{2,6},{6,2},{3,7},{7,3},{8,12},{12,8},{9,1... | collective-permute-start | bytes 3145736 | tf_op jit(solution)/shard_map/ppermute | solution.py:115
  353.4 22.7 %copy-start.1 = (bf16[128,8192]{1,0:T(8,128)(2,1)S(1)}, bf16[128,8192]{1,0:T(8,128)(2,1)}, u32[]{:S(2)}) copy-start(bf16[128,8192]{1,0:T(8,128)(2,1)} %param.5) | copy-start | bytes 6291460
Sparse Core Ops, SparseCore 0:
  23.5 78.4 all-gather.6
  104.6 70.4 all-gather.4

commit v2 on v0

v2 whole, which is shorter than its diff:
```python
import math

import jax
import jax.numpy as jnp
from jax import lax
from jax.experimental import pallas as pl
from jax.experimental.pallas import tpu as pltpu
from jax.sharding import Mesh, PartitionSpec as P

D = 8192
FF = 16384
TOKENS = 4096
F32 = jnp.float32
BF16 = jnp.bfloat16

decay_rate = 0.84
tiny_eps = 1e-30

AXES = ("y", "z", "xl", "xh", "c")
SIZES = (4, 4, 2, 2, 2)
SWAP = [(0, 1), (1, 0)]
DIAG = [(0, 3), (3, 0), (1, 2), (2, 1)]
WIDE = 1024
MIB = 1 << 20
SHORT = pl.CostEstimate(flops=1, bytes_accessed=1, transcendentals=0)
LONG = pl.CostEstimate(flops=2 * 10**10, bytes_accessed=1, transcendentals=0)


def spread(value, axes, count):
    copies = jnp.broadcast_to(value[None], (count,) + value.shape)
    return lax.all_to_all(copies, axes, split_axis=0, concat_axis=0, tiled=True)


def mine(a, n, axis, index):
    return lax.dynamic_slice_in_dim(a, index * n, n, axis)


def shift(a, axis, k):
    return lax.ppermute(a, axis, [(i, (i + k) % 4) for i in range(4)])


def near_three(start, axis):
    return [shift(start, axis, 1), shift(start, axis, 3), shift(start, axis, 2)]


def spread_pieces(start, three, then):
    a, b, c = three
    p, q = jnp.concatenate([start, a]), jnp.concatenate([b, c])
    p1, q3 = shift(p, then, 1), shift(q, then, 3)
    q1, p3 = shift(q, then, 1), shift(p, then, 3)
    p2, q2 = shift(p1, then, 1), shift(q3, then, 3)
    pieces = [p, q, p1, q1, p3, q3, p2, q2]
    places = []
    for d in (0, 1, 3, 2):
        places += [(0, d), (1, d), (3, d), (2, d)]
    return pieces, places


def transposed_tokens(where, blocks):
    def kernel(where_ref, a_ref, b_ref, c_ref, d_ref, out_ref, hold):
        own_x, own_c = where_ref[0] * 128, where_ref[2] * 64
        other_x, other_c = 128 - own_x, 64 - own_c
        for ref, row in (
            (a_ref, own_x + own_c),
            (b_ref, other_x + own_c),
            (c_ref, own_x + other_c),
            (d_ref, other_x + other_c),
        ):
            hold[pl.ds(pl.multiple_of(row, 64), 64), :] = ref[0]
        out_ref[...] = hold[...].T

    block = pl.BlockSpec((1, 64, 512), lambda i, where_ref: (i, 0, 0))
    return pl.pallas_call(
        kernel,
        grid_spec=pltpu.PrefetchScalarGridSpec(
            num_scalar_prefetch=1,
            grid=(16,),
            in_specs=[block] * 4,
            out_specs=pl.BlockSpec((512, 256), lambda i, where_ref: (0, i)),
            scratch_shapes=[pltpu.VMEM((256, 512), BF16)],
        ),
        out_shape=jax.ShapeDtypeStruct((512, TOKENS), BF16),
        cost_estimate=LONG,
    )(where, *blocks)


def squares_of(g, row_ref, col_ref, columns, first):
    squares = g * g
    rows, width = g.shape
    col_ref[:, columns] = jnp.sum(squares.reshape(rows // 8, 8, width), 0)
    sums = squares[:, :128]
    for k in range(128, width, 128):
        sums = sums + squares[:, k : k + 128]
    if first is True:
        row_ref[...] = sums
    else:
        row_ref[...] += sums


def grad_shapes(width):
    return (
        jax.ShapeDtypeStruct((256, width), F32),
        jax.ShapeDtypeStruct((2, 256, width // 2), F32),
        jax.ShapeDtypeStruct((512, 128), F32),
        jax.ShapeDtypeStruct((8, width), F32),
    )


def own_other(a, first, axis):
    low, high = (a[:256], a[256:]) if axis == 0 else (a[:, :256], a[:, 256:])
    return jnp.where(first, low, high), jnp.where(first, high, low)


def gradient_of_pieces(xt, pieces, index, xl):
    width = pieces[0].shape[1]
    n = 2 * len(pieces)
    tile = 256

    def kernel(xl_ref, index_ref, xt_ref, *refs):
        ins = refs[: len(pieces)]
        c_ref, own_ref, other_ref, row_ref, col_ref, hold, in_sems, out_sem = refs[len(pieces) :]
        copies = []
        for k in range(n):
            copies.append(
                pltpu.make_async_copy(
                    ins[k // 2].at[pl.ds(128 * (k % 2), 128)], hold.at[index_ref[k]], in_sems.at[k]
                )
            )
            copies[-1].start()
        for copy in copies:
            copy.wait()
        write = pltpu.make_async_copy(hold, c_ref, out_sem)
        write.start()
        for first in range(0, width, tile):
            block = hold[:, :, first : first + tile].reshape(TOKENS, tile)
            g = jnp.dot(xt_ref[...], block, preferred_element_type=F32) * float(TOKENS) ** (-0.5)
            own, other = own_other(g, xl_ref[0] == 0, 0)
            own_ref[:, first : first + tile] = own
            part, place = divmod(first, width // 2)
            other_ref[part, :, place : place + tile] = other
            squares_of(g, row_ref, col_ref, slice(first, first + tile), first == 0)
        write.wait()

    vmem = pl.BlockSpec(memory_space=pltpu.VMEM)
    anywhere = pl.BlockSpec(memory_space=pl.ANY)
    smem = pl.BlockSpec(memory_space=pltpu.SMEM)
    out = pl.pallas_call(
        kernel,
        out_shape=(jax.ShapeDtypeStruct((n, 128, width), BF16),) + grad_shapes(width),
        in_specs=[smem, smem, vmem] + [anywhere] * len(pieces),
        out_specs=(anywhere,) + (vmem,) * 4,
        scratch_shapes=[
            pltpu.VMEM((n, 128, width), BF16),
            pltpu.SemaphoreType.DMA((n,)),
            pltpu.SemaphoreType.DMA,
        ],
        compiler_params=pltpu.CompilerParams(vmem_limit_bytes=56 * MIB),
        cost_estimate=SHORT,
    )(xl, index, xt, *pieces)
    return (out[0].reshape(TOKENS, width),) + tuple(out[1:])


def gradient(xt, c_all, xl):
    width = c_all.shape[1]
    tile = 256

    def kernel(xl_ref, xt_ref, c_ref, own_ref, other_ref, row_ref, col_ref):
        g = jnp.dot(xt_ref[...], c_ref[...], preferred_element_type=F32) * float(TOKENS) ** (-0.5)
        own_ref[...], other_ref[0] = own_other(g, xl_ref[0] == 0, 0)

        @pl.when(pl.program_id(0) == 0)
        def _():
            row_ref[...] = jnp.zeros_like(row_ref)

        squares_of(g, row_ref, col_ref, slice(None), False)

    return pl.pallas_call(
        kernel,
        grid=(width // tile,),
        out_shape=grad_shapes(width),
        in_specs=[
            pl.BlockSpec(memory_space=pltpu.SMEM),
            pl.BlockSpec((512, TOKENS), lambda j: (0, 0)),
            pl.BlockSpec((TOKENS, tile), lambda j: (0, j)),
        ],
        out_specs=(
            pl.BlockSpec((256, tile), lambda j: (0, j)),
            pl.BlockSpec((1, 256, tile), lambda j: (j // (width // tile // 2), 0, j % (width // tile // 2))),
            pl.BlockSpec((512, 128), lambda j: (0, 0)),
            pl.BlockSpec((8, tile), lambda j: (0, j)),
        ),
        compiler_params=pltpu.CompilerParams(vmem_limit_bytes=56 * MIB),
        cost_estimate=SHORT,
    )(xl, xt, c_all)


NT = (((1,), (1,)), ((), ()))


def terms(where, far, c_1, c_2, w_all, received=None):
    w1, w2 = c_1.shape[1], c_2.shape[1]
    keep = received is not None

    def kernel(where_ref, c1_ref, c2_ref, w_ref, *refs):
        t = lax.dot_general(c1_ref[...], w_ref[:, :w1], NT, preferred_element_type=F32) + lax.dot_general(
            c2_ref[...], w_ref[:, w1:], NT, preferred_element_type=F32
        )
        if not keep:
            refs[0][...] = t
            return
        got_ref, both, own, other = refs
        t = t + got_ref[...]

        @pl.when(pl.program_id(0) == 0)
        def _():
            both[:, :256], both[:, 256:] = own_other(t, where_ref[0] == 0, 1)

        @pl.when(pl.program_id(0) == 1)
        def _():
            own[...], other[...] = own_other(t, where_ref[0] == 0, 1)

    def rows(i, where_ref):
        high = 1 - where_ref[1] if far else where_ref[1]
        core = where_ref[2] if keep else 1 - where_ref[2]
        return ((2 * high + core) * 2 + i, 0)

    step = pl.BlockSpec((512, 512), lambda i, where_ref: (i, 0))
    block = jax.ShapeDtypeStruct((512, 256), F32)
    whole = [pl.BlockSpec((512, n), lambda i, where_ref: (0, 0)) for n in (512, 256, 256)]
    return pl.pallas_call(
        kernel,
        grid_spec=pltpu.PrefetchScalarGridSpec(
            num_scalar_prefetch=1,
            grid=(2,),
            in_specs=[
                pl.BlockSpec((512, w1), rows),
                pl.BlockSpec((512, w2), rows),
                pl.BlockSpec((512, w1 + w2), lambda i, where_ref: (0, 0)),
            ]
            + [step] * keep,
            out_specs=whole if keep else step,
        ),
        out_shape=[jax.ShapeDtypeStruct((512, 512), F32), block, block]
        if keep
        else jax.ShapeDtypeStruct((1024, 512), F32),
        compiler_params=pltpu.CompilerParams(vmem_limit_bytes=56 * MIB),
        cost_estimate=SHORT,
    )(where, c_1, c_2, w_all, *((received,) if keep else ()))


def clipped(where, scale, row_factor, own, received, own_factors, received_factors):
    half = sum(g.shape[1] for g in own)
    tile = math.gcd(*(g.shape[1] for g in own + received))
    steps = half // tile
    blocks, counts = list(own) + list(received), [g.shape[1] // tile for g in own + received]
    starts = [sum(counts[:k]) for k in range(len(counts))]

    def kernel(where_ref, scale_ref, row_ref, col_ref, *refs):
        out_ref = refs[-1]
        j = pl.program_id(0)
        for ref, start, count in zip(refs, starts, counts):

            @pl.when(jnp.logical_and(j >= start, j < start + count))
            def _():
                out_ref[...] = ref[...] * (row_ref[...] * scale_ref[0]) * col_ref[...]

    def spec(start, count):
        return pl.BlockSpec((256, tile), lambda j, where_ref: (0, jnp.clip(j - start, 0, count - 1)))

    def place(j, where_ref):
        own_half = jnp.where(j < steps, where_ref[0], 1 - where_ref[0])
        return (0, own_half * steps + j % steps)

    return pl.pallas_call(
        kernel,
        grid_spec=pltpu.PrefetchScalarGridSpec(
            num_scalar_prefetch=1,
            grid=(2 * steps,),
            in_specs=[
                pl.BlockSpec(memory_space=pltpu.SMEM),
                pl.BlockSpec((256, 1), lambda j, where_ref: (0, 0)),
                pl.BlockSpec((1, tile), lambda j, where_ref: (0, j)),
            ]
            + [spec(s, n) for s, n in zip(starts, counts)],
            out_specs=pl.BlockSpec((256, tile), place),
        ),
        out_shape=jax.ShapeDtypeStruct((256, 2 * half), F32),
        compiler_params=pltpu.CompilerParams(vmem_limit_bytes=56 * MIB),
        cost_estimate=SHORT,
    )(
        where,
        scale.reshape(1),
        row_factor[:, None],
        jnp.concatenate([own_factors, received_factors])[None, :],
        *blocks,
    )


def body(tokens, cotangent, weight, row_prev, col_prev):
    y, z = lax.axis_index("y"), lax.axis_index("z")
    xl, xh, c = lax.axis_index("xl"), lax.axis_index("xh"), lax.axis_index("c")
    half = cotangent.shape[1] // 2
    first_xl = xl == 0
    after = lax.optimization_barrier

    where = jnp.stack([xl, xh, c]).astype(jnp.int32)

    away = mine(cotangent, half, 1, 1 - xl)
    part, away = after((mine(tokens, 64, 0, c), away))
    other = lax.ppermute(away, "xl", SWAP)
    part = part.reshape(64, 16, 512)
    xo = lax.all_to_all(part, ("y", "z"), split_axis=1, concat_axis=0, tiled=False)

    own = mine(cotangent, half, 1, xl)
    row_prev_other = lax.ppermute(row_prev, "xl", SWAP)
    own, other, xo, row_prev_other = after((own, other, xo, row_prev_other))
    own_1, own_2 = own[:, :WIDE], own[:, WIDE:]
    other_1, other_2 = other[:, :WIDE], other[:, WIDE:]
    shard = jnp.where(first_xl, jnp.stack([own_2, other_2]), jnp.stack([other_2, own_2]))
    c_2 = lax.all_gather(shard, ("y", "z"), axis=0, tiled=False).reshape(TOKENS, half - WIDE)
    pieces, places = spread_pieces(own_1, near_three(own_1, "y"), "z")
    index = [((y - dy) % 4 * 4 + (z - dz) % 4) * 2 + xl for dy, dz in places]
    more, places = spread_pieces(other_1, near_three(other_1, "z"), "y")
    index += [((y - dy) % 4 * 4 + (z - dz) % 4) * 2 + 1 - xl for dz, dy in places]

    xp = lax.ppermute(xo, "xl", SWAP)
    to = lax.ppermute(xo, "c", SWAP)
    near = [pieces[2], pieces[5], more[2], more[5]]
    xp, near = after((xp, near))
    pieces[2], pieces[5], more[2], more[5] = near
    tp = lax.ppermute(xp, "c", SWAP)
    xt = transposed_tokens(where, (xo, xp, to, tp))
    w_own = mine(weight, half, 1, xl)
    w_other = lax.ppermute(mine(weight, half, 1, 1 - xl), "xl", SWAP)
    w_all = jnp.where(first_xl, jnp.concatenate([w_own, w_other]), jnp.concatenate([w_other, w_own]))
    w_all, xt, last = after((w_all, xt, pieces[6:] + more[6:]))
    pieces[6:], more[6:] = last[:2], last[2:]

    c_1, g_1, send_1, rows_1, cols_1 = gradient_of_pieces(
        xt, pieces + more, jnp.stack(index).astype(jnp.int32), where
    )
    received_1a = lax.ppermute(send_1[0], "xl", SWAP)
    received_1b = lax.ppermute(send_1[1], "xl", SWAP)
    w_all, _ = after((w_all, rows_1))
    far_terms = terms(where, True, c_1, c_2, w_all)
    far_core = lax.ppermute(far_terms, "c", SWAP)
    xt, _ = after((xt, far_terms))
    g_2, send_2, rows_2, cols_2 = gradient(xt, c_2, where)
    received_2 = lax.ppermute(send_2, "xl", SWAP)

    cols = jnp.sum(jnp.concatenate([cols_1, cols_2], 1), 0)
    cols, received_1a = after((cols, received_1a))
    col_sum = jnp.sum(spread(cols, ("y", "z"), 16), 0)
    w_all, _ = after((w_all, rows_2))
    near_terms = terms(where, False, c_1, c_2, w_all)
    near_core = lax.ppermute(near_terms, "c", SWAP)
    col_prev_mine = mine(col_prev, half, 0, xl)
    col_half = decay_rate * col_prev_mine + (1.0 - decay_rate) * (col_sum / D + tiny_eps)

    def over_columns(g, col):
        return jnp.sum(g * g * (1.0 / col)[None, :], 1)

    col_1, col_2 = col_half[:WIDE], col_half[WIDE:]
    over_own = over_columns(g_1, col_1) + over_columns(g_2, col_2)
    over_other, first = 0.0, 0
    for g in (send_1[0], send_1[1], send_2[0], send_2[1]):
        over_other = over_other + over_columns(g, col_half[first : first + g.shape[1]])
        first += g.shape[1]
    plain = jnp.sum(rows_1 + rows_2, 1)
    plain_own, plain_other = own_other(plain, first_xl, 0)
    sums = jnp.stack([plain_own, over_own, plain_other, over_other])
    sums, received_1b = after((sums, received_1b))
    seen = spread(sums, ("xl", "xh", "c"), 8).reshape(2, 4, 4, 256)
    seen, received_2 = after((seen, received_2))
    same = jnp.sum(jnp.where(first_xl, seen[0], seen[1]), 0)
    cross = jnp.sum(jnp.where(first_xl, seen[1], seen[0]), 0)
    row_sum = jnp.concatenate([same[0] + cross[2], same[2] + cross[0]])
    row_over = jnp.concatenate([same[1] + cross[3], same[3] + cross[1]])
    row_prev_two = jnp.concatenate([row_prev, row_prev_other])
    row_next = decay_rate * row_prev_two + (1.0 - decay_rate) * (row_sum / FF + tiny_eps)
    row_own = row_next[:256]

    send_a, far_give, far_keep = terms(where, True, c_1, c_2, w_all, far_core)
    got_a = lax.ppermute(send_a, ("xl", "xh"), DIAG)
    got_far = lax.ppermute(far_give, "xl", SWAP)
    keep_a, own_b, give_b = terms(where, False, c_1, c_2, w_all, near_core)
    got_b = lax.ppermute(give_b, "xl", SWAP)
    last_b = lax.ppermute(far_keep + got_far, ("xl", "xh"), DIAG)
    last_a = lax.ppermute(keep_a[:, 256:] + got_a[:, :256], "xl", SWAP)
    total_a = (keep_a[:, :256] + got_a[:, 256:]) + last_a
    total_b = (own_b + got_b) + last_b
    total = jnp.concatenate([total_a.astype(BF16), total_b.astype(BF16)])

    lane = lax.broadcasted_iota(jnp.int32, (128,), 0)
    pair = jnp.where(lane == 0, jnp.sum(row_over / row_next), jnp.where(lane == 1, jnp.sum(row_next), 0.0))
    totals = jnp.sum(spread(pair, ("y", "z"), 16), 0)
    col_other = lax.ppermute(col_half, "xl", SWAP)
    totals, col_other = after((totals, col_other))
    row_mean = totals[1] / D
    update_rms = jnp.sqrt(row_mean * (totals[0] / (D * FF)))
    scale = jnp.sqrt(row_mean) / jnp.maximum(1.0, update_rms)
    update = clipped(
        where,
        scale,
        1.0 / jnp.sqrt(row_own),
        (g_1, g_2),
        (received_1a, received_1b, received_2[0], received_2[1]),
        1.0 / jnp.sqrt(col_half),
        1.0 / jnp.sqrt(col_other),
    )
    col_next = jnp.where(
        first_xl, jnp.concatenate([col_half, col_other]), jnp.concatenate([col_other, col_half])
    )

    return (total, update, row_own, col_next, update_rms)


def solution(mesh):
    fine = Mesh(mesh.devices.reshape(SIZES), AXES)
    fsdp, mp = ("y", "z", "xl"), ("xh", "c")
    in_specs = (P(fsdp, None), P(fsdp, mp), P(fsdp, mp), P(fsdp), P(mp))
    out_specs = (P(mp, fsdp), P(fsdp, mp), P(fsdp), P(mp), P())
    return jax.shard_map(body, mesh=fine, in_specs=in_specs, out_specs=out_specs, check_vma=False)
```

time: 1060 us -> 276 us (0.26)
  waiting for transfers between devices: 716 us -> 92.8 us
  blocking collectives: 269 us -> 0 us
  Pallas kernels: 0 us -> 69.6 us
  starting transfers between devices: 0.08 us -> 61.3 us
  matrix products: 34.3 us -> 0 us
    all_gather x1, waiting for transfers between devices: 715 us -> 0.01 us  [body(): lax.all_gather(shard, ('y', 'z'), axis=0, tiled=False)]
    psum x3 -> x0, blocking collectives: 224 us -> none  [the longest x1 154 us: body(): row_total = lax.psum(jnp.sum(row_next), 'fsdp')]
    ppermute x0 -> x35, waiting for transfers between devices: none -> 73.7 us  [the longest x18 47.3 us: shift(): return lax.ppermute(a, axis, [(i, (i + k) % 4) for i in range(4)])]
    pallas_call x0 -> x8, Pallas kernels: none -> 69.6 us  [the longest x4 28.8 us: terms(): pl.pallas_call(kernel, grid_spec=pltpu.PrefetchScalarGridSpec(num_scalar_...]
    all_to_all x1 -> x0, blocking collectives: 45.8 us -> none  [body(): lax.all_to_all(tokens, 'fsdp', split_axis=1, concat_axis=0, tiled=True)]
    ppermute x0 -> x35, starting transfers between devices: none -> 38.8 us  [the longest x18 22.6 us: shift(): return lax.ppermute(a, axis, [(i, (i + k) % 4) for i in range(4)])]
    dot_general x2 -> x0, matrix products: 34.3 us -> none  [the longest x1 17.2 us: body(): lax.dot_general(gathered, weight, (((1,), (1,)), ((), ())), preferred_ele...]
    all_to_all x0 -> x4, starting transfers between devices: none -> 22.4 us  [the longest x3 14.2 us: spread(): return lax.all_to_all(copies, axes, split_axis=0, concat_axis=0, tiled=True)]
  transfers between devices with their start and end apart: 2 -> 40, of which waited for: 1 -> 17; matrix products, arithmetic and copies ran while one was open for 3% -> 9% of each run, Pallas kernels for 0% -> 25%
where the time goes in v2:
time: 276 us; the launch traced here: 274 us
  waiting for transfers between devices  92.8 us (34%)
  Pallas kernels  69.6 us (25%)
  starting transfers between devices  61.3 us (22%)
  between operations  17.7 us (6%)
  local copies, waits for them, and re-layouts  16.7 us (6%)
  other arithmetic  15.7 us (6%)
    ppermute x18, waiting for transfers between devices, shift(): return lax.ppermute(a, axis, [(i, (i + k) % 4) for i in range(4)])  47.3 us
    pallas_call x4, Pallas kernels, terms(): pl.pallas_call(kernel, grid_spec=pltpu.PrefetchScalarGridSpec(num_scalar_...  28.8 us
    ppermute x18, starting transfers between devices, shift(): return lax.ppermute(a, axis, [(i, (i + k) % 4) for i in range(4)])  22.6 us
    all_to_all x3, waiting for transfers between devices, spread(): return lax.all_to_all(copies, axes, split_axis=0, concat_axis=0, tiled=True)  14.9 us
    all_to_all x3, starting transfers between devices, spread(): return lax.all_to_all(copies, axes, split_axis=0, concat_axis=0, tiled=True)  14.2 us
    pallas_call x1, Pallas kernels, gradient_of_pieces(): pl.pallas_call(kernel, out_shape=(jax.ShapeDtypeStruct((n, 128, width), B...  11.9 us
    pallas_call x1, Pallas kernels, transposed_tokens(): pl.pallas_call(kernel, grid_spec=pltpu.PrefetchScalarGridSpec(num_scalar_...  11.6 us
    ppermute x1, waiting for transfers between devices, body(): row_prev_other = lax.ppermute(row_prev, 'xl', SWAP)  11.4 us
  transfers between devices with their start and end apart: 40, of which 17 were waited for; matrix products, arithmetic and copies ran while one was open for 9% of the time, Pallas kernels for 25%

profile of v2, /device:TPU:0, one launch (start us, length us, event | category | flops | bytes accessed | tf_op | source)
XLA Modules:
  0.0 273.9 jit_solution(16389420546980181369)
XLA Ops:
  11.0 8.2 %all-to-all-start = ((bf16[1,64,16,512]{3,1,0,2:T(8,128)(2,1)}), bf16[1,64,16,512]{3,1,0,2:T(8,128)(2,1)}, u32[]{:S(2)}, u32[]{:S(2)}) async-start(bf16[1,64,16,512]{3,1,0,2:T(8,128)(2,1)} %copy.16), calls=%async_computation | async-start | bytes 2097152 | tf_op jit(solution)/shard_map/all_to_all | solution.py:312
  21.4 11.4 %collective-permute-done.2 = f32[256]{0:T(256)S(1)} collective-permute-done((f32[256]{0:T(256)S(1)}, f32[256]{0:T(256)S(1)}, u32[]{:S(2)}, u32[]{:S(2)}) %collective-permute-start.2) | collective-permute-done | bytes 1056 | tf_op jit(solution)/shard_map/ppermute | solution.py:315
  32.8 4.2 %all-to-all-done = bf16[1,64,16,512]{3,1,0,2:T(8,128)(2,1)} async-done(((bf16[1,64,16,512]{3,1,0,2:T(8,128)(2,1)}), bf16[1,64,16,512]{3,1,0,2:T(8,128)(2,1)}, u32[]{:S(2)}, u32[]{:S(2)}) %all-to-all-start) | async-done | bytes 1048608 | tf_op jit(solution)/shard_map/all_to_all | solution.py:312
  42.8 3.6 %collective-permute-done.11 = bf16[128,1024]{1,0:T(8,128)(2,1)S(1)} collective-permute-done((bf16[128,1024]{1,0:T(8,128)(2,1)S(1)}, bf16[128,1024]{1,0:T(8,128)(2,1)S(1)}, u32[]{:S(2)}, u32[]{:S(2)}) %collective-permute-start.11) | collective-permute-done | bytes 262176 | tf_op jit(solution)/shard_map/ppermute | solution.py:39
  51.9 2.7 collective-permute-done.9
  56.2 3.7 %collective-permute-start.8 = (bf16[256,1024]{1,0:T(8,128)(2,1)S(1)}, bf16[256,1024]{1,0:T(8,128)(2,1)}, u32[]{:S(2)}, u32[]{:S(2)}) collective-permute-start(bf16[256,1024]{1,0:T(8,128)(2,1)S(1)} %constant_dynamic-update-slice_fusion.refs_1_), channel_id=1, source_target_pairs={{0,24},{8,0},{16,8},{24,16},{1,25},{9,1},{17,9},{25,17},{2,26},{10... | collective-permute-start | bytes 1572872 | tf_op jit(solution)/shard_map/ppermute | solution.py:39
  59.9 7.5 %collective-permute-done.4 = bf16[128,1024]{1,0:T(8,128)(2,1)S(1)} collective-permute-done((bf16[128,1024]{1,0:T(8,128)(2,1)S(1)}, bf16[128,1024]{1,0:T(8,128)(2,1)S(1)}, u32[]{:S(2)}, u32[]{:S(2)}) %collective-permute-start.4) | collective-permute-done | bytes 262176 | tf_op jit(solution)/shard_map/ppermute | solution.py:39
  68.0 3.3 %collective-permute-done.13.refs_13_ = bf16[256,1024]{1,0:T(8,128)(2,1)} collective-permute-done((bf16[256,1024]{1,0:T(8,128)(2,1)S(1)}, bf16[256,1024]{1,0:T(8,128)(2,1)}, u32[]{:S(2)}, u32[]{:S(2)}) %collective-permute-start.13) | collective-permute-done | bytes 524320 | tf_op jit(solution)/shard_map/ppermute | solution.py:39
  72.8 4.9 %collective-permute-done.10.refs_10_ = bf16[256,1024]{1,0:T(8,128)(2,1)} collective-permute-done((bf16[256,1024]{1,0:T(8,128)(2,1)S(1)}, bf16[256,1024]{1,0:T(8,128)(2,1)}, u32[]{:S(2)}, u32[]{:S(2)}) %collective-permute-start.10) | collective-permute-done | bytes 524320 | tf_op jit(solution)/shard_map/ppermute | solution.py:39
  77.7 3.4 %collective-permute-done.5.refs_2_ = bf16[256,1024]{1,0:T(8,128)(2,1)} collective-permute-done((bf16[256,1024]{1,0:T(8,128)(2,1)S(1)}, bf16[256,1024]{1,0:T(8,128)(2,1)}, u32[]{:S(2)}, u32[]{:S(2)}) %collective-permute-start.5) | collective-permute-done | bytes 524320 | tf_op jit(solution)/shard_map/ppermute | solution.py:39
  83.1 11.0 %collective-permute-done = bf16[256,2048]{1,0:T(8,128)(2,1)} collective-permute-done((bf16[256,2048]{1,0:T(8,128)(2,1)S(1)}, bf16[256,2048]{1,0:T(8,128)(2,1)}, u32[]{:S(2)}, u32[]{:S(2)}) %collective-permute-start) | collective-permute-done | bytes 1048608 | tf_op jit(solution)/shard_map/ppermute | solution.py:334
  94.1 2.6 collective-permute-start.17
  97.9 3.9 %maximum_select_fusion.w_ref = bf16[512,2048]{1,0:T(8,128)(2,1)} fusion(bf16[256,2048]{1,0:T(8,128)(2,1)} %collective-permute-done, bf16[256,2048]{1,0:T(8,128)(2,1)S(1)} %get-tuple-element.104, pred[]{:T(512)S(6)} %eq.88), kind=kLoop, calls=%fused_computation | loop fusion | flops 9437184 | bytes 4194305 | tf_op jit(solution)/shard_map/jit(_where)/select_n | solution.py:335
  103.2 4.0 %collective-permute-done.19.refs_15_ = bf16[256,1024]{1,0:T(8,128)(2,1)} collective-permute-done((bf16[256,1024]{1,0:T(8,128)(2,1)}, bf16[256,1024]{1,0:T(8,128)(2,1)}, u32[]{:S(2)}, u32[]{:S(2)}) %collective-permute-start.19) | collective-permute-done | bytes 524320 | tf_op jit(solution)/shard_map/ppermute | solution.py:39
  109.3 10.6 %collective-permute-done.17.refs_7_ = bf16[256,1024]{1,0:T(8,128)(2,1)} collective-permute-done((bf16[256,1024]{1,0:T(8,128)(2,1)}, bf16[256,1024]{1,0:T(8,128)(2,1)}, u32[]{:S(2)}, u32[]{:S(2)}) %collective-permute-start.17) | collective-permute-done | bytes 524320 | tf_op jit(solution)/shard_map/ppermute | solution.py:39
  119.9 3.0 %collective-permute-start.21 = (bf16[256,1024]{1,0:T(8,128)(2,1)S(1)}, bf16[256,1024]{1,0:T(8,128)(2,1)}, u32[]{:S(2)}, u32[]{:S(2)}) collective-permute-start(bf16[256,1024]{1,0:T(8,128)(2,1)S(1)} %pad_maximum_fusion.refs_0_), channel_id=1, source_target_pairs={{0,24},{8,0},{16,8},{24,16},{1,25},{9,1},{17,9},{25,17},{2,26},{10... | collective-permute-start | bytes 1572872 | tf_op jit(solution)/shard_map/ppermute | solution.py:39
  122.9 11.6 %shard_map.92.xt_ref = bf16[512,4096]{1,0:T(8,128)(2,1)} custom-call(s32[3]{0:T(128)} %pad_add_fusion.where_ref.xl_ref, bf16[16,64,512]{2,1,0:T(8,128)(2,1)} %bitcast.37.a_ref, bf16[16,64,512]{2,1,0:T(8,128)(2,1)} %collective-permute-done.3.b_ref, bf16[16,64,512]{2,1,0:T(8,128)(2,1)} %collective-permute-done.14.c_ref, ...), custom_call_target="tpu_custom_call" | custom-call | flops 20000000000 | bytes 1 | tf_op jit(solution)/shard_map/pallas_call | solution.py:73
  134.5 6.0 %collective-permute-done.16.refs_6_ = bf16[256,1024]{1,0:T(8,128)(2,1)} collective-permute-done((bf16[256,1024]{1,0:T(8,128)(2,1)}, bf16[256,1024]{1,0:T(8,128)(2,1)}, u32[]{:S(2)}, u32[]{:S(2)}) %collective-permute-start.16) | collective-permute-done | bytes 524320 | tf_op jit(solution)/shard_map/ppermute | solution.py:39
  141.6 11.9 %shard_map.93 = (bf16[32,128,1024]{2,1,0:T(8,128)(2,1)}, f32[256,1024]{1,0:T(8,128)}, f32[2,256,512]{2,1,0:T(8,128)}, f32[512,128]{1,0:T(8,128)}, f32[8,1024]{1,0:T(8,128)}) custom-call(s32[3]{0:T(128)} %pad_add_fusion.where_ref.xl_ref, s32[32]{0:T(128)} %stack.172.index_ref, bf16[512,4096]{1,0:T(8,128)(2,1)} %shard_map.92.xt_ref, ...), custom_call_target="tpu_custom_call" | custom-call | flops 1 | bytes 1 | tf_op jit(solution)/shard_map/pallas_call | solution.py:147
  157.2 6.6 %shard_map.94 = f32[1024,512]{1,0:T(8,128)} custom-call(s32[3]{0:T(128)} %pad_add_fusion.where_ref.xl_ref, bf16[4096,1024]{1,0:T(8,128)(2,1)} %bitcast.89, bf16[4096,1024]{1,0:T(8,128)(2,1)} %bitcast.84, bf16[512,2048]{1,0:T(8,128)(2,1)} %maximum_select_fusion.w_ref), custom_call_target="tpu_custom_call" | custom-call | flops 1 | bytes 1 | tf_op jit(solution)/shard_map/pallas_call | solution.py:230
  164.2 9.6 %shard_map.95 = (f32[256,1024]{1,0:T(8,128)}, f32[2,256,512]{2,1,0:T(8,128)}, f32[512,128]{1,0:T(8,128)}, f32[8,1024]{1,0:T(8,128)}) custom-call(s32[3]{0:T(128)} %pad_add_fusion.where_ref.xl_ref, bf16[512,4096]{1,0:T(8,128)(2,1)} %shard_map.92.xt_ref, bf16[4096,1024]{1,0:T(8,128)(2,1)} %bitcast.85), custom_call_target="tpu_custom_call" | custom-call | flops 1 | bytes 1 | tf_op jit(solution)/shard_map/pallas_call | solution.py:177
  175.5 3.5 %all-to-all-start.1 = ((f32[16,1,2048]{2,1,0:T(1,128)}), f32[16,1,2048]{2,1,0:T(1,128)S(1)}, u32[]{:S(2)}, u32[]{:S(2)}) async-start(f32[16,1,2048]{2,1,0:T(1,128)} %broadcast_in_dim.22), calls=%async_computation.1 | async-start | bytes 262144 | tf_op jit(solution)/shard_map/all_to_all | solution.py:31
  180.7 6.6 %shard_map.96 = f32[1024,512]{1,0:T(8,128)} custom-call(s32[3]{0:T(128)} %pad_add_fusion.where_ref.xl_ref, bf16[4096,1024]{1,0:T(8,128)(2,1)} %bitcast.90, bf16[4096,1024]{1,0:T(8,128)(2,1)} %bitcast.86, bf16[512,2048]{1,0:T(8,128)(2,1)} %maximum_select_fusion.w_ref), custom_call_target="tpu_custom_call" | custom-call | flops 1 | bytes 1 | tf_op jit(solution)/shard_map/pallas_call | solution.py:230
  190.1 3.9 %all-to-all-start.2 = ((f32[8,4,256]{2,1,0:T(4,128)}), f32[8,4,256]{2,1,0:T(4,128)S(1)}, u32[]{:S(2)}, u32[]{:S(2)}) async-start(f32[8,4,256]{2,1,0:T(4,128)} %broadcast_in_dim.23), calls=%async_computation.2 | async-start | bytes 65536 | tf_op jit(solution)/shard_map/all_to_all | solution.py:31
  196.1 11.0 %all-to-all-done.2 = f32[8,4,256]{2,1,0:T(4,128)S(1)} async-done(((f32[8,4,256]{2,1,0:T(4,128)}), f32[8,4,256]{2,1,0:T(4,128)S(1)}, u32[]{:S(2)}, u32[]{:S(2)}) %all-to-all-start.2) | async-done | bytes 32800 | tf_op jit(solution)/shard_map/all_to_all | solution.py:31
  207.1 7.7 %shard_map.98 = (f32[512,512]{1,0:T(8,128)}, f32[512,256]{1,0:T(8,128)}, f32[512,256]{1,0:T(8,128)}) custom-call(s32[3]{0:T(128)} %pad_add_fusion.where_ref.xl_ref, bf16[4096,1024]{1,0:T(8,128)(2,1)} %bitcast.91, bf16[4096,1024]{1,0:T(8,128)(2,1)} %bitcast.87, bf16[512,2048]{1,0:T(8,128)(2,1)} %maximum_select_fusion.w_ref, ...), custom_call_target="tpu_custom_call" | custom-call | flops 1 | bytes 1 | tf_op jit(solution)/shard_map/pallas_call | solution.py:230
  218.2 6.8 %all-to-all-start.3 = ((f32[16,1,128]{2,1,0:T(1,128)}), f32[16,1,128]{2,1,0:T(1,128)S(1)}, u32[]{:S(2)}, u32[]{:S(2)}) async-start(f32[16,1,128]{2,1,0:T(1,128)} %broadcast_in_dim.47), calls=%async_computation.3 | async-start | bytes 16384 | tf_op jit(solution)/shard_map/all_to_all | solution.py:31
  228.6 3.9 %all-to-all-done.3 = f32[16,1,128]{2,1,0:T(1,128)S(1)} async-done(((f32[16,1,128]{2,1,0:T(1,128)}), f32[16,1,128]{2,1,0:T(1,128)S(1)}, u32[]{:S(2)}, u32[]{:S(2)}) %all-to-all-start.3) | async-done | bytes 8224 | tf_op jit(solution)/shard_map/all_to_all | solution.py:31
  232.5 7.9 %shard_map.97 = (f32[512,512]{1,0:T(8,128)}, f32[512,256]{1,0:T(8,128)}, f32[512,256]{1,0:T(8,128)}) custom-call(s32[3]{0:T(128)} %pad_add_fusion.where_ref.xl_ref, bf16[4096,1024]{1,0:T(8,128)(2,1)} %bitcast.92, bf16[4096,1024]{1,0:T(8,128)(2,1)} %bitcast.88, bf16[512,2048]{1,0:T(8,128)(2,1)} %maximum_select_fusion.w_ref, ...), custom_call_target="tpu_custom_call" | custom-call | flops 1 | bytes 1 | tf_op jit(solution)/shard_map/pallas_call | solution.py:230
  242.3 2.7 collective-permute-start.30
  250.2 7.7 %shard_map.99 = f32[256,4096]{1,0:T(8,128)} custom-call(s32[3]{0:T(128)} %pad_add_fusion.where_ref.xl_ref, f32[1]{0:T(128)} %bitcast.58.scale_ref, f32[256,1]{1,0:T(8,128)} %copy.19.row_ref, f32[1,4096]{1,0:T(1,128)} %bitcast.96, f32[256,1024]{1,0:T(8,128)} %get-tuple-element.76.refs_0_, f32[256,1024]{1,0:T(8,128)} %get-tuple-element.81.refs_1_, ...), custom_call_target="tpu_custom_call" | custom-call | flops 1 | bytes 1 | tf_op jit(solution)/shard_map/pallas_call | solution.py:274
  259.9 4.0 %collective-permute-done.27 = f32[512,256]{1,0:T(8,128)} collective-permute-done((f32[512,256]{1,0:T(8,128)}, f32[512,256]{1,0:T(8,128)}, u32[]{:S(2)}, u32[]{:S(2)}) %collective-permute-start.27) | collective-permute-done | bytes 524320 | tf_op jit(solution)/shard_map/ppermute | solution.py:389
  (153 shorter events, 56.7 us)
Async XLA Ops:
  11.0 25.9 %all-to-all-start = ((bf16[1,64,16,512]{3,1,0,2:T(8,128)(2,1)}), bf16[1,64,16,512]{3,1,0,2:T(8,128)(2,1)}, u32[]{:S(2)}, u32[]{:S(2)}) async-start(bf16[1,64,16,512]{3,1,0,2:T(8,128)(2,1)} %copy.16), calls=%async_computation | async-start | bytes 2097152 | tf_op jit(solution)/shard_map/all_to_all | solution.py:312
  19.2 137.9 %all-gather.2.cloned.1.call-start = ((), (), s32[]{:S(2)}) async-start(), calls=%async_computation.4 | async-start | bytes 8912896 | tf_op jit(solution)/shard_map/all_gather | solution.py:320
  40.7 14.0 %collective-permute-start.6 = (bf16[128,1024]{1,0:T(8,128)(2,1)S(1)}, bf16[128,1024]{1,0:T(8,128)(2,1)S(1)}, u32[]{:S(2)}, u32[]{:S(2)}) collective-permute-start(bf16[128,1024]{1,0:T(8,128)(2,1)S(1)} %get-tuple-element.113), channel_id=1, source_target_pairs={{0,96},{32,0},{64,32},{96,64},{1,97},{33,1},{65,33},{97,65},{2,98}... | collective-permute-start | bytes 786440 | tf_op jit(solution)/shard_map/ppermute | solution.py:39
  41.3 14.8 %collective-permute-start.7 = (bf16[128,1024]{1,0:T(8,128)(2,1)S(1)}, bf16[128,1024]{1,0:T(8,128)(2,1)S(1)}, u32[]{:S(2)}, u32[]{:S(2)}) collective-permute-start(bf16[128,1024]{1,0:T(8,128)(2,1)S(1)} %get-tuple-element.113), channel_id=1, source_target_pairs={{0,64},{32,96},{64,0},{96,32},{1,65},{33,97},{65,1},{97,33},{2,66}... | collective-permute-start | bytes 786440 | tf_op jit(solution)/shard_map/ppermute | solution.py:39
  46.4 34.7 %collective-permute-start.3 = (bf16[16,64,512]{2,1,0:T(8,128)(2,1)}, bf16[16,64,512]{2,1,0:T(8,128)(2,1)}, u32[]{:S(2)}, u32[]{:S(2)}) collective-permute-start(bf16[16,64,512]{2,1,0:T(8,128)(2,1)} %bitcast.37.a_ref), channel_id=1, source_target_pairs={{0,4},{4,0},{1,5},{5,1},{2,6},{6,2},{3,7},{7,3},{8,12},{12,8},{9,1... | collective-permute-start | bytes 3145736 | tf_op jit(solution)/shard_map/ppermute | solution.py:326
  49.0 22.3 %collective-permute-start.13 = (bf16[256,1024]{1,0:T(8,128)(2,1)S(1)}, bf16[256,1024]{1,0:T(8,128)(2,1)}, u32[]{:S(2)}, u32[]{:S(2)}) collective-permute-start(bf16[256,1024]{1,0:T(8,128)(2,1)S(1)} %constant_dynamic-update-slice_fusion.2.refs_9_), channel_id=1, source_target_pairs={{0,96},{32,0},{64,32},{96,64},{1,97},{33,1},{65,33},{97,65},{2,98}... | collective-permute-start | bytes 1572872 | tf_op jit(solution)/shard_map/ppermute | solution.py:39
  54.7 23.0 %collective-permute-start.10 = (bf16[256,1024]{1,0:T(8,128)(2,1)S(1)}, bf16[256,1024]{1,0:T(8,128)(2,1)}, u32[]{:S(2)}, u32[]{:S(2)}) collective-permute-start(bf16[256,1024]{1,0:T(8,128)(2,1)S(1)} %pad_maximum_fusion.1.refs_8_), channel_id=1, source_target_pairs={{0,32},{32,64},{64,96},{96,0},{1,33},{33,65},{65,97},{97,1},{2,34}... | collective-permute-start | bytes 1572872 | tf_op jit(solution)/shard_map/ppermute | solution.py:39
  56.2 21.5 %collective-permute-start.8 = (bf16[256,1024]{1,0:T(8,128)(2,1)S(1)}, bf16[256,1024]{1,0:T(8,128)(2,1)}, u32[]{:S(2)}, u32[]{:S(2)}) collective-permute-start(bf16[256,1024]{1,0:T(8,128)(2,1)S(1)} %constant_dynamic-update-slice_fusion.refs_1_), channel_id=1, source_target_pairs={{0,24},{8,0},{16,8},{24,16},{1,25},{9,1},{17,9},{25,17},{2,26},{10... | collective-permute-start | bytes 1572872 | tf_op jit(solution)/shard_map/ppermute | solution.py:39
  71.3 22.9 %collective-permute-start = (bf16[256,2048]{1,0:T(8,128)(2,1)S(1)}, bf16[256,2048]{1,0:T(8,128)(2,1)}, u32[]{:S(2)}, u32[]{:S(2)}) collective-permute-start(bf16[256,2048]{1,0:T(8,128)(2,1)S(1)} %get-tuple-element.105), channel_id=1, source_target_pairs={{0,4},{4,0},{1,5},{5,1},{2,6},{6,2},{3,7},{7,3},{8,12},{12,8},{9,1... | collective-permute-start | bytes 3145736 | tf_op jit(solution)/shard_map/ppermute | solution.py:334
  77.7 24.2 %collective-permute-start.14 = (bf16[16,64,512]{2,1,0:T(8,128)(2,1)}, bf16[16,64,512]{2,1,0:T(8,128)(2,1)}, u32[]{:S(2)}, u32[]{:S(2)}) collective-permute-start(bf16[16,64,512]{2,1,0:T(8,128)(2,1)} %bitcast.37.a_ref), channel_id=1, source_target_pairs={{0,1},{1,0},{2,3},{3,2},{4,5},{5,4},{6,7},{7,6},{8,9},{9,8},{10,11... | collective-permute-start | bytes 3145736 | tf_op jit(solution)/shard_map/ppermute | solution.py:327
  81.1 41.8 %collective-permute-start.15 = (bf16[16,64,512]{2,1,0:T(8,128)(2,1)}, bf16[16,64,512]{2,1,0:T(8,128)(2,1)}, u32[]{:S(2)}, u32[]{:S(2)}) collective-permute-start(bf16[16,64,512]{2,1,0:T(8,128)(2,1)} %collective-permute-done.3.b_ref), channel_id=1, source_target_pairs={{0,1},{1,0},{2,3},{3,2},{4,5},{5,4},{6,7},{7,6},{8,9},{9,8},{10,11... | collective-permute-start | bytes 3145736 | tf_op jit(solution)/shard_map/ppermute | solution.py:331
  81.1 26.2 %collective-permute-start.19 = (bf16[256,1024]{1,0:T(8,128)(2,1)}, bf16[256,1024]{1,0:T(8,128)(2,1)}, u32[]{:S(2)}, u32[]{:S(2)}) collective-permute-start(bf16[256,1024]{1,0:T(8,128)(2,1)} %collective-permute-done.13.refs_13_), channel_id=1, source_target_pairs={{0,96},{32,0},{64,32},{96,64},{1,97},{33,1},{65,33},{97,65},{2,98}... | collective-permute-start | bytes 1572872 | tf_op jit(solution)/shard_map/ppermute | solution.py:39
  81.8 27.5 %collective-permute-start.18 = (bf16[256,1024]{1,0:T(8,128)(2,1)}, bf16[256,1024]{1,0:T(8,128)(2,1)}, u32[]{:S(2)}, u32[]{:S(2)}) collective-permute-start(bf16[256,1024]{1,0:T(8,128)(2,1)} %collective-permute-done.10.refs_10_), channel_id=1, source_target_pairs={{0,32},{32,64},{64,96},{96,0},{1,33},{33,65},{65,97},{97,1},{2,34}... | collective-permute-start | bytes 1572872 | tf_op jit(solution)/shard_map/ppermute | solution.py:39
  94.1 25.7 %collective-permute-start.17 = (bf16[256,1024]{1,0:T(8,128)(2,1)}, bf16[256,1024]{1,0:T(8,128)(2,1)}, u32[]{:S(2)}, u32[]{:S(2)}) collective-permute-start(bf16[256,1024]{1,0:T(8,128)(2,1)} %collective-permute-done.8.refs_5_), channel_id=1, source_target_pairs={{0,24},{8,0},{16,8},{24,16},{1,25},{9,1},{17,9},{25,17},{2,26},{10... | collective-permute-start | bytes 1572872 | tf_op jit(solution)/shard_map/ppermute | solution.py:39
  101.8 38.7 %collective-permute-start.22 = (bf16[256,1024]{1,0:T(8,128)(2,1)S(1)}, bf16[256,1024]{1,0:T(8,128)(2,1)S(1)}, u32[]{:S(2)}, u32[]{:S(2)}) collective-permute-start(bf16[256,1024]{1,0:T(8,128)(2,1)S(1)} %constant_dynamic-update-slice_fusion.2.refs_9_), channel_id=1, source_target_pairs={{0,32},{32,64},{64,96},{96,0},{1,33},{33,65},{65,97},{97,1},{2,34}... | collective-permute-start | bytes 1572872 | tf_op jit(solution)/shard_map/ppermute | solution.py:39
  107.3 33.3 %collective-permute-start.23 = (bf16[256,1024]{1,0:T(8,128)(2,1)S(1)}, bf16[256,1024]{1,0:T(8,128)(2,1)S(1)}, u32[]{:S(2)}, u32[]{:S(2)}) collective-permute-start(bf16[256,1024]{1,0:T(8,128)(2,1)S(1)} %pad_maximum_fusion.1.refs_8_), channel_id=1, source_target_pairs={{0,96},{32,0},{64,32},{96,64},{1,97},{33,1},{65,33},{97,65},{2,98}... | collective-permute-start | bytes 1572872 | tf_op jit(solution)/shard_map/ppermute | solution.py:39
  109.3 31.3 %collective-permute-start.20 = (bf16[256,1024]{1,0:T(8,128)(2,1)S(1)}, bf16[256,1024]{1,0:T(8,128)(2,1)}, u32[]{:S(2)}, u32[]{:S(2)}) collective-permute-start(bf16[256,1024]{1,0:T(8,128)(2,1)S(1)} %constant_dynamic-update-slice_fusion.refs_1_), channel_id=1, source_target_pairs={{0,8},{8,16},{16,24},{24,0},{1,9},{9,17},{17,25},{25,1},{2,10},{10... | collective-permute-start | bytes 1572872 | tf_op jit(solution)/shard_map/ppermute | solution.py:39
  119.9 20.7 %collective-permute-start.21 = (bf16[256,1024]{1,0:T(8,128)(2,1)S(1)}, bf16[256,1024]{1,0:T(8,128)(2,1)}, u32[]{:S(2)}, u32[]{:S(2)}) collective-permute-start(bf16[256,1024]{1,0:T(8,128)(2,1)S(1)} %pad_maximum_fusion.refs_0_), channel_id=1, source_target_pairs={{0,24},{8,0},{16,8},{24,16},{1,25},{9,1},{17,9},{25,17},{2,26},{10... | collective-permute-start | bytes 1572872 | tf_op jit(solution)/shard_map/ppermute | solution.py:39
  122.9 17.6 %collective-permute-start.16 = (bf16[256,1024]{1,0:T(8,128)(2,1)}, bf16[256,1024]{1,0:T(8,128)(2,1)}, u32[]{:S(2)}, u32[]{:S(2)}) collective-permute-start(bf16[256,1024]{1,0:T(8,128)(2,1)} %collective-permute-done.5.refs_2_), channel_id=1, source_target_pairs={{0,8},{8,16},{16,24},{24,0},{1,9},{9,17},{17,25},{25,1},{2,10},{10... | collective-permute-start | bytes 1572872 | tf_op jit(solution)/shard_map/ppermute | solution.py:39
  155.5 19.1 %collective-permute-start.31 = (f32[256,512]{1,0:T(8,128)S(1)}, f32[256,512]{1,0:T(8,128)S(1)}, u32[]{:S(2)}, u32[]{:S(2)}) collective-permute-start(f32[256,512]{1,0:T(8,128)S(1)} %get-tuple-element.109), channel_id=1, source_target_pairs={{0,4},{4,0},{1,5},{5,1},{2,6},{6,2},{3,7},{7,3},{8,12},{12,8},{9,1... | collective-permute-start | bytes 1572872 | tf_op jit(solution)/shard_map/ppermute | solution.py:342
  163.7 43.4 %collective-permute-start.25 = (f32[1024,512]{1,0:T(8,128)}, f32[1024,512]{1,0:T(8,128)}, u32[]{:S(2)}, u32[]{:S(2)}) collective-permute-start(f32[1024,512]{1,0:T(8,128)} %shard_map.94), channel_id=1, source_target_pairs={{0,1},{1,0},{2,3},{3,2},{4,5},{5,4},{6,7},{7,6},{8,9},{9,8},{10,11... | collective-permute-start | bytes 6291464 | tf_op jit(solution)/shard_map/ppermute | solution.py:346
  163.7 25.7 %collective-permute-start.32 = (f32[256,512]{1,0:T(8,128)}, f32[256,512]{1,0:T(8,128)}, u32[]{:S(2)}, u32[]{:S(2)}) collective-permute-start(f32[256,512]{1,0:T(8,128)} %get-tuple-element.108), channel_id=1, source_target_pairs={{0,4},{4,0},{1,5},{5,1},{2,6},{6,2},{3,7},{7,3},{8,12},{12,8},{9,1... | collective-permute-start | bytes 1572872 | tf_op jit(solution)/shard_map/ppermute | solution.py:343
  179.0 28.1 %collective-permute-start.33 = (f32[2,256,512]{2,1,0:T(8,128)}, f32[2,256,512]{2,1,0:T(8,128)}, u32[]{:S(2)}, u32[]{:S(2)}) collective-permute-start(f32[2,256,512]{2,1,0:T(8,128)} %get-tuple-element.82), channel_id=1, source_target_pairs={{0,4},{4,0},{1,5},{5,1},{2,6},{6,2},{3,7},{7,3},{8,12},{12,8},{9,1... | collective-permute-start | bytes 3145736 | tf_op jit(solution)/shard_map/ppermute | solution.py:349
  187.3 45.2 %collective-permute-start.24 = (f32[1024,512]{1,0:T(8,128)}, f32[1024,512]{1,0:T(8,128)}, u32[]{:S(2)}, u32[]{:S(2)}) collective-permute-start(f32[1024,512]{1,0:T(8,128)} %shard_map.96), channel_id=1, source_target_pairs={{0,1},{1,0},{2,3},{3,2},{4,5},{5,4},{6,7},{7,6},{8,9},{9,8},{10,11... | collective-permute-start | bytes 6291464 | tf_op jit(solution)/shard_map/ppermute | solution.py:356
  190.1 17.0 %all-to-all-start.2 = ((f32[8,4,256]{2,1,0:T(4,128)}), f32[8,4,256]{2,1,0:T(4,128)S(1)}, u32[]{:S(2)}, u32[]{:S(2)}) async-start(f32[8,4,256]{2,1,0:T(4,128)} %broadcast_in_dim.23), calls=%async_computation.2 | async-start | bytes 65536 | tf_op jit(solution)/shard_map/all_to_all | solution.py:31
  194.0 38.5 %collective-permute-start.34 = (f32[2048]{0:T(1024)S(1)}, f32[2048]{0:T(1024)S(1)}, u32[]{:S(2)}, u32[]{:S(2)}) collective-permute-start(f32[2048]{0:T(1024)S(1)} %get-tuple-element.100), channel_id=1, source_target_pairs={{0,4},{4,0},{1,5},{5,1},{2,6},{6,2},{3,7},{7,3},{8,12},{12,8},{9,1... | collective-permute-start | bytes 24584 | tf_op jit(solution)/shard_map/ppermute | solution.py:397
  214.8 30.2 %collective-permute-start.26 = (f32[512,512]{1,0:T(8,128)}, f32[512,512]{1,0:T(8,128)S(1)}, u32[]{:S(2)}, u32[]{:S(2)}) collective-permute-start(f32[512,512]{1,0:T(8,128)} %get-tuple-element.71), channel_id=1, source_target_pairs={{0,6},{6,0},{2,4},{4,2},{1,7},{7,1},{3,5},{5,3},{8,14},{14,8},{10,... | collective-permute-start | bytes 3145736 | tf_op jit(solution)/shard_map/ppermute | solution.py:384
  216.1 26.1 %collective-permute-start.29 = (f32[512,256]{1,0:T(8,128)}, f32[512,256]{1,0:T(8,128)S(1)}, u32[]{:S(2)}, u32[]{:S(2)}) collective-permute-start(f32[512,256]{1,0:T(8,128)} %get-tuple-element.75), channel_id=1, source_target_pairs={{0,4},{4,0},{1,5},{5,1},{2,6},{6,2},{3,7},{7,3},{8,12},{12,8},{9,1... | collective-permute-start | bytes 1572872 | tf_op jit(solution)/shard_map/ppermute | solution.py:385
  218.2 14.3 %all-to-all-start.3 = ((f32[16,1,128]{2,1,0:T(1,128)}), f32[16,1,128]{2,1,0:T(1,128)S(1)}, u32[]{:S(2)}, u32[]{:S(2)}) async-start(f32[16,1,128]{2,1,0:T(1,128)} %broadcast_in_dim.47), calls=%async_computation.3 | async-start | bytes 16384 | tf_op jit(solution)/shard_map/all_to_all | solution.py:31
  240.4 18.1 %collective-permute-start.28 = (f32[512,256]{1,0:T(8,128)}, f32[512,256]{1,0:T(8,128)}, u32[]{:S(2)}, u32[]{:S(2)}) collective-permute-start(f32[512,256]{1,0:T(8,128)} %get-tuple-element.73), channel_id=1, source_target_pairs={{0,4},{4,0},{1,5},{5,1},{2,6},{6,2},{3,7},{7,3},{8,12},{12,8},{9,1... | collective-permute-start | bytes 1572872 | tf_op jit(solution)/shard_map/ppermute | solution.py:387
  242.3 16.1 %collective-permute-start.30 = (f32[512,256]{1,0:T(8,128)S(1)}, f32[512,256]{1,0:T(8,128)}, u32[]{:S(2)}, u32[]{:S(2)}) collective-permute-start(f32[512,256]{1,0:T(8,128)S(1)} %add.433), channel_id=1, source_target_pairs={{0,6},{6,0},{2,4},{4,2},{1,7},{7,1},{3,5},{5,3},{8,14},{14,8},{10,... | collective-permute-start | bytes 1572872 | tf_op jit(solution)/shard_map/ppermute | solution.py:388
  246.9 17.0 %collective-permute-start.27 = (f32[512,256]{1,0:T(8,128)}, f32[512,256]{1,0:T(8,128)}, u32[]{:S(2)}, u32[]{:S(2)}) collective-permute-start(f32[512,256]{1,0:T(8,128)} %slice_add_fusion), channel_id=1, source_target_pairs={{0,4},{4,0},{1,5},{5,1},{2,6},{6,2},{3,7},{7,3},{8,12},{12,8},{9,1... | collective-permute-start | bytes 1572872 | tf_op jit(solution)/shard_map/ppermute | solution.py:389
  (30 other events, 404.1 us)
Sparse Core Ops, SparseCore 0:
  38.1 98.5 all-gather.1

commit v3 on v2

v3 whole, which is shorter than its diff:
```python
import jax
import jax.numpy as jnp
from jax import lax
from jax.experimental import pallas as pl
from jax.experimental.pallas import tpu as pltpu
from jax.sharding import Mesh, PartitionSpec as P

D = 8192
FF = 16384
TOKENS = 4096
F32 = jnp.float32
BF16 = jnp.bfloat16

decay_rate = 0.84
tiny_eps = 1e-30

AXES = ("y", "z", "xl", "xh", "c")
SIZES = (4, 4, 2, 2, 2)
SWAP = [(0, 1), (1, 0)]
DIAG = [(0, 3), (3, 0), (1, 2), (2, 1)]
WIDE = 1024
MIB = 1 << 20
TILE = 512
SHORT = pl.CostEstimate(flops=1, bytes_accessed=1, transcendentals=0)
LONG = pl.CostEstimate(flops=2 * 10**10, bytes_accessed=1, transcendentals=0)


def spread(value, axes, count):
    copies = jnp.broadcast_to(value[None], (count,) + value.shape)
    return lax.all_to_all(copies, axes, split_axis=0, concat_axis=0, tiled=True)


def mine(a, n, axis, index):
    return lax.dynamic_slice_in_dim(a, index * n, n, axis)


def shift(a, axis, k):
    return lax.ppermute(a, axis, [(i, (i + k) % 4) for i in range(4)])


def near_three(start, axis):
    return [shift(start, axis, 1), shift(start, axis, 3), shift(start, axis, 2)]


def first_pieces(start, three, then):
    a, b, c = three
    pair = [jnp.concatenate([start, a]), jnp.concatenate([b, c])]
    near = [shift(pair[0], then, 1), shift(pair[1], then, 3)]
    return pair, near, [shift(near[0], then, 1), shift(near[1], then, 3)]


def other_pieces(pair, then):
    return [shift(pair[1], then, 1), shift(pair[0], then, 3)]


PLACES = [
    (a, d)
    for halves, d in (("p", 0), ("q", 0), ("p", 1), ("q", 3), ("p", 2), ("q", 2), ("q", 1), ("p", 3))
    for a in {"p": (0, 1), "q": (3, 2)}[halves]
]


def transposed_tokens(where, mine_first, others, swapped, other_swapped):
    def kernel(where_ref, a_ref, *refs):
        b_refs, c_ref, d_ref, out_ref, hold = refs[:3], *refs[3:]
        xl, xh, c = where_ref[0], where_ref[1], where_ref[2]

        def put(value, xl, xh, c):
            hold[pl.ds(pl.multiple_of(xl * 128 + xh * 64 + c * 32, 32), 32), :] = value

        places = ((xl, xh), (1 - xl, xh), (xl, 1 - xh), (1 - xl, 1 - xh))
        put(a_ref[0], *places[0], c)
        put(c_ref[0], *places[0], 1 - c)
        for k in range(3):
            put(b_refs[k][0], *places[k + 1], c)
            put(d_ref[k, 0], *places[k + 1], 1 - c)
        out_ref[...] = hold[...].T

    block = pl.BlockSpec((1, 32, 512), lambda i, where_ref: (i, 0, 0))
    return pl.pallas_call(
        kernel,
        grid_spec=pltpu.PrefetchScalarGridSpec(
            num_scalar_prefetch=1,
            grid=(16,),
            in_specs=[block] * 5 + [pl.BlockSpec((3, 1, 32, 512), lambda i, where_ref: (0, i, 0, 0))],
            out_specs=pl.BlockSpec((512, 256), lambda i, where_ref: (0, i)),
            scratch_shapes=[pltpu.VMEM((256, 512), BF16)],
        ),
        out_shape=jax.ShapeDtypeStruct((512, TOKENS), BF16),
        cost_estimate=LONG,
    )(where, mine_first, *others, swapped, other_swapped)


def squares_of(g, row_ref, col_ref, columns, first):
    squares = g * g
    rows, width = g.shape
    col_ref[:, columns] = jnp.sum(squares.reshape(rows // 8, 8, width), 0)
    sums = squares[:, :128]
    for k in range(128, width, 128):
        sums = sums + squares[:, k : k + 128]
    if first is True:
        row_ref[...] = sums
    else:
        row_ref[...] += sums


def grad_shapes(width):
    parts = tuple(jax.ShapeDtypeStruct((256, TILE), F32) for _ in range(width // TILE))
    return (
        jax.ShapeDtypeStruct((256, width), F32),
        jax.ShapeDtypeStruct((512, 128), F32),
        jax.ShapeDtypeStruct((8, width), F32),
    ) + parts


def own_other(a, first, axis):
    low, high = (a[:256], a[256:]) if axis == 0 else (a[:, :256], a[:, 256:])
    return jnp.where(first, low, high), jnp.where(first, high, low)


def gradient_of_pieces(xt, pieces, index, xl):
    rows, width = pieces[0].shape
    each = rows // 128
    n = each * len(pieces)

    def kernel(xl_ref, index_ref, xt_ref, *refs):
        ins = refs[: len(pieces)]
        c_ref, own_ref, row_ref, col_ref, *others = refs[len(pieces) : -3]
        hold, in_sems, out_sem = refs[-3:]
        copies = []
        for k in range(n):
            copies.append(
                pltpu.make_async_copy(
                    ins[k // each].at[pl.ds(128 * (k % each), 128)], hold.at[index_ref[k]], in_sems.at[k]
                )
            )
            copies[-1].start()
        for copy in copies:
            copy.wait()
        write = pltpu.make_async_copy(hold, c_ref, out_sem)
        write.start()
        for k, other_ref in enumerate(others):
            columns = slice(k * TILE, (k + 1) * TILE)
            block = hold[:, :, columns].reshape(TOKENS, TILE)
            g = jnp.dot(xt_ref[...], block, preferred_element_type=F32) * float(TOKENS) ** (-0.5)
            own_ref[:, columns], other_ref[...] = own_other(g, xl_ref[0] == 0, 0)
            squares_of(g, row_ref, col_ref, columns, k == 0)
        write.wait()

    vmem = pl.BlockSpec(memory_space=pltpu.VMEM)
    anywhere = pl.BlockSpec(memory_space=pl.ANY)
    smem = pl.BlockSpec(memory_space=pltpu.SMEM)
    out = pl.pallas_call(
        kernel,
        out_shape=(jax.ShapeDtypeStruct((n, 128, width), BF16),) + grad_shapes(width),
        in_specs=[smem, smem, vmem] + [anywhere] * len(pieces),
        out_specs=(anywhere,) + (vmem,) * (3 + width // TILE),
        scratch_shapes=[
            pltpu.VMEM((n, 128, width), BF16),
            pltpu.SemaphoreType.DMA((n,)),
            pltpu.SemaphoreType.DMA,
        ],
        compiler_params=pltpu.CompilerParams(vmem_limit_bytes=56 * MIB),
        cost_estimate=LONG,
    )(xl, index, xt, *pieces)
    return out[0].reshape(TOKENS, width), *out[1:4], out[4:]


def gradient(xt, c_all, xl):
    width = c_all.shape[1]

    def kernel(xl_ref, xt_ref, c_ref, own_ref, row_ref, col_ref, *others):
        g = jnp.dot(xt_ref[...], c_ref[...], preferred_element_type=F32) * float(TOKENS) ** (-0.5)
        own, other = own_other(g, xl_ref[0] == 0, 0)
        own_ref[...] = own
        for k, other_ref in enumerate(others):

            @pl.when(pl.program_id(0) == k)
            def _():
                other_ref[...] = other

        @pl.when(pl.program_id(0) == 0)
        def _():
            row_ref[...] = jnp.zeros_like(row_ref)

        squares_of(g, row_ref, col_ref, slice(None), False)

    out = pl.pallas_call(
        kernel,
        grid=(width // TILE,),
        out_shape=grad_shapes(width),
        in_specs=[
            pl.BlockSpec(memory_space=pltpu.SMEM),
            pl.BlockSpec((512, TOKENS), lambda j: (0, 0)),
            pl.BlockSpec((TOKENS, TILE), lambda j: (0, j)),
        ],
        out_specs=(
            pl.BlockSpec((256, TILE), lambda j: (0, j)),
            pl.BlockSpec((512, 128), lambda j: (0, 0)),
            pl.BlockSpec((8, TILE), lambda j: (0, j)),
        )
        + (pl.BlockSpec((256, TILE), lambda j: (0, 0)),) * (width // TILE),
        compiler_params=pltpu.CompilerParams(vmem_limit_bytes=56 * MIB),
        cost_estimate=LONG,
    )(xl, xt, c_all)
    return *out[:3], out[3:]


def terms(where, far, c_1, c_2, w_all, received=None):
    w1, w2 = c_1.shape[1], c_2.shape[1]
    keep = received is not None

    def kernel(where_ref, c1_ref, c2_ref, w_ref, *refs):
        t = jnp.dot(c1_ref[...], w_ref[:w1], preferred_element_type=F32)
        t = t + jnp.dot(c2_ref[...], w_ref[w1:], preferred_element_type=F32)
        if not keep:
            refs[0][...] = t
            return
        got_ref, both_1, both_2, own, other = refs
        t = t + got_ref[...]

        @pl.when(pl.program_id(0) == 0)
        def _():
            for ref, rows in ((both_1, t[:256]), (both_2, t[256:])):
                ref[:, :256], ref[:, 256:] = own_other(rows, where_ref[0] == 0, 1)

        @pl.when(pl.program_id(0) == 1)
        def _():
            own[...], other[...] = own_other(t, where_ref[0] == 0, 1)

    def rows(i, where_ref):
        high = 1 - where_ref[1] if far else where_ref[1]
        core = where_ref[2] if keep else 1 - where_ref[2]
        return ((2 * high + core) * 2 + i, 0)

    step = pl.BlockSpec((512, 512), lambda i, where_ref: (i, 0))
    block = jax.ShapeDtypeStruct((512, 256), F32)
    whole = [pl.BlockSpec(shape, lambda i, where_ref: (0, 0)) for shape in ((256, 512), (256, 512), (512, 256), (512, 256))]
    return pl.pallas_call(
        kernel,
        grid_spec=pltpu.PrefetchScalarGridSpec(
            num_scalar_prefetch=1,
            grid=(2,),
            in_specs=[
                pl.BlockSpec((512, w1), rows),
                pl.BlockSpec((512, w2), rows),
                pl.BlockSpec((w1 + w2, 512), lambda i, where_ref: (0, 0)),
            ]
            + [step] * keep,
            out_specs=whole if keep else step,
        ),
        out_shape=[jax.ShapeDtypeStruct((256, 512), F32)] * 2 + [block, block]
        if keep
        else jax.ShapeDtypeStruct((1024, 512), F32),
        compiler_params=pltpu.CompilerParams(vmem_limit_bytes=56 * MIB),
        cost_estimate=LONG,
    )(where, c_1, c_2, w_all, *((received,) if keep else ()))


def clipped(where, scale, row_factor, own, received, own_factors, received_factors):
    half = sum(g.shape[1] for g in own)
    tile = half // 2
    blocks = own + received
    firsts = [sum(g.shape[1] for g in blocks[:k]) for k in range(len(blocks))]

    def kernel(where_ref, scale_ref, row_ref, col_ref, *refs):
        out_ref = refs[-1]
        rows = row_ref[...] * scale_ref[0]
        for step in range(4):

            @pl.when(pl.program_id(0) == step)
            def _():
                for ref, first in zip(refs, firsts):
                    low, high = max(first, step * tile), min(first + ref.shape[1], (step + 1) * tile)
                    if low < high:
                        to = slice(low - step * tile, high - step * tile)
                        out_ref[:, to] = ref[:, low - first : high - first] * rows * col_ref[:, to]

    def place(j, where_ref):
        own_half = where_ref[0] + (j // 2) * (1 - 2 * where_ref[0])
        return (0, own_half * 2 + j % 2)

    return pl.pallas_call(
        kernel,
        grid_spec=pltpu.PrefetchScalarGridSpec(
            num_scalar_prefetch=1,
            grid=(4,),
            in_specs=[
                pl.BlockSpec(memory_space=pltpu.SMEM),
                pl.BlockSpec((256, 1), lambda j, where_ref: (0, 0)),
                pl.BlockSpec((1, tile), lambda j, where_ref: (0, j)),
            ]
            + [pl.BlockSpec(g.shape, lambda j, where_ref: (0, 0)) for g in blocks],
            out_specs=pl.BlockSpec((256, tile), place),
        ),
        out_shape=jax.ShapeDtypeStruct((256, 2 * half), F32),
        compiler_params=pltpu.CompilerParams(vmem_limit_bytes=56 * MIB),
        cost_estimate=LONG,
    )(
        where,
        scale.reshape(1),
        row_factor[:, None],
        jnp.concatenate([own_factors, received_factors])[None, :],
        *blocks,
    )


def body(tokens, cotangent, weight, row_prev, col_prev):
    y, z = lax.axis_index("y"), lax.axis_index("z")
    xl, xh, c = lax.axis_index("xl"), lax.axis_index("xh"), lax.axis_index("c")
    half = cotangent.shape[1] // 2
    first_xl = xl == 0
    after = lax.optimization_barrier

    where = jnp.stack([xl, xh, c]).astype(jnp.int32)

    away = mine(cotangent, half, 1, 1 - xl)
    part, away = after((mine(tokens, 32, 0, 2 * xh + c), away))
    other = lax.ppermute(away, "xl", SWAP)
    part = part.reshape(32, 16, 512)
    xo = lax.all_to_all(part, ("y", "z"), split_axis=1, concat_axis=0, tiled=False)

    own = mine(cotangent, half, 1, xl)
    row_prev_other = lax.ppermute(row_prev, "xl", SWAP)
    own, other, xo, row_prev_other = after((own, other, xo, row_prev_other))
    own_1, own_2 = own[:, :WIDE], own[:, WIDE:]
    other_1, other_2 = other[:, :WIDE], other[:, WIDE:]
    shard = jnp.where(first_xl, jnp.stack([own_2, other_2]), jnp.stack([other_2, own_2]))
    c_2 = lax.all_gather(shard, ("y", "z"), axis=0, tiled=False).reshape(TOKENS, half - WIDE)
    pair, near, far = first_pieces(own_1, near_three(own_1, "y"), "z")
    pair_2, near_2, far_2 = first_pieces(other_1, near_three(other_1, "z"), "y")

    to = lax.ppermute(xo, "c", SWAP)
    xs = [lax.ppermute(xo, "xl", SWAP), lax.ppermute(xo, "xh", SWAP), lax.ppermute(xo, ("xl", "xh"), DIAG)]
    xs, near, near_2 = after((xs, near, near_2))
    xt = transposed_tokens(where, xo, xs, to, lax.ppermute(jnp.stack(xs), "c", SWAP))
    pair, pair_2, xt = after((pair, pair_2, xt))
    pieces = pair + near + far + other_pieces(pair, "z") + pair_2 + near_2 + far_2 + other_pieces(pair_2, "y")
    index = [((y - dy) % 4 * 4 + (z - dz) % 4) * 2 + xl for dy, dz in PLACES]
    index += [((y - dy) % 4 * 4 + (z - dz) % 4) * 2 + 1 - xl for dz, dy in PLACES]
    w_own = mine(weight, half, 1, xl)
    w_other = lax.ppermute(mine(weight, half, 1, 1 - xl), "xl", SWAP)
    w_other, xt = after((w_other, xt))
    w_all = jnp.where(first_xl, jnp.concatenate([w_own, w_other]), jnp.concatenate([w_other, w_own])).T

    g_2, rows_2, cols_2, send_2 = gradient(xt, c_2, where)
    received_2 = [lax.ppermute(g, "xl", SWAP) for g in send_2]
    pieces, w_all, xt, rows_2 = after((pieces, w_all, xt, rows_2))
    c_1, g_1, rows_1, cols_1, send_1 = gradient_of_pieces(xt, pieces, jnp.stack(index).astype(jnp.int32), where)
    received_1 = [lax.ppermute(g, "xl", SWAP) for g in send_1]
    cols = jnp.sum(jnp.concatenate([cols_1, cols_2], 1), 0)
    w_all, received_2[0], cols = after((w_all, received_2[0], cols))
    col_sum = jnp.sum(spread(cols, ("y", "z"), 16), 0)
    far_terms = terms(where, True, c_1, c_2, w_all)
    far_core = lax.ppermute(far_terms, "c", SWAP)
    far_terms, received_1[0], col_sum, w_all = after((far_terms, received_1[0], col_sum, w_all))

    col_prev_mine = mine(col_prev, half, 0, xl)
    col_half = decay_rate * col_prev_mine + (1.0 - decay_rate) * (col_sum / D + tiny_eps)
    near_terms = terms(where, False, c_1, c_2, w_all)
    near_core = lax.ppermute(near_terms, "c", SWAP)
    near_terms, far_core, received_1[1] = after((near_terms, far_core, received_1[1]))

    def over_columns(g, col):
        return jnp.sum(g * g * (1.0 / col)[None, :], 1)

    col_1, col_2 = col_half[:WIDE], col_half[WIDE:]
    over_own = over_columns(g_1, col_1) + over_columns(g_2, col_2)
    over_other, first = 0.0, 0
    for g in send_1 + send_2:
        over_other = over_other + over_columns(g, col_half[first : first + g.shape[1]])
        first += g.shape[1]
    plain = jnp.sum(rows_1 + rows_2, 1)
    plain_own, plain_other = own_other(plain, first_xl, 0)
    sums = jnp.stack([plain_own, over_own, plain_other, over_other])
    give_1, give_2, far_give, far_keep = terms(where, True, c_1, c_2, w_all, far_core)
    seen = spread(sums, ("xl", "xh", "c"), 8).reshape(2, 4, 4, 256)
    got_1 = lax.ppermute(give_1, ("xl", "xh"), DIAG)
    got_far = lax.ppermute(far_give, "xl", SWAP)
    keep_1, keep_2, own_b, give_b = terms(where, False, c_1, c_2, w_all, near_core)
    seen, far_keep, received_2[1], got_1, got_far, keep_1, give_b = after(
        (seen, far_keep, received_2[1], got_1, got_far, keep_1, give_b)
    )
    same = jnp.sum(jnp.where(first_xl, seen[0], seen[1]), 0)
    cross = jnp.sum(jnp.where(first_xl, seen[1], seen[0]), 0)
    row_sum = jnp.concatenate([same[0] + cross[2], same[2] + cross[0]])
    row_over = jnp.concatenate([same[1] + cross[3], same[3] + cross[1]])
    row_prev_two = jnp.concatenate([row_prev, row_prev_other])
    row_next = decay_rate * row_prev_two + (1.0 - decay_rate) * (row_sum / FF + tiny_eps)
    row_own = row_next[:256]

    lane = lax.broadcasted_iota(jnp.int32, (128,), 0)
    pair = jnp.where(lane == 0, jnp.sum(row_over / row_next), jnp.where(lane == 1, jnp.sum(row_next), 0.0))
    totals = spread(pair, ("y", "z"), 16)
    got_2 = lax.ppermute(give_2, ("xl", "xh"), DIAG)
    col_other = lax.ppermute(col_half, "xl", SWAP)
    got_b = lax.ppermute(give_b, "xl", SWAP)
    totals, col_other, got_2, got_b = after((totals, col_other, got_2, got_b))
    totals = jnp.sum(totals, 0)
    last_b = lax.ppermute(far_keep + got_far, ("xl", "xh"), DIAG)
    keep_a, got_a = jnp.concatenate([keep_1, keep_2]), jnp.concatenate([got_1, got_2])
    last_a = lax.ppermute(keep_a[:, 256:] + got_a[:, :256], "xl", SWAP)
    row_mean = totals[1] / D
    update_rms = jnp.sqrt(row_mean * (totals[0] / (D * FF)))
    scale = jnp.sqrt(row_mean) / jnp.maximum(1.0, update_rms)
    update = clipped(
        where,
        scale,
        1.0 / jnp.sqrt(row_own),
        (g_1, g_2),
        (*received_1, *received_2),
        1.0 / jnp.sqrt(col_half),
        1.0 / jnp.sqrt(col_other),
    )
    col_next = jnp.where(
        first_xl, jnp.concatenate([col_half, col_other]), jnp.concatenate([col_other, col_half])
    )

    total_a = (keep_a[:, :256] + got_a[:, 256:]) + last_a
    total_b = (own_b + got_b) + last_b
    total = jnp.concatenate([total_a.astype(BF16), total_b.astype(BF16)])

    return (total, update, row_own, col_next, update_rms)


def solution(mesh):
    fine = Mesh(mesh.devices.reshape(SIZES), AXES)
    fsdp, mp = ("y", "z", "xl"), ("xh", "c")
    in_specs = (P(fsdp, None), P(fsdp, mp), P(fsdp, mp), P(fsdp), P(mp))
    out_specs = (P(mp, fsdp), P(fsdp, mp), P(fsdp), P(mp), P())
    return jax.shard_map(body, mesh=fine, in_specs=in_specs, out_specs=out_specs, check_vma=False)
```

time: 276 us -> 259 us (0.938)
  waiting for transfers between devices: 92.8 us -> 68.3 us
  starting transfers between devices: 61.3 us -> 67.8 us
    ppermute x18, waiting for transfers between devices: 47.3 us -> 34.7 us  [shift(): return lax.ppermute(a, axis, [(i, (i + k) % 4) for i in range(4)])]
    all_to_all x3, waiting for transfers between devices: 14.9 us -> 3.39 us  [spread(): return lax.all_to_all(copies, axes, split_axis=0, concat_axis=0, tiled=True)]
    ppermute x1, waiting for transfers between devices: 11.4 us -> 3.03 us  [body(): row_prev_other = lax.ppermute(row_prev, 'xl', SWAP)]
    ppermute x6 -> x10, starting transfers between devices: 5.95 us -> 13.4 us  [the longest x1 3.23 us: body(): got_1 = lax.ppermute(give_1, ('xl', 'xh'), DIAG)]
    ppermute x1, waiting for transfers between devices: 11 us -> 4.45 us  [body(): w_other = lax.ppermute(mine(weight, half, 1, 1 - xl), 'xl', SWAP)]
    ppermute x1, waiting for transfers between devices: 0.01 us -> 5.38 us  [body(): got_b = lax.ppermute(give_b, 'xl', SWAP)]
    unnamed x47 -> x85, local copies, waits for them, and re-layouts: 4.2 us -> 8.73 us
    ppermute x6 -> x10, waiting for transfers between devices: 0.02 us -> 4.33 us  [the longest x1 3.77 us: body(): got_1 = lax.ppermute(give_1, ('xl', 'xh'), DIAG)]
  transfers between devices with their start and end apart: 40 -> 44, of which waited for: 17 -> 20; matrix products, arithmetic and copies ran while one was open for 9% -> 10% of each run, Pallas kernels for 25% -> 26%
where the time goes in v3:
time: 259 us; the launch traced here: 257 us
  waiting for transfers between devices  68.3 us (26%)
  Pallas kernels  68.1 us (26%)
  starting transfers between devices  67.8 us (26%)
  local copies, waits for them, and re-layouts  18.9 us (7%)
  between operations  17.8 us (7%)
  other arithmetic  16.1 us (6%)
    ppermute x18, waiting for transfers between devices, shift(): return lax.ppermute(a, axis, [(i, (i + k) % 4) for i in range(4)])  34.7 us
    pallas_call x4, Pallas kernels, terms(): pl.pallas_call(kernel, grid_spec=pltpu.PrefetchScalarGridSpec(num_scalar_...  28.3 us
    ppermute x18, starting transfers between devices, shift(): return lax.ppermute(a, axis, [(i, (i + k) % 4) for i in range(4)])  22.1 us
    all_to_all x3, starting transfers between devices, spread(): return lax.all_to_all(copies, axes, split_axis=0, concat_axis=0, tiled=True)  17 us
    pallas_call x1, Pallas kernels, transposed_tokens(): pl.pallas_call(kernel, grid_spec=pltpu.PrefetchScalarGridSpec(num_scalar_...  12.1 us
    pallas_call x1, Pallas kernels, gradient_of_pieces(): pl.pallas_call(kernel, out_shape=(jax.ShapeDtypeStruct((n, 128, width), B...  11.9 us
    pallas_call x1, Pallas kernels, gradient(): pl.pallas_call(kernel, grid=(width // TILE,), out_shape=grad_shapes(width...  9.81 us
    unnamed x85, local copies, waits for them, and re-layouts  8.73 us
  transfers between devices with their start and end apart: 44, of which 20 were waited for; matrix products, arithmetic and copies ran while one was open for 10% of the time, Pallas kernels for 26%

profile of v3, /device:TPU:0, one launch (start us, length us, event | category | flops | bytes accessed | tf_op | source)
XLA Modules:
  0.0 257.2 jit_solution(9800895524097305964)
XLA Ops:
  13.0 8.1 %all-to-all-start = ((bf16[1,32,16,512]{3,1,0,2:T(8,128)(2,1)}), bf16[1,32,16,512]{3,1,0,2:T(8,128)(2,1)}, u32[]{:S(2)}, u32[]{:S(2)}) async-start(bf16[1,32,16,512]{3,1,0,2:T(8,128)(2,1)} %copy.24), calls=%async_computation | async-start | bytes 1048576 | tf_op jit(solution)/shard_map/all_to_all | solution.py:321
  21.8 3.0 %collective-permute-done.1 = f32[256]{0:T(256)S(1)} collective-permute-done((f32[256]{0:T(256)S(1)}, f32[256]{0:T(256)S(1)}, u32[]{:S(2)}, u32[]{:S(2)}) %collective-permute-start.1) | collective-permute-done | bytes 1056 | tf_op jit(solution)/shard_map/ppermute | solution.py:324
  24.8 7.6 %all-to-all-done = bf16[1,32,16,512]{3,1,0,2:T(8,128)(2,1)} async-done(((bf16[1,32,16,512]{3,1,0,2:T(8,128)(2,1)}), bf16[1,32,16,512]{3,1,0,2:T(8,128)(2,1)}, u32[]{:S(2)}, u32[]{:S(2)}) %all-to-all-start) | async-done | bytes 524320 | tf_op jit(solution)/shard_map/all_to_all | solution.py:321
  43.6 2.7 %collective-permute-start.9 = (bf16[16,32,512]{2,1,0:T(8,128)(2,1)}, bf16[16,32,512]{2,1,0:T(8,128)(2,1)S(1)}, u32[]{:S(2)}, u32[]{:S(2)}) collective-permute-start(bf16[16,32,512]{2,1,0:T(8,128)(2,1)} %bitcast.37.a_ref), channel_id=1, source_target_pairs={{0,2},{2,0},{1,3},{3,1},{4,6},{6,4},{5,7},{7,5},{8,10},{10,8},{9,1... | collective-permute-start | bytes 1572872 | tf_op jit(solution)/shard_map/ppermute | solution.py:334
  48.3 4.1 %collective-permute-done.5 = bf16[128,1024]{1,0:T(8,128)(2,1)S(1)} collective-permute-done((bf16[128,1024]{1,0:T(8,128)(2,1)S(1)}, bf16[128,1024]{1,0:T(8,128)(2,1)S(1)}, u32[]{:S(2)}, u32[]{:S(2)}) %collective-permute-start.5) | collective-permute-done | bytes 262176 | tf_op jit(solution)/shard_map/ppermute | solution.py:38
  52.8 9.0 %collective-permute-done.4 = bf16[128,1024]{1,0:T(8,128)(2,1)S(1)} collective-permute-done((bf16[128,1024]{1,0:T(8,128)(2,1)S(1)}, bf16[128,1024]{1,0:T(8,128)(2,1)S(1)}, u32[]{:S(2)}, u32[]{:S(2)}) %collective-permute-start.4) | collective-permute-done | bytes 262176 | tf_op jit(solution)/shard_map/ppermute | solution.py:38
  66.4 4.0 %collective-permute-done.13.refs_10_ = bf16[256,1024]{1,0:T(8,128)(2,1)S(1)} collective-permute-done((bf16[256,1024]{1,0:T(8,128)(2,1)S(1)}, bf16[256,1024]{1,0:T(8,128)(2,1)S(1)}, u32[]{:S(2)}, u32[]{:S(2)}) %collective-permute-start.13) | collective-permute-done | bytes 524320 | tf_op jit(solution)/shard_map/ppermute | solution.py:38
  71.2 5.7 %collective-permute-done.11.refs_2_ = bf16[256,1024]{1,0:T(8,128)(2,1)S(1)} collective-permute-done((bf16[256,1024]{1,0:T(8,128)(2,1)S(1)}, bf16[256,1024]{1,0:T(8,128)(2,1)S(1)}, u32[]{:S(2)}, u32[]{:S(2)}) %collective-permute-start.11) | collective-permute-done | bytes 524320 | tf_op jit(solution)/shard_map/ppermute | solution.py:38
  76.9 5.7 %collective-permute-done.12.refs_3_ = bf16[256,1024]{1,0:T(8,128)(2,1)S(1)} collective-permute-done((bf16[256,1024]{1,0:T(8,128)(2,1)}, bf16[256,1024]{1,0:T(8,128)(2,1)S(1)}, u32[]{:S(2)}, u32[]{:S(2)}) %collective-permute-start.12) | collective-permute-done | bytes 524320 | tf_op jit(solution)/shard_map/ppermute | solution.py:38
  88.7 3.2 %collective-permute-start.22 = (bf16[256,1024]{1,0:T(8,128)(2,1)}, bf16[256,1024]{1,0:T(8,128)(2,1)}, u32[]{:S(2)}, u32[]{:S(2)}) collective-permute-start(bf16[256,1024]{1,0:T(8,128)(2,1)} %copy-done.31), channel_id=1, source_target_pairs={{0,96},{32,0},{64,32},{96,64},{1,97},{33,1},{65,33},{97,65},{2,98}... | collective-permute-start | bytes 1572872 | tf_op jit(solution)/shard_map/ppermute | solution.py:38
  91.9 3.7 %collective-permute-start.18 = (bf16[256,1024]{1,0:T(8,128)(2,1)}, bf16[256,1024]{1,0:T(8,128)(2,1)}, u32[]{:S(2)}, u32[]{:S(2)}) collective-permute-start(bf16[256,1024]{1,0:T(8,128)(2,1)} %copy-done.33), channel_id=1, source_target_pairs={{0,24},{8,0},{16,8},{24,16},{1,25},{9,1},{17,9},{25,17},{2,26},{10... | collective-permute-start | bytes 1572872 | tf_op jit(solution)/shard_map/ppermute | solution.py:38
  95.6 12.1 %shard_map.92.xt_ref = bf16[512,4096]{1,0:T(8,128)(2,1)} custom-call(s32[3]{0:T(128)} %pad_add_fusion.where_ref.xl_ref, bf16[16,32,512]{2,1,0:T(8,128)(2,1)} %bitcast.37.a_ref, bf16[16,32,512]{2,1,0:T(8,128)(2,1)} %copy-done.22, bf16[16,32,512]{2,1,0:T(8,128)(2,1)} %copy-done.21, bf16[16,32,512]{2,1,0:T(8,128)(2,1)} %copy-done.20, ...), custom_call_target="tpu_custom_call" | custom-call | flops 20000000000 | bytes 1 | tf_op jit(solution)/shard_map/pallas_call | solution.py:80
  107.7 4.4 %collective-permute-done.25 = bf16[256,2048]{0,1:T(8,128)(2,1)S(1)} collective-permute-done((bf16[256,2048]{0,1:T(8,128)(2,1)}, bf16[256,2048]{0,1:T(8,128)(2,1)S(1)}, u32[]{:S(2)}, u32[]{:S(2)}) %collective-permute-start.25) | collective-permute-done | bytes 1048608 | tf_op jit(solution)/shard_map/ppermute | solution.py:342
  112.1 3.6 %collective-permute-start.20 = (bf16[256,1024]{1,0:T(8,128)(2,1)S(1)}, bf16[256,1024]{1,0:T(8,128)(2,1)}, u32[]{:S(2)}, u32[]{:S(2)}) collective-permute-start(bf16[256,1024]{1,0:T(8,128)(2,1)S(1)} %copy-done.13), channel_id=1, source_target_pairs={{0,24},{8,0},{16,8},{24,16},{1,25},{9,1},{17,9},{25,17},{2,26},{10... | collective-permute-start | bytes 1572872 | tf_op jit(solution)/shard_map/ppermute | solution.py:38
  117.6 3.0 %collective-permute-start.24 = (bf16[256,1024]{1,0:T(8,128)(2,1)S(1)}, bf16[256,1024]{1,0:T(8,128)(2,1)S(1)}, u32[]{:S(2)}, u32[]{:S(2)}) collective-permute-start(bf16[256,1024]{1,0:T(8,128)(2,1)S(1)} %copy-done.11), channel_id=1, source_target_pairs={{0,96},{32,0},{64,32},{96,64},{1,97},{33,1},{65,33},{97,65},{2,98}... | collective-permute-start | bytes 1572872 | tf_op jit(solution)/shard_map/ppermute | solution.py:38
  122.1 9.8 %shard_map.93 = (f32[256,1024]{1,0:T(8,128)}, f32[512,128]{1,0:T(8,128)}, f32[8,1024]{1,0:T(8,128)}, f32[256,512]{1,0:T(8,128)}, f32[256,512]{1,0:T(8,128)}) custom-call(s32[3]{0:T(128)} %pad_add_fusion.where_ref.xl_ref, bf16[512,4096]{1,0:T(8,128)(2,1)} %shard_map.92.xt_ref, bf16[4096,1024]{1,0:T(8,128)(2,1)} %bitcast.86), custom_call_target="tpu_custom_call" | custom-call | flops 20000000000 | bytes 1 | tf_op jit(solution)/shard_map/pallas_call | solution.py:188
  131.9 2.6 %collective-permute-done.23.refs_14_ = bf16[256,1024]{1,0:T(8,128)(2,1)S(1)} collective-permute-done((bf16[256,1024]{1,0:T(8,128)(2,1)}, bf16[256,1024]{1,0:T(8,128)(2,1)S(1)}, u32[]{:S(2)}, u32[]{:S(2)}) %collective-permute-start.23) | collective-permute-done | bytes 524320 | tf_op jit(solution)/shard_map/ppermute | solution.py:38
  136.0 11.9 %shard_map.94 = (bf16[32,128,1024]{2,1,0:T(8,128)(2,1)}, f32[256,1024]{1,0:T(8,128)}, f32[512,128]{1,0:T(8,128)}, f32[8,1024]{1,0:T(8,128)}, f32[256,512]{1,0:T(8,128)}, /*index=5*/f32[256,512]{1,0:T(8,128)}) custom-call(s32[3]{0:T(128)} %pad_add_fusion.where_ref.xl_ref, s32[32]{0:T(128)} %stack.184.index_ref, bf16[512,4096]{1,0:T(8,128)(2,1)} %shard_map.92.xt_ref, ...), custom_call_target="tpu_custom_call" | custom-call | flops 20000000000 | bytes 1 | tf_op jit(solution)/shard_map/pallas_call | solution.py:153
  154.2 7.0 %all-to-all-start.1 = ((f32[16,1,2048]{2,1,0:T(1,128)}), f32[16,1,2048]{2,1,0:T(1,128)S(1)}, u32[]{:S(2)}, u32[]{:S(2)}) async-start(f32[16,1,2048]{2,1,0:T(1,128)} %broadcast_in_dim.22), calls=%async_computation.1 | async-start | bytes 262144 | tf_op jit(solution)/shard_map/all_to_all | solution.py:30
  161.2 6.6 %shard_map.95 = f32[1024,512]{1,0:T(8,128)} custom-call(s32[3]{0:T(128)} %pad_add_fusion.where_ref.xl_ref, bf16[4096,1024]{1,0:T(8,128)(2,1)} %bitcast.91, bf16[4096,1024]{1,0:T(8,128)(2,1)} %bitcast.87, bf16[2048,512]{1,0:T(8,128)(2,1)} %fusion.w_ref), custom_call_target="tpu_custom_call" | custom-call | flops 20000000000 | bytes 1 | tf_op jit(solution)/shard_map/pallas_call | solution.py:239
  171.1 6.5 %shard_map.96 = f32[1024,512]{1,0:T(8,128)} custom-call(s32[3]{0:T(128)} %pad_add_fusion.where_ref.xl_ref, bf16[4096,1024]{1,0:T(8,128)(2,1)} %bitcast.92, bf16[4096,1024]{1,0:T(8,128)(2,1)} %bitcast.88, bf16[2048,512]{1,0:T(8,128)(2,1)} %fusion.w_ref), custom_call_target="tpu_custom_call" | custom-call | flops 20000000000 | bytes 1 | tf_op jit(solution)/shard_map/pallas_call | solution.py:239
  180.3 3.7 %all-to-all-start.2 = ((f32[8,4,256]{2,1,0:T(4,128)}), f32[8,4,256]{2,1,0:T(4,128)S(1)}, u32[]{:S(2)}, u32[]{:S(2)}) async-start(f32[8,4,256]{2,1,0:T(4,128)} %broadcast_in_dim.23), calls=%async_computation.2 | async-start | bytes 65536 | tf_op jit(solution)/shard_map/all_to_all | solution.py:30
  184.0 7.6 %shard_map.97 = (f32[256,512]{1,0:T(8,128)}, f32[256,512]{1,0:T(8,128)}, f32[512,256]{1,0:T(8,128)}, f32[512,256]{1,0:T(8,128)}) custom-call(s32[3]{0:T(128)} %pad_add_fusion.where_ref.xl_ref, bf16[4096,1024]{1,0:T(8,128)(2,1)} %bitcast.93, bf16[4096,1024]{1,0:T(8,128)(2,1)} %bitcast.89, bf16[2048,512]{1,0:T(8,128)(2,1)} %fusion.w_ref, ...), custom_call_target="tpu_custom_call" | custom-call | flops 20000000000 | bytes 1 | tf_op jit(solution)/shard_map/pallas_call | solution.py:239
  191.6 3.2 %collective-permute-start.31 = (f32[256,512]{1,0:T(8,128)}, f32[256,512]{1,0:T(8,128)S(1)}, u32[]{:S(2)}, u32[]{:S(2)}) collective-permute-start(f32[256,512]{1,0:T(8,128)} %get-tuple-element.137), channel_id=1, source_target_pairs={{0,6},{6,0},{2,4},{4,2},{1,7},{7,1},{3,5},{5,3},{8,14},{14,8},{10,... | collective-permute-start | bytes 1572872 | tf_op jit(solution)/shard_map/ppermute | solution.py:378
  196.3 7.6 %shard_map.98 = (f32[256,512]{1,0:T(8,128)}, f32[256,512]{1,0:T(8,128)}, f32[512,256]{1,0:T(8,128)}, f32[512,256]{1,0:T(8,128)}) custom-call(s32[3]{0:T(128)} %pad_add_fusion.where_ref.xl_ref, bf16[4096,1024]{1,0:T(8,128)(2,1)} %bitcast.94, bf16[4096,1024]{1,0:T(8,128)(2,1)} %bitcast.90, bf16[2048,512]{1,0:T(8,128)(2,1)} %fusion.w_ref, ...), custom_call_target="tpu_custom_call" | custom-call | flops 20000000000 | bytes 1 | tf_op jit(solution)/shard_map/pallas_call | solution.py:239
  203.9 3.8 %collective-permute-done.31 = f32[256,512]{1,0:T(8,128)S(1)} collective-permute-done((f32[256,512]{1,0:T(8,128)}, f32[256,512]{1,0:T(8,128)S(1)}, u32[]{:S(2)}, u32[]{:S(2)}) %collective-permute-start.31) | collective-permute-done | bytes 524320 | tf_op jit(solution)/shard_map/ppermute | solution.py:378
  211.3 6.3 %all-to-all-start.3 = ((f32[16,1,128]{2,1,0:T(1,128)}), f32[16,1,128]{2,1,0:T(1,128)S(1)}, u32[]{:S(2)}, u32[]{:S(2)}) async-start(f32[16,1,128]{2,1,0:T(1,128)} %broadcast_in_dim.47), calls=%async_computation.3 | async-start | bytes 16384 | tf_op jit(solution)/shard_map/all_to_all | solution.py:30
  219.3 2.1 collective-permute-start.38
  223.0 2.1 all-to-all-done.3
  225.1 5.4 %collective-permute-done.36 = f32[512,256]{1,0:T(8,128)S(1)} collective-permute-done((f32[512,256]{1,0:T(8,128)}, f32[512,256]{1,0:T(8,128)S(1)}, u32[]{:S(2)}, u32[]{:S(2)}) %collective-permute-start.36) | collective-permute-done | bytes 524320 | tf_op jit(solution)/shard_map/ppermute | solution.py:397
  236.2 6.0 %shard_map.99 = f32[256,4096]{1,0:T(8,128)} custom-call(s32[3]{0:T(128)} %pad_add_fusion.where_ref.xl_ref, f32[1]{0:T(128)} %bitcast.58.scale_ref, f32[256,1]{1,0:T(8,128)} %copy.28.row_ref, f32[1,4096]{1,0:T(1,128)} %bitcast.76, f32[256,1024]{1,0:T(8,128)} %get-tuple-element.121.refs_0_, f32[256,1024]{1,0:T(8,128)} %get-tuple-element.131.refs_1_, ...), custom_call_target="tpu_custom_call" | custom-call | flops 20000000000 | bytes 1 | tf_op jit(solution)/shard_map/pallas_call | solution.py:283
  244.2 3.0 %collective-permute-done.37 = f32[512,256]{1,0:T(8,128)} collective-permute-done((f32[512,256]{1,0:T(8,128)}, f32[512,256]{1,0:T(8,128)}, u32[]{:S(2)}, u32[]{:S(2)}) %collective-permute-start.37) | collective-permute-done | bytes 524320 | tf_op jit(solution)/shard_map/ppermute | solution.py:402
  (200 shorter events, 64.1 us)
Async XLA Ops:
  10.1 22.3 %collective-permute-start = (bf16[128,2048]{1,0:T(8,128)(2,1)S(1)}, bf16[128,2048]{1,0:T(8,128)(2,1)S(1)}, u32[]{:S(2)}, u32[]{:S(2)}) collective-permute-start(bf16[128,2048]{1,0:T(8,128)(2,1)S(1)} %get-tuple-element.82), channel_id=1, source_target_pairs={{0,4},{4,0},{1,5},{5,1},{2,6},{6,2},{3,7},{7,3},{8,12},{12,8},{9,1... | collective-permute-start | bytes 1572872 | tf_op jit(solution)/shard_map/ppermute | solution.py:319
  13.0 19.4 %all-to-all-start = ((bf16[1,32,16,512]{3,1,0,2:T(8,128)(2,1)}), bf16[1,32,16,512]{3,1,0,2:T(8,128)(2,1)}, u32[]{:S(2)}, u32[]{:S(2)}) async-start(bf16[1,32,16,512]{3,1,0,2:T(8,128)(2,1)} %copy.24), calls=%async_computation | async-start | bytes 1048576 | tf_op jit(solution)/shard_map/all_to_all | solution.py:321
  21.1 100.9 %all-gather.2.cloned.1.call-start = ((), (), s32[]{:S(2)}) async-start(), calls=%async_computation.4 | async-start | bytes 8912896 | tf_op jit(solution)/shard_map/all_gather | solution.py:329
  37.2 15.3 %collective-permute-start.2 = (bf16[128,1024]{1,0:T(8,128)(2,1)S(1)}, bf16[128,1024]{1,0:T(8,128)(2,1)S(1)}, u32[]{:S(2)}, u32[]{:S(2)}) collective-permute-start(bf16[128,1024]{1,0:T(8,128)(2,1)S(1)} %get-tuple-element.173), channel_id=1, source_target_pairs={{0,32},{32,64},{64,96},{96,0},{1,33},{33,65},{65,97},{97,1},{2,34}... | collective-permute-start | bytes 786440 | tf_op jit(solution)/shard_map/ppermute | solution.py:38
  38.1 14.4 %collective-permute-start.5 = (bf16[128,1024]{1,0:T(8,128)(2,1)S(1)}, bf16[128,1024]{1,0:T(8,128)(2,1)S(1)}, u32[]{:S(2)}, u32[]{:S(2)}) collective-permute-start(bf16[128,1024]{1,0:T(8,128)(2,1)S(1)} %get-tuple-element.175), channel_id=1, source_target_pairs={{0,8},{8,16},{16,24},{24,0},{1,9},{9,17},{17,25},{25,1},{2,10},{10... | collective-permute-start | bytes 786440 | tf_op jit(solution)/shard_map/ppermute | solution.py:38
  39.8 23.3 %collective-permute-start.10 = (bf16[16,32,512]{2,1,0:T(8,128)(2,1)}, bf16[16,32,512]{2,1,0:T(8,128)(2,1)S(1)}, u32[]{:S(2)}, u32[]{:S(2)}) collective-permute-start(bf16[16,32,512]{2,1,0:T(8,128)(2,1)} %bitcast.37.a_ref), channel_id=1, source_target_pairs={{0,6},{6,0},{2,4},{4,2},{1,7},{7,1},{3,5},{5,3},{8,14},{14,8},{10,... | collective-permute-start | bytes 1572872 | tf_op jit(solution)/shard_map/ppermute | solution.py:334
  43.6 21.1 %collective-permute-start.9 = (bf16[16,32,512]{2,1,0:T(8,128)(2,1)}, bf16[16,32,512]{2,1,0:T(8,128)(2,1)S(1)}, u32[]{:S(2)}, u32[]{:S(2)}) collective-permute-start(bf16[16,32,512]{2,1,0:T(8,128)(2,1)} %bitcast.37.a_ref), channel_id=1, source_target_pairs={{0,2},{2,0},{1,3},{3,1},{4,6},{6,4},{5,7},{7,5},{8,10},{10,8},{9,1... | collective-permute-start | bytes 1572872 | tf_op jit(solution)/shard_map/ppermute | solution.py:334
  47.1 14.7 %collective-permute-start.4 = (bf16[128,1024]{1,0:T(8,128)(2,1)S(1)}, bf16[128,1024]{1,0:T(8,128)(2,1)S(1)}, u32[]{:S(2)}, u32[]{:S(2)}) collective-permute-start(bf16[128,1024]{1,0:T(8,128)(2,1)S(1)} %get-tuple-element.173), channel_id=1, source_target_pairs={{0,64},{32,96},{64,0},{96,32},{1,65},{33,97},{65,1},{97,33},{2,66}... | collective-permute-start | bytes 786440 | tf_op jit(solution)/shard_map/ppermute | solution.py:38
  52.5 17.8 %collective-permute-start.13 = (bf16[256,1024]{1,0:T(8,128)(2,1)S(1)}, bf16[256,1024]{1,0:T(8,128)(2,1)S(1)}, u32[]{:S(2)}, u32[]{:S(2)}) collective-permute-start(bf16[256,1024]{1,0:T(8,128)(2,1)S(1)} %pad_maximum_fusion.2.refs_8_), channel_id=1, source_target_pairs={{0,32},{32,64},{64,96},{96,0},{1,33},{33,65},{65,97},{97,1},{2,34}... | collective-permute-start | bytes 1572872 | tf_op jit(solution)/shard_map/ppermute | solution.py:38
  64.7 17.9 %collective-permute-start.12 = (bf16[256,1024]{1,0:T(8,128)(2,1)}, bf16[256,1024]{1,0:T(8,128)(2,1)S(1)}, u32[]{:S(2)}, u32[]{:S(2)}) collective-permute-start(bf16[256,1024]{1,0:T(8,128)(2,1)} %constant_dynamic-update-slice_fusion.refs_1_), channel_id=1, source_target_pairs={{0,24},{8,0},{16,8},{24,16},{1,25},{9,1},{17,9},{25,17},{2,26},{10... | collective-permute-start | bytes 1572872 | tf_op jit(solution)/shard_map/ppermute | solution.py:38
  86.8 25.3 %collective-permute-start.25 = (bf16[256,2048]{0,1:T(8,128)(2,1)}, bf16[256,2048]{0,1:T(8,128)(2,1)S(1)}, u32[]{:S(2)}, u32[]{:S(2)}) collective-permute-start(bf16[256,2048]{0,1:T(8,128)(2,1)} %copy.31), channel_id=1, source_target_pairs={{0,4},{4,0},{1,5},{5,1},{2,6},{6,2},{3,7},{7,3},{8,12},{12,8},{9,1... | collective-permute-start | bytes 3145736 | tf_op jit(solution)/shard_map/ppermute | solution.py:342
  88.7 28.9 %collective-permute-start.21 = (bf16[256,1024]{1,0:T(8,128)(2,1)}, bf16[256,1024]{1,0:T(8,128)(2,1)}, u32[]{:S(2)}, u32[]{:S(2)}) collective-permute-start(bf16[256,1024]{1,0:T(8,128)(2,1)} %copy-done.30), channel_id=1, source_target_pairs={{0,32},{32,64},{64,96},{96,0},{1,33},{33,65},{65,97},{97,1},{2,34}... | collective-permute-start | bytes 1572872 | tf_op jit(solution)/shard_map/ppermute | solution.py:38
  88.7 28.9 %collective-permute-start.22 = (bf16[256,1024]{1,0:T(8,128)(2,1)}, bf16[256,1024]{1,0:T(8,128)(2,1)}, u32[]{:S(2)}, u32[]{:S(2)}) collective-permute-start(bf16[256,1024]{1,0:T(8,128)(2,1)} %copy-done.31), channel_id=1, source_target_pairs={{0,96},{32,0},{64,32},{96,64},{1,97},{33,1},{65,33},{97,65},{2,98}... | collective-permute-start | bytes 1572872 | tf_op jit(solution)/shard_map/ppermute | solution.py:38
  91.9 28.6 %collective-permute-start.17 = (bf16[256,1024]{1,0:T(8,128)(2,1)}, bf16[256,1024]{1,0:T(8,128)(2,1)}, u32[]{:S(2)}, u32[]{:S(2)}) collective-permute-start(bf16[256,1024]{1,0:T(8,128)(2,1)} %copy-done.32), channel_id=1, source_target_pairs={{0,8},{8,16},{16,24},{24,0},{1,9},{9,17},{17,25},{25,1},{2,10},{10... | collective-permute-start | bytes 1572872 | tf_op jit(solution)/shard_map/ppermute | solution.py:38
  91.9 39.9 %collective-permute-start.18 = (bf16[256,1024]{1,0:T(8,128)(2,1)}, bf16[256,1024]{1,0:T(8,128)(2,1)}, u32[]{:S(2)}, u32[]{:S(2)}) collective-permute-start(bf16[256,1024]{1,0:T(8,128)(2,1)} %copy-done.33), channel_id=1, source_target_pairs={{0,24},{8,0},{16,8},{24,16},{1,25},{9,1},{17,9},{25,17},{2,26},{10... | collective-permute-start | bytes 1572872 | tf_op jit(solution)/shard_map/ppermute | solution.py:38
  112.1 19.7 %collective-permute-start.20 = (bf16[256,1024]{1,0:T(8,128)(2,1)S(1)}, bf16[256,1024]{1,0:T(8,128)(2,1)}, u32[]{:S(2)}, u32[]{:S(2)}) collective-permute-start(bf16[256,1024]{1,0:T(8,128)(2,1)S(1)} %copy-done.13), channel_id=1, source_target_pairs={{0,24},{8,0},{16,8},{24,16},{1,25},{9,1},{17,9},{25,17},{2,26},{10... | collective-permute-start | bytes 1572872 | tf_op jit(solution)/shard_map/ppermute | solution.py:38
  117.5 14.4 %collective-permute-start.19 = (bf16[256,1024]{1,0:T(8,128)(2,1)}, bf16[256,1024]{1,0:T(8,128)(2,1)S(1)}, u32[]{:S(2)}, u32[]{:S(2)}) collective-permute-start(bf16[256,1024]{1,0:T(8,128)(2,1)} %constant_dynamic-update-slice_fusion.refs_1_), channel_id=1, source_target_pairs={{0,8},{8,16},{16,24},{24,0},{1,9},{9,17},{17,25},{25,1},{2,10},{10... | collective-permute-start | bytes 1572872 | tf_op jit(solution)/shard_map/ppermute | solution.py:38
  117.6 14.4 %collective-permute-start.24 = (bf16[256,1024]{1,0:T(8,128)(2,1)S(1)}, bf16[256,1024]{1,0:T(8,128)(2,1)S(1)}, u32[]{:S(2)}, u32[]{:S(2)}) collective-permute-start(bf16[256,1024]{1,0:T(8,128)(2,1)S(1)} %copy-done.11), channel_id=1, source_target_pairs={{0,96},{32,0},{64,32},{96,64},{1,97},{33,1},{65,33},{97,65},{2,98}... | collective-permute-start | bytes 1572872 | tf_op jit(solution)/shard_map/ppermute | solution.py:38
  120.6 14.0 %collective-permute-start.23 = (bf16[256,1024]{1,0:T(8,128)(2,1)}, bf16[256,1024]{1,0:T(8,128)(2,1)S(1)}, u32[]{:S(2)}, u32[]{:S(2)}) collective-permute-start(bf16[256,1024]{1,0:T(8,128)(2,1)} %constant_dynamic-update-slice_fusion.2.refs_9_), channel_id=1, source_target_pairs={{0,32},{32,64},{64,96},{96,0},{1,33},{33,65},{65,97},{97,1},{2,34}... | collective-permute-start | bytes 1572872 | tf_op jit(solution)/shard_map/ppermute | solution.py:38
  135.3 18.0 %collective-permute-start.26 = (f32[256,512]{1,0:T(8,128)}, f32[256,512]{1,0:T(8,128)S(1)}, u32[]{:S(2)}, u32[]{:S(2)}) collective-permute-start(f32[256,512]{1,0:T(8,128)} %get-tuple-element.124), channel_id=1, source_target_pairs={{0,4},{4,0},{1,5},{5,1},{2,6},{6,2},{3,7},{7,3},{8,12},{12,8},{9,1... | collective-permute-start | bytes 1572872 | tf_op jit(solution)/shard_map/ppermute | solution.py:347
  148.0 21.2 %collective-permute-start.27 = (f32[256,512]{1,0:T(8,128)}, f32[256,512]{1,0:T(8,128)S(1)}, u32[]{:S(2)}, u32[]{:S(2)}) collective-permute-start(f32[256,512]{1,0:T(8,128)} %get-tuple-element.128), channel_id=1, source_target_pairs={{0,4},{4,0},{1,5},{5,1},{2,6},{6,2},{3,7},{7,3},{8,12},{12,8},{9,1... | collective-permute-start | bytes 1572872 | tf_op jit(solution)/shard_map/ppermute | solution.py:350
  149.4 34.6 %collective-permute-start.29 = (f32[256,512]{1,0:T(8,128)}, f32[256,512]{1,0:T(8,128)}, u32[]{:S(2)}, u32[]{:S(2)}) collective-permute-start(f32[256,512]{1,0:T(8,128)} %get-tuple-element.132), channel_id=1, source_target_pairs={{0,4},{4,0},{1,5},{5,1},{2,6},{6,2},{3,7},{7,3},{8,12},{12,8},{9,1... | collective-permute-start | bytes 1572872 | tf_op jit(solution)/shard_map/ppermute | solution.py:350
  150.1 53.9 %collective-permute-start.30 = (f32[256,512]{1,0:T(8,128)}, f32[256,512]{1,0:T(8,128)}, u32[]{:S(2)}, u32[]{:S(2)}) collective-permute-start(f32[256,512]{1,0:T(8,128)} %get-tuple-element.133), channel_id=1, source_target_pairs={{0,4},{4,0},{1,5},{5,1},{2,6},{6,2},{3,7},{7,3},{8,12},{12,8},{9,1... | collective-permute-start | bytes 1572872 | tf_op jit(solution)/shard_map/ppermute | solution.py:347
  154.2 14.9 %all-to-all-start.1 = ((f32[16,1,2048]{2,1,0:T(1,128)}), f32[16,1,2048]{2,1,0:T(1,128)S(1)}, u32[]{:S(2)}, u32[]{:S(2)}) async-start(f32[16,1,2048]{2,1,0:T(1,128)} %broadcast_in_dim.22), calls=%async_computation.1 | async-start | bytes 262144 | tf_op jit(solution)/shard_map/all_to_all | solution.py:30
  167.8 16.2 %collective-permute-start.28 = (f32[1024,512]{1,0:T(8,128)}, f32[1024,512]{1,0:T(8,128)}, u32[]{:S(2)}, u32[]{:S(2)}) collective-permute-start(f32[1024,512]{1,0:T(8,128)} %shard_map.95), channel_id=1, source_target_pairs={{0,1},{1,0},{2,3},{3,2},{4,5},{5,4},{6,7},{7,6},{8,9},{9,8},{10,11... | collective-permute-start | bytes 6291464 | tf_op jit(solution)/shard_map/ppermute | solution.py:355
  170.0 53.0 %collective-permute-start.34 = (f32[2048]{0:T(1024)S(1)}, f32[2048]{0:T(1024)S(1)}, u32[]{:S(2)}, u32[]{:S(2)}) collective-permute-start(f32[2048]{0:T(1024)S(1)} %get-tuple-element.164), channel_id=1, source_target_pairs={{0,4},{4,0},{1,5},{5,1},{2,6},{6,2},{3,7},{7,3},{8,12},{12,8},{9,1... | collective-permute-start | bytes 24584 | tf_op jit(solution)/shard_map/ppermute | solution.py:396
  177.6 17.4 %collective-permute-start.33 = (f32[1024,512]{1,0:T(8,128)}, f32[1024,512]{1,0:T(8,128)}, u32[]{:S(2)}, u32[]{:S(2)}) collective-permute-start(f32[1024,512]{1,0:T(8,128)} %shard_map.96), channel_id=1, source_target_pairs={{0,1},{1,0},{2,3},{3,2},{4,5},{5,4},{6,7},{7,6},{8,9},{9,8},{10,11... | collective-permute-start | bytes 6291464 | tf_op jit(solution)/shard_map/ppermute | solution.py:361
  180.3 23.7 %all-to-all-start.2 = ((f32[8,4,256]{2,1,0:T(4,128)}), f32[8,4,256]{2,1,0:T(4,128)S(1)}, u32[]{:S(2)}, u32[]{:S(2)}) async-start(f32[8,4,256]{2,1,0:T(4,128)} %broadcast_in_dim.23), calls=%async_computation.2 | async-start | bytes 65536 | tf_op jit(solution)/shard_map/all_to_all | solution.py:30
  191.6 16.1 %collective-permute-start.31 = (f32[256,512]{1,0:T(8,128)}, f32[256,512]{1,0:T(8,128)S(1)}, u32[]{:S(2)}, u32[]{:S(2)}) collective-permute-start(f32[256,512]{1,0:T(8,128)} %get-tuple-element.137), channel_id=1, source_target_pairs={{0,6},{6,0},{2,4},{4,2},{1,7},{7,1},{3,5},{5,3},{8,14},{14,8},{10,... | collective-permute-start | bytes 1572872 | tf_op jit(solution)/shard_map/ppermute | solution.py:378
  194.8 13.9 %collective-permute-start.32 = (f32[512,256]{1,0:T(8,128)}, f32[512,256]{1,0:T(8,128)S(1)}, u32[]{:S(2)}, u32[]{:S(2)}) collective-permute-start(f32[512,256]{1,0:T(8,128)} %get-tuple-element.138), channel_id=1, source_target_pairs={{0,4},{4,0},{1,5},{5,1},{2,6},{6,2},{3,7},{7,3},{8,12},{12,8},{9,1... | collective-permute-start | bytes 1572872 | tf_op jit(solution)/shard_map/ppermute | solution.py:379
  195.1 27.9 %collective-permute-start.35 = (f32[256,512]{1,0:T(8,128)}, f32[256,512]{1,0:T(8,128)}, u32[]{:S(2)}, u32[]{:S(2)}) collective-permute-start(f32[256,512]{1,0:T(8,128)} %get-tuple-element.146), channel_id=1, source_target_pairs={{0,6},{6,0},{2,4},{4,2},{1,7},{7,1},{3,5},{5,3},{8,14},{14,8},{10,... | collective-permute-start | bytes 1572872 | tf_op jit(solution)/shard_map/ppermute | solution.py:395
  219.3 23.5 %collective-permute-start.38 = (f32[512,256]{1,0:T(8,128)S(1)}, f32[512,256]{1,0:T(8,128)}, u32[]{:S(2)}, u32[]{:S(2)}) collective-permute-start(f32[512,256]{1,0:T(8,128)S(1)} %add.458), channel_id=1, source_target_pairs={{0,6},{6,0},{2,4},{4,2},{1,7},{7,1},{3,5},{5,3},{8,14},{14,8},{10,... | collective-permute-start | bytes 1572872 | tf_op jit(solution)/shard_map/ppermute | solution.py:400
  (51 other events, 573.3 us)
Sparse Core Ops, SparseCore 0:
  33.5 88.5 all-gather.1

commit v4 on v3

--- a/solution.py
+++ b/solution.py
@@ -378,9 +378,7 @@
     got_1 = lax.ppermute(give_1, ("xl", "xh"), DIAG)
     got_far = lax.ppermute(far_give, "xl", SWAP)
     keep_1, keep_2, own_b, give_b = terms(where, False, c_1, c_2, w_all, near_core)
-    seen, far_keep, received_2[1], got_1, got_far, keep_1, give_b = after(
-        (seen, far_keep, received_2[1], got_1, got_far, keep_1, give_b)
-    )
+    seen, far_keep, received_2[1], keep_1, give_b = after((seen, far_keep, received_2[1], keep_1, give_b))
     same = jnp.sum(jnp.where(first_xl, seen[0], seen[1]), 0)
     cross = jnp.sum(jnp.where(first_xl, seen[1], seen[0]), 0)
     row_sum = jnp.concatenate([same[0] + cross[2], same[2] + cross[0]])
@@ -395,7 +393,7 @@
     got_2 = lax.ppermute(give_2, ("xl", "xh"), DIAG)
     col_other = lax.ppermute(col_half, "xl", SWAP)
     got_b = lax.ppermute(give_b, "xl", SWAP)
-    totals, col_other, got_2, got_b = after((totals, col_other, got_2, got_b))
+    totals, col_other, got_1, got_far, got_2, got_b = after((totals, col_other, got_1, got_far, got_2, got_b))
     totals = jnp.sum(totals, 0)
     last_b = lax.ppermute(far_keep + got_far, ("xl", "xh"), DIAG)
     keep_a, got_a = jnp.concatenate([keep_1, keep_2]), jnp.concatenate([got_1, got_2])

time: 259 us -> 252 us (0.973)
  waiting for transfers between devices: 68.3 us -> 59.2 us
  local copies, waits for them, and re-layouts: 18.9 us -> 21.6 us
    ppermute x1, waiting for transfers between devices: 5.38 us -> 0.01 us  [body(): got_b = lax.ppermute(give_b, 'xl', SWAP)]
    ppermute x1, waiting for transfers between devices: 3.77 us -> 0.01 us  [body(): got_1 = lax.ppermute(give_1, ('xl', 'xh'), DIAG)]
  transfers between devices with their start and end apart: 44 -> 44, of which waited for: 20 -> 18; matrix products, arithmetic and copies ran while one was open for 10% -> 10% of each run, Pallas kernels for 26% -> 27%
where the time goes in v4:
time: 252 us; the launch traced here: 251 us
  starting transfers between devices  68.8 us (27%)
  Pallas kernels  68.1 us (27%)
  waiting for transfers between devices  59.2 us (23%)
  local copies, waits for them, and re-layouts  21.6 us (9%)
  between operations  17.8 us (7%)
  other arithmetic  15.4 us (6%)
    ppermute x18, waiting for transfers between devices, shift(): return lax.ppermute(a, axis, [(i, (i + k) % 4) for i in range(4)])  34.6 us
    pallas_call x4, Pallas kernels, terms(): pl.pallas_call(kernel, grid_spec=pltpu.PrefetchScalarGridSpec(num_scalar_...  28.3 us
    ppermute x18, starting transfers between devices, shift(): return lax.ppermute(a, axis, [(i, (i + k) % 4) for i in range(4)])  22.1 us
    all_to_all x3, starting transfers between devices, spread(): return lax.all_to_all(copies, axes, split_axis=0, concat_axis=0, tiled=True)  16.7 us
    pallas_call x1, Pallas kernels, transposed_tokens(): pl.pallas_call(kernel, grid_spec=pltpu.PrefetchScalarGridSpec(num_scalar_...  12.1 us
    pallas_call x1, Pallas kernels, gradient_of_pieces(): pl.pallas_call(kernel, out_shape=(jax.ShapeDtypeStruct((n, 128, width), B...  11.9 us
    unnamed x85, local copies, waits for them, and re-layouts  10.6 us
    pallas_call x1, Pallas kernels, gradient(): pl.pallas_call(kernel, grid=(width // TILE,), out_shape=grad_shapes(width...  9.82 us
  transfers between devices with their start and end apart: 44, of which 18 were waited for; matrix products, arithmetic and copies ran while one was open for 10% of the time, Pallas kernels for 27%

profile of v4, /device:TPU:0, one launch (start us, length us, event | category | flops | bytes accessed | tf_op | source)
XLA Modules:
  0.0 251.0 jit_solution(3386298074707098414)
XLA Ops:
  13.0 8.1 %all-to-all-start = ((bf16[1,32,16,512]{3,1,0,2:T(8,128)(2,1)}), bf16[1,32,16,512]{3,1,0,2:T(8,128)(2,1)}, u32[]{:S(2)}, u32[]{:S(2)}) async-start(bf16[1,32,16,512]{3,1,0,2:T(8,128)(2,1)} %copy.24), calls=%async_computation | async-start | bytes 1048576 | tf_op jit(solution)/shard_map/all_to_all | solution.py:321
  21.8 3.0 %collective-permute-done.1 = f32[256]{0:T(256)S(1)} collective-permute-done((f32[256]{0:T(256)S(1)}, f32[256]{0:T(256)S(1)}, u32[]{:S(2)}, u32[]{:S(2)}) %collective-permute-start.1) | collective-permute-done | bytes 1056 | tf_op jit(solution)/shard_map/ppermute | solution.py:324
  24.8 7.6 %all-to-all-done = bf16[1,32,16,512]{3,1,0,2:T(8,128)(2,1)} async-done(((bf16[1,32,16,512]{3,1,0,2:T(8,128)(2,1)}), bf16[1,32,16,512]{3,1,0,2:T(8,128)(2,1)}, u32[]{:S(2)}, u32[]{:S(2)}) %all-to-all-start) | async-done | bytes 524320 | tf_op jit(solution)/shard_map/all_to_all | solution.py:321
  35.2 2.0 collective-permute-start.7
  39.8 2.1 collective-permute-start.10
  43.6 2.7 %collective-permute-start.9 = (bf16[16,32,512]{2,1,0:T(8,128)(2,1)}, bf16[16,32,512]{2,1,0:T(8,128)(2,1)S(1)}, u32[]{:S(2)}, u32[]{:S(2)}) collective-permute-start(bf16[16,32,512]{2,1,0:T(8,128)(2,1)} %bitcast.37.a_ref), channel_id=1, source_target_pairs={{0,2},{2,0},{1,3},{3,1},{4,6},{6,4},{5,7},{7,5},{8,10},{10,8},{9,1... | collective-permute-start | bytes 1572872 | tf_op jit(solution)/shard_map/ppermute | solution.py:334
  48.3 4.2 %collective-permute-done.5 = bf16[128,1024]{1,0:T(8,128)(2,1)S(1)} collective-permute-done((bf16[128,1024]{1,0:T(8,128)(2,1)S(1)}, bf16[128,1024]{1,0:T(8,128)(2,1)S(1)}, u32[]{:S(2)}, u32[]{:S(2)}) %collective-permute-start.5) | collective-permute-done | bytes 262176 | tf_op jit(solution)/shard_map/ppermute | solution.py:38
  52.8 9.0 %collective-permute-done.4 = bf16[128,1024]{1,0:T(8,128)(2,1)S(1)} collective-permute-done((bf16[128,1024]{1,0:T(8,128)(2,1)S(1)}, bf16[128,1024]{1,0:T(8,128)(2,1)S(1)}, u32[]{:S(2)}, u32[]{:S(2)}) %collective-permute-start.4) | collective-permute-done | bytes 262176 | tf_op jit(solution)/shard_map/ppermute | solution.py:38
  66.4 4.0 %collective-permute-done.13.refs_10_ = bf16[256,1024]{1,0:T(8,128)(2,1)S(1)} collective-permute-done((bf16[256,1024]{1,0:T(8,128)(2,1)S(1)}, bf16[256,1024]{1,0:T(8,128)(2,1)S(1)}, u32[]{:S(2)}, u32[]{:S(2)}) %collective-permute-start.13) | collective-permute-done | bytes 524320 | tf_op jit(solution)/shard_map/ppermute | solution.py:38
  71.2 5.6 %collective-permute-done.11.refs_2_ = bf16[256,1024]{1,0:T(8,128)(2,1)S(1)} collective-permute-done((bf16[256,1024]{1,0:T(8,128)(2,1)S(1)}, bf16[256,1024]{1,0:T(8,128)(2,1)S(1)}, u32[]{:S(2)}, u32[]{:S(2)}) %collective-permute-start.11) | collective-permute-done | bytes 524320 | tf_op jit(solution)/shard_map/ppermute | solution.py:38
  76.8 5.7 %collective-permute-done.12.refs_3_ = bf16[256,1024]{1,0:T(8,128)(2,1)S(1)} collective-permute-done((bf16[256,1024]{1,0:T(8,128)(2,1)}, bf16[256,1024]{1,0:T(8,128)(2,1)S(1)}, u32[]{:S(2)}, u32[]{:S(2)}) %collective-permute-start.12) | collective-permute-done | bytes 524320 | tf_op jit(solution)/shard_map/ppermute | solution.py:38
  88.7 3.2 %collective-permute-start.22 = (bf16[256,1024]{1,0:T(8,128)(2,1)}, bf16[256,1024]{1,0:T(8,128)(2,1)}, u32[]{:S(2)}, u32[]{:S(2)}) collective-permute-start(bf16[256,1024]{1,0:T(8,128)(2,1)} %copy-done.30), channel_id=1, source_target_pairs={{0,96},{32,0},{64,32},{96,64},{1,97},{33,1},{65,33},{97,65},{2,98}... | collective-permute-start | bytes 1572872 | tf_op jit(solution)/shard_map/ppermute | solution.py:38
  91.9 3.7 %collective-permute-start.18 = (bf16[256,1024]{1,0:T(8,128)(2,1)}, bf16[256,1024]{1,0:T(8,128)(2,1)}, u32[]{:S(2)}, u32[]{:S(2)}) collective-permute-start(bf16[256,1024]{1,0:T(8,128)(2,1)} %copy-done.32), channel_id=1, source_target_pairs={{0,24},{8,0},{16,8},{24,16},{1,25},{9,1},{17,9},{25,17},{2,26},{10... | collective-permute-start | bytes 1572872 | tf_op jit(solution)/shard_map/ppermute | solution.py:38
  95.6 12.1 %shard_map.92.xt_ref = bf16[512,4096]{1,0:T(8,128)(2,1)} custom-call(s32[3]{0:T(128)} %pad_add_fusion.where_ref.xl_ref, bf16[16,32,512]{2,1,0:T(8,128)(2,1)} %bitcast.37.a_ref, bf16[16,32,512]{2,1,0:T(8,128)(2,1)} %copy-done.21, bf16[16,32,512]{2,1,0:T(8,128)(2,1)} %copy-done.20, bf16[16,32,512]{2,1,0:T(8,128)(2,1)} %copy-done.19, ...), custom_call_target="tpu_custom_call" | custom-call | flops 20000000000 | bytes 1 | tf_op jit(solution)/shard_map/pallas_call | solution.py:80
  107.7 4.4 %collective-permute-done.25 = bf16[256,2048]{0,1:T(8,128)(2,1)S(1)} collective-permute-done((bf16[256,2048]{0,1:T(8,128)(2,1)}, bf16[256,2048]{0,1:T(8,128)(2,1)S(1)}, u32[]{:S(2)}, u32[]{:S(2)}) %collective-permute-start.25) | collective-permute-done | bytes 1048608 | tf_op jit(solution)/shard_map/ppermute | solution.py:342
  112.1 3.6 %collective-permute-start.20 = (bf16[256,1024]{1,0:T(8,128)(2,1)S(1)}, bf16[256,1024]{1,0:T(8,128)(2,1)}, u32[]{:S(2)}, u32[]{:S(2)}) collective-permute-start(bf16[256,1024]{1,0:T(8,128)(2,1)S(1)} %copy-done.14), channel_id=1, source_target_pairs={{0,24},{8,0},{16,8},{24,16},{1,25},{9,1},{17,9},{25,17},{2,26},{10... | collective-permute-start | bytes 1572872 | tf_op jit(solution)/shard_map/ppermute | solution.py:38
  115.7 1.8 fusion.w_ref
  117.5 3.0 %collective-permute-start.24 = (bf16[256,1024]{1,0:T(8,128)(2,1)S(1)}, bf16[256,1024]{1,0:T(8,128)(2,1)S(1)}, u32[]{:S(2)}, u32[]{:S(2)}) collective-permute-start(bf16[256,1024]{1,0:T(8,128)(2,1)S(1)} %copy-done.12), channel_id=1, source_target_pairs={{0,96},{32,0},{64,32},{96,64},{1,97},{33,1},{65,33},{97,65},{2,98}... | collective-permute-start | bytes 1572872 | tf_op jit(solution)/shard_map/ppermute | solution.py:38
  122.1 9.8 %shard_map.93 = (f32[256,1024]{1,0:T(8,128)}, f32[512,128]{1,0:T(8,128)}, f32[8,1024]{1,0:T(8,128)}, f32[256,512]{1,0:T(8,128)}, f32[256,512]{1,0:T(8,128)}) custom-call(s32[3]{0:T(128)} %pad_add_fusion.where_ref.xl_ref, bf16[512,4096]{1,0:T(8,128)(2,1)} %shard_map.92.xt_ref, bf16[4096,1024]{1,0:T(8,128)(2,1)} %bitcast.86), custom_call_target="tpu_custom_call" | custom-call | flops 20000000000 | bytes 1 | tf_op jit(solution)/shard_map/pallas_call | solution.py:188
  132.0 2.5 %collective-permute-done.23.refs_14_ = bf16[256,1024]{1,0:T(8,128)(2,1)S(1)} collective-permute-done((bf16[256,1024]{1,0:T(8,128)(2,1)}, bf16[256,1024]{1,0:T(8,128)(2,1)S(1)}, u32[]{:S(2)}, u32[]{:S(2)}) %collective-permute-start.23) | collective-permute-done | bytes 524320 | tf_op jit(solution)/shard_map/ppermute | solution.py:38
  136.0 11.9 %shard_map.94 = (bf16[32,128,1024]{2,1,0:T(8,128)(2,1)}, f32[256,1024]{1,0:T(8,128)}, f32[512,128]{1,0:T(8,128)}, f32[8,1024]{1,0:T(8,128)}, f32[256,512]{1,0:T(8,128)}, /*index=5*/f32[256,512]{1,0:T(8,128)}) custom-call(s32[3]{0:T(128)} %pad_add_fusion.where_ref.xl_ref, s32[32]{0:T(128)} %stack.184.index_ref, bf16[512,4096]{1,0:T(8,128)(2,1)} %shard_map.92.xt_ref, ...), custom_call_target="tpu_custom_call" | custom-call | flops 20000000000 | bytes 1 | tf_op jit(solution)/shard_map/pallas_call | solution.py:153
  154.1 7.1 %all-to-all-start.1 = ((f32[16,1,2048]{2,1,0:T(1,128)}), f32[16,1,2048]{2,1,0:T(1,128)S(1)}, u32[]{:S(2)}, u32[]{:S(2)}) async-start(f32[16,1,2048]{2,1,0:T(1,128)} %broadcast_in_dim.22), calls=%async_computation.1 | async-start | bytes 262144 | tf_op jit(solution)/shard_map/all_to_all | solution.py:30
  161.3 6.6 %shard_map.95 = f32[1024,512]{1,0:T(8,128)} custom-call(s32[3]{0:T(128)} %pad_add_fusion.where_ref.xl_ref, bf16[4096,1024]{1,0:T(8,128)(2,1)} %bitcast.91, bf16[4096,1024]{1,0:T(8,128)(2,1)} %bitcast.87, bf16[2048,512]{1,0:T(8,128)(2,1)} %fusion.w_ref), custom_call_target="tpu_custom_call" | custom-call | flops 20000000000 | bytes 1 | tf_op jit(solution)/shard_map/pallas_call | solution.py:239
  171.2 6.5 %shard_map.96 = f32[1024,512]{1,0:T(8,128)} custom-call(s32[3]{0:T(128)} %pad_add_fusion.where_ref.xl_ref, bf16[4096,1024]{1,0:T(8,128)(2,1)} %bitcast.92, bf16[4096,1024]{1,0:T(8,128)(2,1)} %bitcast.88, bf16[2048,512]{1,0:T(8,128)(2,1)} %fusion.w_ref), custom_call_target="tpu_custom_call" | custom-call | flops 20000000000 | bytes 1 | tf_op jit(solution)/shard_map/pallas_call | solution.py:239
  180.1 3.6 %all-to-all-start.2 = ((f32[8,4,256]{2,1,0:T(4,128)}), f32[8,4,256]{2,1,0:T(4,128)S(1)}, u32[]{:S(2)}, u32[]{:S(2)}) async-start(f32[8,4,256]{2,1,0:T(4,128)} %broadcast_in_dim.23), calls=%async_computation.2 | async-start | bytes 65536 | tf_op jit(solution)/shard_map/all_to_all | solution.py:30
  183.7 7.6 %shard_map.97 = (f32[256,512]{1,0:T(8,128)}, f32[256,512]{1,0:T(8,128)}, f32[512,256]{1,0:T(8,128)}, f32[512,256]{1,0:T(8,128)}) custom-call(s32[3]{0:T(128)} %pad_add_fusion.where_ref.xl_ref, bf16[4096,1024]{1,0:T(8,128)(2,1)} %bitcast.93, bf16[4096,1024]{1,0:T(8,128)(2,1)} %bitcast.89, bf16[2048,512]{1,0:T(8,128)(2,1)} %fusion.w_ref, ...), custom_call_target="tpu_custom_call" | custom-call | flops 20000000000 | bytes 1 | tf_op jit(solution)/shard_map/pallas_call | solution.py:239
  191.3 3.2 %collective-permute-start.33 = (f32[256,512]{1,0:T(8,128)}, f32[256,512]{1,0:T(8,128)S(1)}, u32[]{:S(2)}, u32[]{:S(2)}) collective-permute-start(f32[256,512]{1,0:T(8,128)} %get-tuple-element.143), channel_id=1, source_target_pairs={{0,6},{6,0},{2,4},{4,2},{1,7},{7,1},{3,5},{5,3},{8,14},{14,8},{10,... | collective-permute-start | bytes 1572872 | tf_op jit(solution)/shard_map/ppermute | solution.py:378
  196.0 7.6 %shard_map.98 = (f32[256,512]{1,0:T(8,128)}, f32[256,512]{1,0:T(8,128)}, f32[512,256]{1,0:T(8,128)}, f32[512,256]{1,0:T(8,128)}) custom-call(s32[3]{0:T(128)} %pad_add_fusion.where_ref.xl_ref, bf16[4096,1024]{1,0:T(8,128)(2,1)} %bitcast.94, bf16[4096,1024]{1,0:T(8,128)(2,1)} %bitcast.90, bf16[2048,512]{1,0:T(8,128)(2,1)} %fusion.w_ref, ...), custom_call_target="tpu_custom_call" | custom-call | flops 20000000000 | bytes 1 | tf_op jit(solution)/shard_map/pallas_call | solution.py:239
  207.0 6.0 %all-to-all-start.3 = ((f32[16,1,128]{2,1,0:T(1,128)}), f32[16,1,128]{2,1,0:T(1,128)S(1)}, u32[]{:S(2)}, u32[]{:S(2)}) async-start(f32[16,1,128]{2,1,0:T(1,128)} %broadcast_in_dim.47), calls=%async_computation.3 | async-start | bytes 16384 | tf_op jit(solution)/shard_map/all_to_all | solution.py:30
  216.5 3.9 %all-to-all-done.3 = f32[16,1,128]{2,1,0:T(1,128)S(1)} async-done(((f32[16,1,128]{2,1,0:T(1,128)}), f32[16,1,128]{2,1,0:T(1,128)S(1)}, u32[]{:S(2)}, u32[]{:S(2)}) %all-to-all-start.3) | async-done | bytes 8224 | tf_op jit(solution)/shard_map/all_to_all | solution.py:30
  228.4 2.1 collective-permute-start.38
  231.1 6.0 %shard_map.99 = f32[256,4096]{1,0:T(8,128)} custom-call(s32[3]{0:T(128)} %pad_add_fusion.where_ref.xl_ref, f32[1]{0:T(128)} %bitcast.58.scale_ref, f32[256,1]{1,0:T(8,128)} %copy.28.row_ref, f32[1,4096]{1,0:T(1,128)} %bitcast.76, f32[256,1024]{1,0:T(8,128)} %get-tuple-element.121.refs_0_, f32[256,1024]{1,0:T(8,128)} %get-tuple-element.131.refs_1_, ...), custom_call_target="tpu_custom_call" | custom-call | flops 20000000000 | bytes 1 | tf_op jit(solution)/shard_map/pallas_call | solution.py:283
  (200 shorter events, 62.8 us)
Async XLA Ops:
  10.1 22.3 %collective-permute-start = (bf16[128,2048]{1,0:T(8,128)(2,1)S(1)}, bf16[128,2048]{1,0:T(8,128)(2,1)S(1)}, u32[]{:S(2)}, u32[]{:S(2)}) collective-permute-start(bf16[128,2048]{1,0:T(8,128)(2,1)S(1)} %get-tuple-element.82), channel_id=1, source_target_pairs={{0,4},{4,0},{1,5},{5,1},{2,6},{6,2},{3,7},{7,3},{8,12},{12,8},{9,1... | collective-permute-start | bytes 1572872 | tf_op jit(solution)/shard_map/ppermute | solution.py:319
  13.0 19.4 %all-to-all-start = ((bf16[1,32,16,512]{3,1,0,2:T(8,128)(2,1)}), bf16[1,32,16,512]{3,1,0,2:T(8,128)(2,1)}, u32[]{:S(2)}, u32[]{:S(2)}) async-start(bf16[1,32,16,512]{3,1,0,2:T(8,128)(2,1)} %copy.24), calls=%async_computation | async-start | bytes 1048576 | tf_op jit(solution)/shard_map/all_to_all | solution.py:321
  21.1 100.9 %all-gather.2.cloned.1.call-start = ((), (), s32[]{:S(2)}) async-start(), calls=%async_computation.4 | async-start | bytes 8912896 | tf_op jit(solution)/shard_map/all_gather | solution.py:329
  37.2 15.3 %collective-permute-start.2 = (bf16[128,1024]{1,0:T(8,128)(2,1)S(1)}, bf16[128,1024]{1,0:T(8,128)(2,1)S(1)}, u32[]{:S(2)}, u32[]{:S(2)}) collective-permute-start(bf16[128,1024]{1,0:T(8,128)(2,1)S(1)} %get-tuple-element.173), channel_id=1, source_target_pairs={{0,32},{32,64},{64,96},{96,0},{1,33},{33,65},{65,97},{97,1},{2,34}... | collective-permute-start | bytes 786440 | tf_op jit(solution)/shard_map/ppermute | solution.py:38
  38.1 14.4 %collective-permute-start.5 = (bf16[128,1024]{1,0:T(8,128)(2,1)S(1)}, bf16[128,1024]{1,0:T(8,128)(2,1)S(1)}, u32[]{:S(2)}, u32[]{:S(2)}) collective-permute-start(bf16[128,1024]{1,0:T(8,128)(2,1)S(1)} %get-tuple-element.175), channel_id=1, source_target_pairs={{0,8},{8,16},{16,24},{24,0},{1,9},{9,17},{17,25},{25,1},{2,10},{10... | collective-permute-start | bytes 786440 | tf_op jit(solution)/shard_map/ppermute | solution.py:38
  39.8 23.3 %collective-permute-start.10 = (bf16[16,32,512]{2,1,0:T(8,128)(2,1)}, bf16[16,32,512]{2,1,0:T(8,128)(2,1)S(1)}, u32[]{:S(2)}, u32[]{:S(2)}) collective-permute-start(bf16[16,32,512]{2,1,0:T(8,128)(2,1)} %bitcast.37.a_ref), channel_id=1, source_target_pairs={{0,6},{6,0},{2,4},{4,2},{1,7},{7,1},{3,5},{5,3},{8,14},{14,8},{10,... | collective-permute-start | bytes 1572872 | tf_op jit(solution)/shard_map/ppermute | solution.py:334
  43.6 21.1 %collective-permute-start.9 = (bf16[16,32,512]{2,1,0:T(8,128)(2,1)}, bf16[16,32,512]{2,1,0:T(8,128)(2,1)S(1)}, u32[]{:S(2)}, u32[]{:S(2)}) collective-permute-start(bf16[16,32,512]{2,1,0:T(8,128)(2,1)} %bitcast.37.a_ref), channel_id=1, source_target_pairs={{0,2},{2,0},{1,3},{3,1},{4,6},{6,4},{5,7},{7,5},{8,10},{10,8},{9,1... | collective-permute-start | bytes 1572872 | tf_op jit(solution)/shard_map/ppermute | solution.py:334
  47.1 14.7 %collective-permute-start.4 = (bf16[128,1024]{1,0:T(8,128)(2,1)S(1)}, bf16[128,1024]{1,0:T(8,128)(2,1)S(1)}, u32[]{:S(2)}, u32[]{:S(2)}) collective-permute-start(bf16[128,1024]{1,0:T(8,128)(2,1)S(1)} %get-tuple-element.173), channel_id=1, source_target_pairs={{0,64},{32,96},{64,0},{96,32},{1,65},{33,97},{65,1},{97,33},{2,66}... | collective-permute-start | bytes 786440 | tf_op jit(solution)/shard_map/ppermute | solution.py:38
  52.5 17.8 %collective-permute-start.13 = (bf16[256,1024]{1,0:T(8,128)(2,1)S(1)}, bf16[256,1024]{1,0:T(8,128)(2,1)S(1)}, u32[]{:S(2)}, u32[]{:S(2)}) collective-permute-start(bf16[256,1024]{1,0:T(8,128)(2,1)S(1)} %pad_maximum_fusion.2.refs_8_), channel_id=1, source_target_pairs={{0,32},{32,64},{64,96},{96,0},{1,33},{33,65},{65,97},{97,1},{2,34}... | collective-permute-start | bytes 1572872 | tf_op jit(solution)/shard_map/ppermute | solution.py:38
  64.7 17.9 %collective-permute-start.12 = (bf16[256,1024]{1,0:T(8,128)(2,1)}, bf16[256,1024]{1,0:T(8,128)(2,1)S(1)}, u32[]{:S(2)}, u32[]{:S(2)}) collective-permute-start(bf16[256,1024]{1,0:T(8,128)(2,1)} %constant_dynamic-update-slice_fusion.refs_1_), channel_id=1, source_target_pairs={{0,24},{8,0},{16,8},{24,16},{1,25},{9,1},{17,9},{25,17},{2,26},{10... | collective-permute-start | bytes 1572872 | tf_op jit(solution)/shard_map/ppermute | solution.py:38
  86.8 25.3 %collective-permute-start.25 = (bf16[256,2048]{0,1:T(8,128)(2,1)}, bf16[256,2048]{0,1:T(8,128)(2,1)S(1)}, u32[]{:S(2)}, u32[]{:S(2)}) collective-permute-start(bf16[256,2048]{0,1:T(8,128)(2,1)} %copy.31), channel_id=1, source_target_pairs={{0,4},{4,0},{1,5},{5,1},{2,6},{6,2},{3,7},{7,3},{8,12},{12,8},{9,1... | collective-permute-start | bytes 3145736 | tf_op jit(solution)/shard_map/ppermute | solution.py:342
  88.7 28.9 %collective-permute-start.21 = (bf16[256,1024]{1,0:T(8,128)(2,1)}, bf16[256,1024]{1,0:T(8,128)(2,1)}, u32[]{:S(2)}, u32[]{:S(2)}) collective-permute-start(bf16[256,1024]{1,0:T(8,128)(2,1)} %copy-done.29), channel_id=1, source_target_pairs={{0,32},{32,64},{64,96},{96,0},{1,33},{33,65},{65,97},{97,1},{2,34}... | collective-permute-start | bytes 1572872 | tf_op jit(solution)/shard_map/ppermute | solution.py:38
  88.7 28.9 %collective-permute-start.22 = (bf16[256,1024]{1,0:T(8,128)(2,1)}, bf16[256,1024]{1,0:T(8,128)(2,1)}, u32[]{:S(2)}, u32[]{:S(2)}) collective-permute-start(bf16[256,1024]{1,0:T(8,128)(2,1)} %copy-done.30), channel_id=1, source_target_pairs={{0,96},{32,0},{64,32},{96,64},{1,97},{33,1},{65,33},{97,65},{2,98}... | collective-permute-start | bytes 1572872 | tf_op jit(solution)/shard_map/ppermute | solution.py:38
  91.9 28.6 %collective-permute-start.17 = (bf16[256,1024]{1,0:T(8,128)(2,1)}, bf16[256,1024]{1,0:T(8,128)(2,1)}, u32[]{:S(2)}, u32[]{:S(2)}) collective-permute-start(bf16[256,1024]{1,0:T(8,128)(2,1)} %copy-done.31), channel_id=1, source_target_pairs={{0,8},{8,16},{16,24},{24,0},{1,9},{9,17},{17,25},{25,1},{2,10},{10... | collective-permute-start | bytes 1572872 | tf_op jit(solution)/shard_map/ppermute | solution.py:38
  91.9 40.0 %collective-permute-start.18 = (bf16[256,1024]{1,0:T(8,128)(2,1)}, bf16[256,1024]{1,0:T(8,128)(2,1)}, u32[]{:S(2)}, u32[]{:S(2)}) collective-permute-start(bf16[256,1024]{1,0:T(8,128)(2,1)} %copy-done.32), channel_id=1, source_target_pairs={{0,24},{8,0},{16,8},{24,16},{1,25},{9,1},{17,9},{25,17},{2,26},{10... | collective-permute-start | bytes 1572872 | tf_op jit(solution)/shard_map/ppermute | solution.py:38
  112.1 19.8 %collective-permute-start.20 = (bf16[256,1024]{1,0:T(8,128)(2,1)S(1)}, bf16[256,1024]{1,0:T(8,128)(2,1)}, u32[]{:S(2)}, u32[]{:S(2)}) collective-permute-start(bf16[256,1024]{1,0:T(8,128)(2,1)S(1)} %copy-done.14), channel_id=1, source_target_pairs={{0,24},{8,0},{16,8},{24,16},{1,25},{9,1},{17,9},{25,17},{2,26},{10... | collective-permute-start | bytes 1572872 | tf_op jit(solution)/shard_map/ppermute | solution.py:38
  117.5 14.4 %collective-permute-start.19 = (bf16[256,1024]{1,0:T(8,128)(2,1)}, bf16[256,1024]{1,0:T(8,128)(2,1)S(1)}, u32[]{:S(2)}, u32[]{:S(2)}) collective-permute-start(bf16[256,1024]{1,0:T(8,128)(2,1)} %constant_dynamic-update-slice_fusion.refs_1_), channel_id=1, source_target_pairs={{0,8},{8,16},{16,24},{24,0},{1,9},{9,17},{17,25},{25,1},{2,10},{10... | collective-permute-start | bytes 1572872 | tf_op jit(solution)/shard_map/ppermute | solution.py:38
  117.5 14.4 %collective-permute-start.24 = (bf16[256,1024]{1,0:T(8,128)(2,1)S(1)}, bf16[256,1024]{1,0:T(8,128)(2,1)S(1)}, u32[]{:S(2)}, u32[]{:S(2)}) collective-permute-start(bf16[256,1024]{1,0:T(8,128)(2,1)S(1)} %copy-done.12), channel_id=1, source_target_pairs={{0,96},{32,0},{64,32},{96,64},{1,97},{33,1},{65,33},{97,65},{2,98}... | collective-permute-start | bytes 1572872 | tf_op jit(solution)/shard_map/ppermute | solution.py:38
  120.5 14.0 %collective-permute-start.23 = (bf16[256,1024]{1,0:T(8,128)(2,1)}, bf16[256,1024]{1,0:T(8,128)(2,1)S(1)}, u32[]{:S(2)}, u32[]{:S(2)}) collective-permute-start(bf16[256,1024]{1,0:T(8,128)(2,1)} %constant_dynamic-update-slice_fusion.2.refs_9_), channel_id=1, source_target_pairs={{0,32},{32,64},{64,96},{96,0},{1,33},{33,65},{65,97},{97,1},{2,34}... | collective-permute-start | bytes 1572872 | tf_op jit(solution)/shard_map/ppermute | solution.py:38
  135.3 18.0 %collective-permute-start.26 = (f32[256,512]{1,0:T(8,128)}, f32[256,512]{1,0:T(8,128)S(1)}, u32[]{:S(2)}, u32[]{:S(2)}) collective-permute-start(f32[256,512]{1,0:T(8,128)} %get-tuple-element.124), channel_id=1, source_target_pairs={{0,4},{4,0},{1,5},{5,1},{2,6},{6,2},{3,7},{7,3},{8,12},{12,8},{9,1... | collective-permute-start | bytes 1572872 | tf_op jit(solution)/shard_map/ppermute | solution.py:347
  147.9 21.3 %collective-permute-start.27 = (f32[256,512]{1,0:T(8,128)}, f32[256,512]{1,0:T(8,128)S(1)}, u32[]{:S(2)}, u32[]{:S(2)}) collective-permute-start(f32[256,512]{1,0:T(8,128)} %get-tuple-element.128), channel_id=1, source_target_pairs={{0,4},{4,0},{1,5},{5,1},{2,6},{6,2},{3,7},{7,3},{8,12},{12,8},{9,1... | collective-permute-start | bytes 1572872 | tf_op jit(solution)/shard_map/ppermute | solution.py:350
  149.4 34.3 %collective-permute-start.29 = (f32[256,512]{1,0:T(8,128)}, f32[256,512]{1,0:T(8,128)S(1)}, u32[]{:S(2)}, u32[]{:S(2)}) collective-permute-start(f32[256,512]{1,0:T(8,128)} %get-tuple-element.132), channel_id=1, source_target_pairs={{0,4},{4,0},{1,5},{5,1},{2,6},{6,2},{3,7},{7,3},{8,12},{12,8},{9,1... | collective-permute-start | bytes 1572872 | tf_op jit(solution)/shard_map/ppermute | solution.py:350
  150.0 53.5 %collective-permute-start.30 = (f32[256,512]{1,0:T(8,128)S(1)}, f32[256,512]{1,0:T(8,128)}, u32[]{:S(2)}, u32[]{:S(2)}) collective-permute-start(f32[256,512]{1,0:T(8,128)S(1)} %copy-done.15), channel_id=1, source_target_pairs={{0,4},{4,0},{1,5},{5,1},{2,6},{6,2},{3,7},{7,3},{8,12},{12,8},{9,1... | collective-permute-start | bytes 1572872 | tf_op jit(solution)/shard_map/ppermute | solution.py:347
  154.1 14.9 %all-to-all-start.1 = ((f32[16,1,2048]{2,1,0:T(1,128)}), f32[16,1,2048]{2,1,0:T(1,128)S(1)}, u32[]{:S(2)}, u32[]{:S(2)}) async-start(f32[16,1,2048]{2,1,0:T(1,128)} %broadcast_in_dim.22), calls=%async_computation.1 | async-start | bytes 262144 | tf_op jit(solution)/shard_map/all_to_all | solution.py:30
  167.8 15.9 %collective-permute-start.28 = (f32[1024,512]{1,0:T(8,128)}, f32[1024,512]{1,0:T(8,128)}, u32[]{:S(2)}, u32[]{:S(2)}) collective-permute-start(f32[1024,512]{1,0:T(8,128)} %shard_map.95), channel_id=1, source_target_pairs={{0,1},{1,0},{2,3},{3,2},{4,5},{5,4},{6,7},{7,6},{8,9},{9,8},{10,11... | collective-permute-start | bytes 6291464 | tf_op jit(solution)/shard_map/ppermute | solution.py:355
  170.0 46.5 %collective-permute-start.32 = (f32[2048]{0:T(1024)S(1)}, f32[2048]{0:T(1024)S(1)}, u32[]{:S(2)}, u32[]{:S(2)}) collective-permute-start(f32[2048]{0:T(1024)S(1)} %get-tuple-element.164), channel_id=1, source_target_pairs={{0,4},{4,0},{1,5},{5,1},{2,6},{6,2},{3,7},{7,3},{8,12},{12,8},{9,1... | collective-permute-start | bytes 24584 | tf_op jit(solution)/shard_map/ppermute | solution.py:394
  177.7 17.1 %collective-permute-start.31 = (f32[1024,512]{1,0:T(8,128)}, f32[1024,512]{1,0:T(8,128)}, u32[]{:S(2)}, u32[]{:S(2)}) collective-permute-start(f32[1024,512]{1,0:T(8,128)} %shard_map.96), channel_id=1, source_target_pairs={{0,1},{1,0},{2,3},{3,2},{4,5},{5,4},{6,7},{7,6},{8,9},{9,8},{10,11... | collective-permute-start | bytes 6291464 | tf_op jit(solution)/shard_map/ppermute | solution.py:361
  180.1 23.5 %all-to-all-start.2 = ((f32[8,4,256]{2,1,0:T(4,128)}), f32[8,4,256]{2,1,0:T(4,128)S(1)}, u32[]{:S(2)}, u32[]{:S(2)}) async-start(f32[8,4,256]{2,1,0:T(4,128)} %broadcast_in_dim.23), calls=%async_computation.2 | async-start | bytes 65536 | tf_op jit(solution)/shard_map/all_to_all | solution.py:30
  191.3 29.1 %collective-permute-start.33 = (f32[256,512]{1,0:T(8,128)}, f32[256,512]{1,0:T(8,128)S(1)}, u32[]{:S(2)}, u32[]{:S(2)}) collective-permute-start(f32[256,512]{1,0:T(8,128)} %get-tuple-element.143), channel_id=1, source_target_pairs={{0,6},{6,0},{2,4},{4,2},{1,7},{7,1},{3,5},{5,3},{8,14},{14,8},{10,... | collective-permute-start | bytes 1572872 | tf_op jit(solution)/shard_map/ppermute | solution.py:378
  194.5 25.9 %collective-permute-start.34 = (f32[512,256]{1,0:T(8,128)}, f32[512,256]{1,0:T(8,128)S(1)}, u32[]{:S(2)}, u32[]{:S(2)}) collective-permute-start(f32[512,256]{1,0:T(8,128)} %get-tuple-element.144), channel_id=1, source_target_pairs={{0,4},{4,0},{1,5},{5,1},{2,6},{6,2},{3,7},{7,3},{8,12},{12,8},{9,1... | collective-permute-start | bytes 1572872 | tf_op jit(solution)/shard_map/ppermute | solution.py:379
  194.8 25.7 %collective-permute-start.35 = (f32[256,512]{1,0:T(8,128)}, f32[256,512]{1,0:T(8,128)}, u32[]{:S(2)}, u32[]{:S(2)}) collective-permute-start(f32[256,512]{1,0:T(8,128)} %get-tuple-element.145), channel_id=1, source_target_pairs={{0,6},{6,0},{2,4},{4,2},{1,7},{7,1},{3,5},{5,3},{8,14},{14,8},{10,... | collective-permute-start | bytes 1572872 | tf_op jit(solution)/shard_map/ppermute | solution.py:393
  203.6 16.9 %collective-permute-start.36 = (f32[512,256]{1,0:T(8,128)}, f32[512,256]{1,0:T(8,128)S(1)}, u32[]{:S(2)}, u32[]{:S(2)}) collective-permute-start(f32[512,256]{1,0:T(8,128)} %get-tuple-element.146), channel_id=1, source_target_pairs={{0,4},{4,0},{1,5},{5,1},{2,6},{6,2},{3,7},{7,3},{8,12},{12,8},{9,1... | collective-permute-start | bytes 1572872 | tf_op jit(solution)/shard_map/ppermute | solution.py:395
  (51 other events, 529.8 us)
Sparse Core Ops, SparseCore 0:
  33.5 88.5 all-gather.1

commit v5 on v4

--- a/solution.py
+++ b/solution.py
@@ -393,7 +393,7 @@
     got_2 = lax.ppermute(give_2, ("xl", "xh"), DIAG)
     col_other = lax.ppermute(col_half, "xl", SWAP)
     got_b = lax.ppermute(give_b, "xl", SWAP)
-    totals, col_other, got_1, got_far, got_2, got_b = after((totals, col_other, got_1, got_far, got_2, got_b))
+    totals, col_other, got_1, got_far, got_2 = after((totals, col_other, got_1, got_far, got_2))
     totals = jnp.sum(totals, 0)
     last_b = lax.ppermute(far_keep + got_far, ("xl", "xh"), DIAG)
     keep_a, got_a = jnp.concatenate([keep_1, keep_2]), jnp.concatenate([got_1, got_2])

time: 252 us -> 253 us (level)
  transfers between devices with their start and end apart: 44 -> 44, of which waited for: 18 -> 18; matrix products, arithmetic and copies ran while one was open for 10% -> 11% of each run, Pallas kernels for 27% -> 27%
where the time goes in v5:
time: 253 us; the launch traced here: 252 us
  starting transfers between devices  68.8 us (27%)
  Pallas kernels  68.1 us (27%)
  waiting for transfers between devices  58.6 us (23%)
  local copies, waits for them, and re-layouts  22.7 us (9%)
  between operations  17.8 us (7%)
  other arithmetic  15.6 us (6%)
    ppermute x18, waiting for transfers between devices, shift(): return lax.ppermute(a, axis, [(i, (i + k) % 4) for i in range(4)])  34.6 us
    pallas_call x4, Pallas kernels, terms(): pl.pallas_call(kernel, grid_spec=pltpu.PrefetchScalarGridSpec(num_scalar_...  28.3 us
    ppermute x18, starting transfers between devices, shift(): return lax.ppermute(a, axis, [(i, (i + k) % 4) for i in range(4)])  22.1 us
    all_to_all x3, starting transfers between devices, spread(): return lax.all_to_all(copies, axes, split_axis=0, concat_axis=0, tiled=True)  16.9 us
    pallas_call x1, Pallas kernels, transposed_tokens(): pl.pallas_call(kernel, grid_spec=pltpu.PrefetchScalarGridSpec(num_scalar_...  12.1 us
    pallas_call x1, Pallas kernels, gradient_of_pieces(): pl.pallas_call(kernel, out_shape=(jax.ShapeDtypeStruct((n, 128, width), B...  11.9 us
    unnamed x85, local copies, waits for them, and re-layouts  11.7 us
    pallas_call x1, Pallas kernels, gradient(): pl.pallas_call(kernel, grid=(width // TILE,), out_shape=grad_shapes(width...  9.82 us
  transfers between devices with their start and end apart: 44, of which 18 were waited for; matrix products, arithmetic and copies ran while one was open for 11% of the time, Pallas kernels for 27%

profile of v5, /device:TPU:0, one launch (start us, length us, event | category | flops | bytes accessed | tf_op | source)
XLA Modules:
  0.0 251.7 jit_solution(720008519520302138)
XLA Ops:
  13.0 8.1 %all-to-all-start = ((bf16[1,32,16,512]{3,1,0,2:T(8,128)(2,1)}), bf16[1,32,16,512]{3,1,0,2:T(8,128)(2,1)}, u32[]{:S(2)}, u32[]{:S(2)}) async-start(bf16[1,32,16,512]{3,1,0,2:T(8,128)(2,1)} %copy.24), calls=%async_computation | async-start | bytes 1048576 | tf_op jit(solution)/shard_map/all_to_all | solution.py:321
  21.8 3.0 %collective-permute-done.1 = f32[256]{0:T(256)S(1)} collective-permute-done((f32[256]{0:T(256)S(1)}, f32[256]{0:T(256)S(1)}, u32[]{:S(2)}, u32[]{:S(2)}) %collective-permute-start.1) | collective-permute-done | bytes 1056 | tf_op jit(solution)/shard_map/ppermute | solution.py:324
  24.8 7.6 %all-to-all-done = bf16[1,32,16,512]{3,1,0,2:T(8,128)(2,1)} async-done(((bf16[1,32,16,512]{3,1,0,2:T(8,128)(2,1)}), bf16[1,32,16,512]{3,1,0,2:T(8,128)(2,1)}, u32[]{:S(2)}, u32[]{:S(2)}) %all-to-all-start) | async-done | bytes 524320 | tf_op jit(solution)/shard_map/all_to_all | solution.py:321
  35.2 2.0 collective-permute-start.7
  39.8 2.1 collective-permute-start.10
  43.6 2.7 %collective-permute-start.9 = (bf16[16,32,512]{2,1,0:T(8,128)(2,1)}, bf16[16,32,512]{2,1,0:T(8,128)(2,1)S(1)}, u32[]{:S(2)}, u32[]{:S(2)}) collective-permute-start(bf16[16,32,512]{2,1,0:T(8,128)(2,1)} %bitcast.37.a_ref), channel_id=1, source_target_pairs={{0,2},{2,0},{1,3},{3,1},{4,6},{6,4},{5,7},{7,5},{8,10},{10,8},{9,1... | collective-permute-start | bytes 1572872 | tf_op jit(solution)/shard_map/ppermute | solution.py:334
  48.3 4.2 %collective-permute-done.5 = bf16[128,1024]{1,0:T(8,128)(2,1)S(1)} collective-permute-done((bf16[128,1024]{1,0:T(8,128)(2,1)S(1)}, bf16[128,1024]{1,0:T(8,128)(2,1)S(1)}, u32[]{:S(2)}, u32[]{:S(2)}) %collective-permute-start.5) | collective-permute-done | bytes 262176 | tf_op jit(solution)/shard_map/ppermute | solution.py:38
  52.8 9.0 %collective-permute-done.4 = bf16[128,1024]{1,0:T(8,128)(2,1)S(1)} collective-permute-done((bf16[128,1024]{1,0:T(8,128)(2,1)S(1)}, bf16[128,1024]{1,0:T(8,128)(2,1)S(1)}, u32[]{:S(2)}, u32[]{:S(2)}) %collective-permute-start.4) | collective-permute-done | bytes 262176 | tf_op jit(solution)/shard_map/ppermute | solution.py:38
  66.4 4.0 %collective-permute-done.13.refs_10_ = bf16[256,1024]{1,0:T(8,128)(2,1)S(1)} collective-permute-done((bf16[256,1024]{1,0:T(8,128)(2,1)S(1)}, bf16[256,1024]{1,0:T(8,128)(2,1)S(1)}, u32[]{:S(2)}, u32[]{:S(2)}) %collective-permute-start.13) | collective-permute-done | bytes 524320 | tf_op jit(solution)/shard_map/ppermute | solution.py:38
  71.2 5.6 %collective-permute-done.11.refs_2_ = bf16[256,1024]{1,0:T(8,128)(2,1)S(1)} collective-permute-done((bf16[256,1024]{1,0:T(8,128)(2,1)S(1)}, bf16[256,1024]{1,0:T(8,128)(2,1)S(1)}, u32[]{:S(2)}, u32[]{:S(2)}) %collective-permute-start.11) | collective-permute-done | bytes 524320 | tf_op jit(solution)/shard_map/ppermute | solution.py:38
  76.8 5.7 %collective-permute-done.12.refs_3_ = bf16[256,1024]{1,0:T(8,128)(2,1)S(1)} collective-permute-done((bf16[256,1024]{1,0:T(8,128)(2,1)}, bf16[256,1024]{1,0:T(8,128)(2,1)S(1)}, u32[]{:S(2)}, u32[]{:S(2)}) %collective-permute-start.12) | collective-permute-done | bytes 524320 | tf_op jit(solution)/shard_map/ppermute | solution.py:38
  88.7 3.2 %collective-permute-start.22 = (bf16[256,1024]{1,0:T(8,128)(2,1)}, bf16[256,1024]{1,0:T(8,128)(2,1)}, u32[]{:S(2)}, u32[]{:S(2)}) collective-permute-start(bf16[256,1024]{1,0:T(8,128)(2,1)} %copy-done.30), channel_id=1, source_target_pairs={{0,96},{32,0},{64,32},{96,64},{1,97},{33,1},{65,33},{97,65},{2,98}... | collective-permute-start | bytes 1572872 | tf_op jit(solution)/shard_map/ppermute | solution.py:38
  91.9 3.7 %collective-permute-start.18 = (bf16[256,1024]{1,0:T(8,128)(2,1)}, bf16[256,1024]{1,0:T(8,128)(2,1)}, u32[]{:S(2)}, u32[]{:S(2)}) collective-permute-start(bf16[256,1024]{1,0:T(8,128)(2,1)} %copy-done.32), channel_id=1, source_target_pairs={{0,24},{8,0},{16,8},{24,16},{1,25},{9,1},{17,9},{25,17},{2,26},{10... | collective-permute-start | bytes 1572872 | tf_op jit(solution)/shard_map/ppermute | solution.py:38
  95.6 12.1 %shard_map.92.xt_ref = bf16[512,4096]{1,0:T(8,128)(2,1)} custom-call(s32[3]{0:T(128)} %pad_add_fusion.where_ref.xl_ref, bf16[16,32,512]{2,1,0:T(8,128)(2,1)} %bitcast.37.a_ref, bf16[16,32,512]{2,1,0:T(8,128)(2,1)} %copy-done.21, bf16[16,32,512]{2,1,0:T(8,128)(2,1)} %copy-done.20, bf16[16,32,512]{2,1,0:T(8,128)(2,1)} %copy-done.19, ...), custom_call_target="tpu_custom_call" | custom-call | flops 20000000000 | bytes 1 | tf_op jit(solution)/shard_map/pallas_call | solution.py:80
  107.7 4.4 %collective-permute-done.25 = bf16[256,2048]{0,1:T(8,128)(2,1)S(1)} collective-permute-done((bf16[256,2048]{0,1:T(8,128)(2,1)}, bf16[256,2048]{0,1:T(8,128)(2,1)S(1)}, u32[]{:S(2)}, u32[]{:S(2)}) %collective-permute-start.25) | collective-permute-done | bytes 1048608 | tf_op jit(solution)/shard_map/ppermute | solution.py:342
  112.1 3.6 %collective-permute-start.20 = (bf16[256,1024]{1,0:T(8,128)(2,1)S(1)}, bf16[256,1024]{1,0:T(8,128)(2,1)}, u32[]{:S(2)}, u32[]{:S(2)}) collective-permute-start(bf16[256,1024]{1,0:T(8,128)(2,1)S(1)} %copy-done.12), channel_id=1, source_target_pairs={{0,24},{8,0},{16,8},{24,16},{1,25},{9,1},{17,9},{25,17},{2,26},{10... | collective-permute-start | bytes 1572872 | tf_op jit(solution)/shard_map/ppermute | solution.py:38
  117.5 3.0 %collective-permute-start.24 = (bf16[256,1024]{1,0:T(8,128)(2,1)S(1)}, bf16[256,1024]{1,0:T(8,128)(2,1)S(1)}, u32[]{:S(2)}, u32[]{:S(2)}) collective-permute-start(bf16[256,1024]{1,0:T(8,128)(2,1)S(1)} %copy-done.10), channel_id=1, source_target_pairs={{0,96},{32,0},{64,32},{96,64},{1,97},{33,1},{65,33},{97,65},{2,98}... | collective-permute-start | bytes 1572872 | tf_op jit(solution)/shard_map/ppermute | solution.py:38
  122.1 9.8 %shard_map.93 = (f32[256,1024]{1,0:T(8,128)}, f32[512,128]{1,0:T(8,128)}, f32[8,1024]{1,0:T(8,128)}, f32[256,512]{1,0:T(8,128)}, f32[256,512]{1,0:T(8,128)}) custom-call(s32[3]{0:T(128)} %pad_add_fusion.where_ref.xl_ref, bf16[512,4096]{1,0:T(8,128)(2,1)} %shard_map.92.xt_ref, bf16[4096,1024]{1,0:T(8,128)(2,1)} %bitcast.86), custom_call_target="tpu_custom_call" | custom-call | flops 20000000000 | bytes 1 | tf_op jit(solution)/shard_map/pallas_call | solution.py:188
  132.0 2.5 %collective-permute-done.23.refs_14_ = bf16[256,1024]{1,0:T(8,128)(2,1)S(1)} collective-permute-done((bf16[256,1024]{1,0:T(8,128)(2,1)}, bf16[256,1024]{1,0:T(8,128)(2,1)S(1)}, u32[]{:S(2)}, u32[]{:S(2)}) %collective-permute-start.23) | collective-permute-done | bytes 524320 | tf_op jit(solution)/shard_map/ppermute | solution.py:38
  136.0 11.9 %shard_map.94 = (bf16[32,128,1024]{2,1,0:T(8,128)(2,1)}, f32[256,1024]{1,0:T(8,128)}, f32[512,128]{1,0:T(8,128)}, f32[8,1024]{1,0:T(8,128)}, f32[256,512]{1,0:T(8,128)}, /*index=5*/f32[256,512]{1,0:T(8,128)}) custom-call(s32[3]{0:T(128)} %pad_add_fusion.where_ref.xl_ref, s32[32]{0:T(128)} %stack.184.index_ref, bf16[512,4096]{1,0:T(8,128)(2,1)} %shard_map.92.xt_ref, ...), custom_call_target="tpu_custom_call" | custom-call | flops 20000000000 | bytes 1 | tf_op jit(solution)/shard_map/pallas_call | solution.py:153
  154.1 7.1 %all-to-all-start.1 = ((f32[16,1,2048]{2,1,0:T(1,128)}), f32[16,1,2048]{2,1,0:T(1,128)S(1)}, u32[]{:S(2)}, u32[]{:S(2)}) async-start(f32[16,1,2048]{2,1,0:T(1,128)} %broadcast_in_dim.22), calls=%async_computation.1 | async-start | bytes 262144 | tf_op jit(solution)/shard_map/all_to_all | solution.py:30
  161.3 6.6 %shard_map.95 = f32[1024,512]{1,0:T(8,128)} custom-call(s32[3]{0:T(128)} %pad_add_fusion.where_ref.xl_ref, bf16[4096,1024]{1,0:T(8,128)(2,1)} %bitcast.91, bf16[4096,1024]{1,0:T(8,128)(2,1)} %bitcast.87, bf16[2048,512]{1,0:T(8,128)(2,1)} %fusion.w_ref), custom_call_target="tpu_custom_call" | custom-call | flops 20000000000 | bytes 1 | tf_op jit(solution)/shard_map/pallas_call | solution.py:239
  171.2 6.5 %shard_map.96 = f32[1024,512]{1,0:T(8,128)} custom-call(s32[3]{0:T(128)} %pad_add_fusion.where_ref.xl_ref, bf16[4096,1024]{1,0:T(8,128)(2,1)} %bitcast.92, bf16[4096,1024]{1,0:T(8,128)(2,1)} %bitcast.88, bf16[2048,512]{1,0:T(8,128)(2,1)} %fusion.w_ref), custom_call_target="tpu_custom_call" | custom-call | flops 20000000000 | bytes 1 | tf_op jit(solution)/shard_map/pallas_call | solution.py:239
  180.1 3.6 %all-to-all-start.2 = ((f32[8,4,256]{2,1,0:T(4,128)}), f32[8,4,256]{2,1,0:T(4,128)S(1)}, u32[]{:S(2)}, u32[]{:S(2)}) async-start(f32[8,4,256]{2,1,0:T(4,128)} %broadcast_in_dim.23), calls=%async_computation.2 | async-start | bytes 65536 | tf_op jit(solution)/shard_map/all_to_all | solution.py:30
  183.7 7.6 %shard_map.97 = (f32[256,512]{1,0:T(8,128)}, f32[256,512]{1,0:T(8,128)}, f32[512,256]{1,0:T(8,128)}, f32[512,256]{1,0:T(8,128)}) custom-call(s32[3]{0:T(128)} %pad_add_fusion.where_ref.xl_ref, bf16[4096,1024]{1,0:T(8,128)(2,1)} %bitcast.93, bf16[4096,1024]{1,0:T(8,128)(2,1)} %bitcast.89, bf16[2048,512]{1,0:T(8,128)(2,1)} %fusion.w_ref, ...), custom_call_target="tpu_custom_call" | custom-call | flops 20000000000 | bytes 1 | tf_op jit(solution)/shard_map/pallas_call | solution.py:239
  191.3 3.2 %collective-permute-start.33 = (f32[256,512]{1,0:T(8,128)}, f32[256,512]{1,0:T(8,128)S(1)}, u32[]{:S(2)}, u32[]{:S(2)}) collective-permute-start(f32[256,512]{1,0:T(8,128)} %get-tuple-element.142), channel_id=1, source_target_pairs={{0,6},{6,0},{2,4},{4,2},{1,7},{7,1},{3,5},{5,3},{8,14},{14,8},{10,... | collective-permute-start | bytes 1572872 | tf_op jit(solution)/shard_map/ppermute | solution.py:378
  196.0 7.6 %shard_map.98 = (f32[256,512]{1,0:T(8,128)}, f32[256,512]{1,0:T(8,128)}, f32[512,256]{1,0:T(8,128)}, f32[512,256]{1,0:T(8,128)}) custom-call(s32[3]{0:T(128)} %pad_add_fusion.where_ref.xl_ref, bf16[4096,1024]{1,0:T(8,128)(2,1)} %bitcast.94, bf16[4096,1024]{1,0:T(8,128)(2,1)} %bitcast.90, bf16[2048,512]{1,0:T(8,128)(2,1)} %fusion.w_ref, ...), custom_call_target="tpu_custom_call" | custom-call | flops 20000000000 | bytes 1 | tf_op jit(solution)/shard_map/pallas_call | solution.py:239
  206.2 6.2 %all-to-all-start.3 = ((f32[16,1,128]{2,1,0:T(1,128)}), f32[16,1,128]{2,1,0:T(1,128)S(1)}, u32[]{:S(2)}, u32[]{:S(2)}) async-start(f32[16,1,128]{2,1,0:T(1,128)} %broadcast_in_dim.47), calls=%async_computation.3 | async-start | bytes 16384 | tf_op jit(solution)/shard_map/all_to_all | solution.py:30
  216.7 3.2 %all-to-all-done.3 = f32[16,1,128]{2,1,0:T(1,128)S(1)} async-done(((f32[16,1,128]{2,1,0:T(1,128)}), f32[16,1,128]{2,1,0:T(1,128)S(1)}, u32[]{:S(2)}, u32[]{:S(2)}) %all-to-all-start.3) | async-done | bytes 8224 | tf_op jit(solution)/shard_map/all_to_all | solution.py:30
  228.4 2.5 collective-permute-start.38
  231.5 6.0 %shard_map.99 = f32[256,4096]{1,0:T(8,128)} custom-call(s32[3]{0:T(128)} %pad_add_fusion.where_ref.xl_ref, f32[1]{0:T(128)} %bitcast.58.scale_ref, f32[256,1]{1,0:T(8,128)} %copy.28.row_ref, f32[1,4096]{1,0:T(1,128)} %bitcast.76, f32[256,1024]{1,0:T(8,128)} %get-tuple-element.120.refs_0_, f32[256,1024]{1,0:T(8,128)} %get-tuple-element.130.refs_1_, ...), custom_call_target="tpu_custom_call" | custom-call | flops 20000000000 | bytes 1 | tf_op jit(solution)/shard_map/pallas_call | solution.py:283
  238.2 2.2 collective-permute-done.36
  (200 shorter events, 63.2 us)
Async XLA Ops:
  10.1 22.3 %collective-permute-start = (bf16[128,2048]{1,0:T(8,128)(2,1)S(1)}, bf16[128,2048]{1,0:T(8,128)(2,1)S(1)}, u32[]{:S(2)}, u32[]{:S(2)}) collective-permute-start(bf16[128,2048]{1,0:T(8,128)(2,1)S(1)} %get-tuple-element.81), channel_id=1, source_target_pairs={{0,4},{4,0},{1,5},{5,1},{2,6},{6,2},{3,7},{7,3},{8,12},{12,8},{9,1... | collective-permute-start | bytes 1572872 | tf_op jit(solution)/shard_map/ppermute | solution.py:319
  13.0 19.4 %all-to-all-start = ((bf16[1,32,16,512]{3,1,0,2:T(8,128)(2,1)}), bf16[1,32,16,512]{3,1,0,2:T(8,128)(2,1)}, u32[]{:S(2)}, u32[]{:S(2)}) async-start(bf16[1,32,16,512]{3,1,0,2:T(8,128)(2,1)} %copy.24), calls=%async_computation | async-start | bytes 1048576 | tf_op jit(solution)/shard_map/all_to_all | solution.py:321
  21.1 100.9 %all-gather.2.cloned.1.call-start = ((), (), s32[]{:S(2)}) async-start(), calls=%async_computation.4 | async-start | bytes 8912896 | tf_op jit(solution)/shard_map/all_gather | solution.py:329
  37.2 15.3 %collective-permute-start.2 = (bf16[128,1024]{1,0:T(8,128)(2,1)S(1)}, bf16[128,1024]{1,0:T(8,128)(2,1)S(1)}, u32[]{:S(2)}, u32[]{:S(2)}) collective-permute-start(bf16[128,1024]{1,0:T(8,128)(2,1)S(1)} %get-tuple-element.171), channel_id=1, source_target_pairs={{0,32},{32,64},{64,96},{96,0},{1,33},{33,65},{65,97},{97,1},{2,34}... | collective-permute-start | bytes 786440 | tf_op jit(solution)/shard_map/ppermute | solution.py:38
  38.1 14.4 %collective-permute-start.5 = (bf16[128,1024]{1,0:T(8,128)(2,1)S(1)}, bf16[128,1024]{1,0:T(8,128)(2,1)S(1)}, u32[]{:S(2)}, u32[]{:S(2)}) collective-permute-start(bf16[128,1024]{1,0:T(8,128)(2,1)S(1)} %get-tuple-element.173), channel_id=1, source_target_pairs={{0,8},{8,16},{16,24},{24,0},{1,9},{9,17},{17,25},{25,1},{2,10},{10... | collective-permute-start | bytes 786440 | tf_op jit(solution)/shard_map/ppermute | solution.py:38
  39.8 23.3 %collective-permute-start.10 = (bf16[16,32,512]{2,1,0:T(8,128)(2,1)}, bf16[16,32,512]{2,1,0:T(8,128)(2,1)S(1)}, u32[]{:S(2)}, u32[]{:S(2)}) collective-permute-start(bf16[16,32,512]{2,1,0:T(8,128)(2,1)} %bitcast.37.a_ref), channel_id=1, source_target_pairs={{0,6},{6,0},{2,4},{4,2},{1,7},{7,1},{3,5},{5,3},{8,14},{14,8},{10,... | collective-permute-start | bytes 1572872 | tf_op jit(solution)/shard_map/ppermute | solution.py:334
  43.6 21.1 %collective-permute-start.9 = (bf16[16,32,512]{2,1,0:T(8,128)(2,1)}, bf16[16,32,512]{2,1,0:T(8,128)(2,1)S(1)}, u32[]{:S(2)}, u32[]{:S(2)}) collective-permute-start(bf16[16,32,512]{2,1,0:T(8,128)(2,1)} %bitcast.37.a_ref), channel_id=1, source_target_pairs={{0,2},{2,0},{1,3},{3,1},{4,6},{6,4},{5,7},{7,5},{8,10},{10,8},{9,1... | collective-permute-start | bytes 1572872 | tf_op jit(solution)/shard_map/ppermute | solution.py:334
  47.1 14.7 %collective-permute-start.4 = (bf16[128,1024]{1,0:T(8,128)(2,1)S(1)}, bf16[128,1024]{1,0:T(8,128)(2,1)S(1)}, u32[]{:S(2)}, u32[]{:S(2)}) collective-permute-start(bf16[128,1024]{1,0:T(8,128)(2,1)S(1)} %get-tuple-element.171), channel_id=1, source_target_pairs={{0,64},{32,96},{64,0},{96,32},{1,65},{33,97},{65,1},{97,33},{2,66}... | collective-permute-start | bytes 786440 | tf_op jit(solution)/shard_map/ppermute | solution.py:38
  52.5 17.8 %collective-permute-start.13 = (bf16[256,1024]{1,0:T(8,128)(2,1)S(1)}, bf16[256,1024]{1,0:T(8,128)(2,1)S(1)}, u32[]{:S(2)}, u32[]{:S(2)}) collective-permute-start(bf16[256,1024]{1,0:T(8,128)(2,1)S(1)} %pad_maximum_fusion.2.refs_8_), channel_id=1, source_target_pairs={{0,32},{32,64},{64,96},{96,0},{1,33},{33,65},{65,97},{97,1},{2,34}... | collective-permute-start | bytes 1572872 | tf_op jit(solution)/shard_map/ppermute | solution.py:38
  64.7 17.9 %collective-permute-start.12 = (bf16[256,1024]{1,0:T(8,128)(2,1)}, bf16[256,1024]{1,0:T(8,128)(2,1)S(1)}, u32[]{:S(2)}, u32[]{:S(2)}) collective-permute-start(bf16[256,1024]{1,0:T(8,128)(2,1)} %constant_dynamic-update-slice_fusion.refs_1_), channel_id=1, source_target_pairs={{0,24},{8,0},{16,8},{24,16},{1,25},{9,1},{17,9},{25,17},{2,26},{10... | collective-permute-start | bytes 1572872 | tf_op jit(solution)/shard_map/ppermute | solution.py:38
  86.8 25.3 %collective-permute-start.25 = (bf16[256,2048]{0,1:T(8,128)(2,1)}, bf16[256,2048]{0,1:T(8,128)(2,1)S(1)}, u32[]{:S(2)}, u32[]{:S(2)}) collective-permute-start(bf16[256,2048]{0,1:T(8,128)(2,1)} %copy.31), channel_id=1, source_target_pairs={{0,4},{4,0},{1,5},{5,1},{2,6},{6,2},{3,7},{7,3},{8,12},{12,8},{9,1... | collective-permute-start | bytes 3145736 | tf_op jit(solution)/shard_map/ppermute | solution.py:342
  88.7 28.9 %collective-permute-start.21 = (bf16[256,1024]{1,0:T(8,128)(2,1)}, bf16[256,1024]{1,0:T(8,128)(2,1)}, u32[]{:S(2)}, u32[]{:S(2)}) collective-permute-start(bf16[256,1024]{1,0:T(8,128)(2,1)} %copy-done.29), channel_id=1, source_target_pairs={{0,32},{32,64},{64,96},{96,0},{1,33},{33,65},{65,97},{97,1},{2,34}... | collective-permute-start | bytes 1572872 | tf_op jit(solution)/shard_map/ppermute | solution.py:38
  88.7 28.9 %collective-permute-start.22 = (bf16[256,1024]{1,0:T(8,128)(2,1)}, bf16[256,1024]{1,0:T(8,128)(2,1)}, u32[]{:S(2)}, u32[]{:S(2)}) collective-permute-start(bf16[256,1024]{1,0:T(8,128)(2,1)} %copy-done.30), channel_id=1, source_target_pairs={{0,96},{32,0},{64,32},{96,64},{1,97},{33,1},{65,33},{97,65},{2,98}... | collective-permute-start | bytes 1572872 | tf_op jit(solution)/shard_map/ppermute | solution.py:38
  91.9 28.6 %collective-permute-start.17 = (bf16[256,1024]{1,0:T(8,128)(2,1)}, bf16[256,1024]{1,0:T(8,128)(2,1)}, u32[]{:S(2)}, u32[]{:S(2)}) collective-permute-start(bf16[256,1024]{1,0:T(8,128)(2,1)} %copy-done.31), channel_id=1, source_target_pairs={{0,8},{8,16},{16,24},{24,0},{1,9},{9,17},{17,25},{25,1},{2,10},{10... | collective-permute-start | bytes 1572872 | tf_op jit(solution)/shard_map/ppermute | solution.py:38
  91.9 40.0 %collective-permute-start.18 = (bf16[256,1024]{1,0:T(8,128)(2,1)}, bf16[256,1024]{1,0:T(8,128)(2,1)}, u32[]{:S(2)}, u32[]{:S(2)}) collective-permute-start(bf16[256,1024]{1,0:T(8,128)(2,1)} %copy-done.32), channel_id=1, source_target_pairs={{0,24},{8,0},{16,8},{24,16},{1,25},{9,1},{17,9},{25,17},{2,26},{10... | collective-permute-start | bytes 1572872 | tf_op jit(solution)/shard_map/ppermute | solution.py:38
  112.1 19.8 %collective-permute-start.20 = (bf16[256,1024]{1,0:T(8,128)(2,1)S(1)}, bf16[256,1024]{1,0:T(8,128)(2,1)}, u32[]{:S(2)}, u32[]{:S(2)}) collective-permute-start(bf16[256,1024]{1,0:T(8,128)(2,1)S(1)} %copy-done.12), channel_id=1, source_target_pairs={{0,24},{8,0},{16,8},{24,16},{1,25},{9,1},{17,9},{25,17},{2,26},{10... | collective-permute-start | bytes 1572872 | tf_op jit(solution)/shard_map/ppermute | solution.py:38
  117.5 14.4 %collective-permute-start.19 = (bf16[256,1024]{1,0:T(8,128)(2,1)}, bf16[256,1024]{1,0:T(8,128)(2,1)S(1)}, u32[]{:S(2)}, u32[]{:S(2)}) collective-permute-start(bf16[256,1024]{1,0:T(8,128)(2,1)} %constant_dynamic-update-slice_fusion.refs_1_), channel_id=1, source_target_pairs={{0,8},{8,16},{16,24},{24,0},{1,9},{9,17},{17,25},{25,1},{2,10},{10... | collective-permute-start | bytes 1572872 | tf_op jit(solution)/shard_map/ppermute | solution.py:38
  117.5 14.4 %collective-permute-start.24 = (bf16[256,1024]{1,0:T(8,128)(2,1)S(1)}, bf16[256,1024]{1,0:T(8,128)(2,1)S(1)}, u32[]{:S(2)}, u32[]{:S(2)}) collective-permute-start(bf16[256,1024]{1,0:T(8,128)(2,1)S(1)} %copy-done.10), channel_id=1, source_target_pairs={{0,96},{32,0},{64,32},{96,64},{1,97},{33,1},{65,33},{97,65},{2,98}... | collective-permute-start | bytes 1572872 | tf_op jit(solution)/shard_map/ppermute | solution.py:38
  120.5 14.0 %collective-permute-start.23 = (bf16[256,1024]{1,0:T(8,128)(2,1)}, bf16[256,1024]{1,0:T(8,128)(2,1)S(1)}, u32[]{:S(2)}, u32[]{:S(2)}) collective-permute-start(bf16[256,1024]{1,0:T(8,128)(2,1)} %constant_dynamic-update-slice_fusion.2.refs_9_), channel_id=1, source_target_pairs={{0,32},{32,64},{64,96},{96,0},{1,33},{33,65},{65,97},{97,1},{2,34}... | collective-permute-start | bytes 1572872 | tf_op jit(solution)/shard_map/ppermute | solution.py:38
  135.3 18.0 %collective-permute-start.26 = (f32[256,512]{1,0:T(8,128)}, f32[256,512]{1,0:T(8,128)S(1)}, u32[]{:S(2)}, u32[]{:S(2)}) collective-permute-start(f32[256,512]{1,0:T(8,128)} %get-tuple-element.123), channel_id=1, source_target_pairs={{0,4},{4,0},{1,5},{5,1},{2,6},{6,2},{3,7},{7,3},{8,12},{12,8},{9,1... | collective-permute-start | bytes 1572872 | tf_op jit(solution)/shard_map/ppermute | solution.py:347
  147.9 21.3 %collective-permute-start.27 = (f32[256,512]{1,0:T(8,128)}, f32[256,512]{1,0:T(8,128)S(1)}, u32[]{:S(2)}, u32[]{:S(2)}) collective-permute-start(f32[256,512]{1,0:T(8,128)} %get-tuple-element.127), channel_id=1, source_target_pairs={{0,4},{4,0},{1,5},{5,1},{2,6},{6,2},{3,7},{7,3},{8,12},{12,8},{9,1... | collective-permute-start | bytes 1572872 | tf_op jit(solution)/shard_map/ppermute | solution.py:350
  149.4 34.3 %collective-permute-start.29 = (f32[256,512]{1,0:T(8,128)}, f32[256,512]{1,0:T(8,128)S(1)}, u32[]{:S(2)}, u32[]{:S(2)}) collective-permute-start(f32[256,512]{1,0:T(8,128)} %get-tuple-element.131), channel_id=1, source_target_pairs={{0,4},{4,0},{1,5},{5,1},{2,6},{6,2},{3,7},{7,3},{8,12},{12,8},{9,1... | collective-permute-start | bytes 1572872 | tf_op jit(solution)/shard_map/ppermute | solution.py:350
  150.0 53.6 %collective-permute-start.30 = (f32[256,512]{1,0:T(8,128)S(1)}, f32[256,512]{1,0:T(8,128)}, u32[]{:S(2)}, u32[]{:S(2)}) collective-permute-start(f32[256,512]{1,0:T(8,128)S(1)} %copy-done.13), channel_id=1, source_target_pairs={{0,4},{4,0},{1,5},{5,1},{2,6},{6,2},{3,7},{7,3},{8,12},{12,8},{9,1... | collective-permute-start | bytes 1572872 | tf_op jit(solution)/shard_map/ppermute | solution.py:347
  154.1 14.9 %all-to-all-start.1 = ((f32[16,1,2048]{2,1,0:T(1,128)}), f32[16,1,2048]{2,1,0:T(1,128)S(1)}, u32[]{:S(2)}, u32[]{:S(2)}) async-start(f32[16,1,2048]{2,1,0:T(1,128)} %broadcast_in_dim.22), calls=%async_computation.1 | async-start | bytes 262144 | tf_op jit(solution)/shard_map/all_to_all | solution.py:30
  167.8 15.9 %collective-permute-start.28 = (f32[1024,512]{1,0:T(8,128)}, f32[1024,512]{1,0:T(8,128)}, u32[]{:S(2)}, u32[]{:S(2)}) collective-permute-start(f32[1024,512]{1,0:T(8,128)} %shard_map.95), channel_id=1, source_target_pairs={{0,1},{1,0},{2,3},{3,2},{4,5},{5,4},{6,7},{7,6},{8,9},{9,8},{10,11... | collective-permute-start | bytes 6291464 | tf_op jit(solution)/shard_map/ppermute | solution.py:355
  170.0 46.7 %collective-permute-start.32 = (f32[2048]{0:T(1024)S(1)}, f32[2048]{0:T(1024)S(1)}, u32[]{:S(2)}, u32[]{:S(2)}) collective-permute-start(f32[2048]{0:T(1024)S(1)} %get-tuple-element.162), channel_id=1, source_target_pairs={{0,4},{4,0},{1,5},{5,1},{2,6},{6,2},{3,7},{7,3},{8,12},{12,8},{9,1... | collective-permute-start | bytes 24584 | tf_op jit(solution)/shard_map/ppermute | solution.py:394
  177.7 17.1 %collective-permute-start.31 = (f32[1024,512]{1,0:T(8,128)}, f32[1024,512]{1,0:T(8,128)}, u32[]{:S(2)}, u32[]{:S(2)}) collective-permute-start(f32[1024,512]{1,0:T(8,128)} %shard_map.96), channel_id=1, source_target_pairs={{0,1},{1,0},{2,3},{3,2},{4,5},{5,4},{6,7},{7,6},{8,9},{9,8},{10,11... | collective-permute-start | bytes 6291464 | tf_op jit(solution)/shard_map/ppermute | solution.py:361
  180.1 23.6 %all-to-all-start.2 = ((f32[8,4,256]{2,1,0:T(4,128)}), f32[8,4,256]{2,1,0:T(4,128)S(1)}, u32[]{:S(2)}, u32[]{:S(2)}) async-start(f32[8,4,256]{2,1,0:T(4,128)} %broadcast_in_dim.23), calls=%async_computation.2 | async-start | bytes 65536 | tf_op jit(solution)/shard_map/all_to_all | solution.py:30
  191.3 28.6 %collective-permute-start.33 = (f32[256,512]{1,0:T(8,128)}, f32[256,512]{1,0:T(8,128)S(1)}, u32[]{:S(2)}, u32[]{:S(2)}) collective-permute-start(f32[256,512]{1,0:T(8,128)} %get-tuple-element.142), channel_id=1, source_target_pairs={{0,6},{6,0},{2,4},{4,2},{1,7},{7,1},{3,5},{5,3},{8,14},{14,8},{10,... | collective-permute-start | bytes 1572872 | tf_op jit(solution)/shard_map/ppermute | solution.py:378
  194.5 25.3 %collective-permute-start.34 = (f32[512,256]{1,0:T(8,128)}, f32[512,256]{1,0:T(8,128)S(1)}, u32[]{:S(2)}, u32[]{:S(2)}) collective-permute-start(f32[512,256]{1,0:T(8,128)} %get-tuple-element.143), channel_id=1, source_target_pairs={{0,4},{4,0},{1,5},{5,1},{2,6},{6,2},{3,7},{7,3},{8,12},{12,8},{9,1... | collective-permute-start | bytes 1572872 | tf_op jit(solution)/shard_map/ppermute | solution.py:379
  194.8 25.1 %collective-permute-start.35 = (f32[256,512]{1,0:T(8,128)}, f32[256,512]{1,0:T(8,128)S(1)}, u32[]{:S(2)}, u32[]{:S(2)}) collective-permute-start(f32[256,512]{1,0:T(8,128)} %get-tuple-element.144), channel_id=1, source_target_pairs={{0,6},{6,0},{2,4},{4,2},{1,7},{7,1},{3,5},{5,3},{8,14},{14,8},{10,... | collective-permute-start | bytes 1572872 | tf_op jit(solution)/shard_map/ppermute | solution.py:393
  215.9 25.5 %collective-permute-start.37 = (f32[512,256]{1,0:T(8,128)}, f32[512,256]{1,0:T(8,128)}, u32[]{:S(2)}, u32[]{:S(2)}) collective-permute-start(f32[512,256]{1,0:T(8,128)} %get-tuple-element.148), channel_id=1, source_target_pairs={{0,4},{4,0},{1,5},{5,1},{2,6},{6,2},{3,7},{7,3},{8,12},{12,8},{9,1... | collective-permute-start | bytes 1572872 | tf_op jit(solution)/shard_map/ppermute | solution.py:395
  (51 other events, 531.5 us)
Sparse Core Ops, SparseCore 0:
  33.5 88.5 all-gather.1
